TPU v7x, 32 devices: a whole 2x2x4 slice. The times are simulated.
32 devices in a mesh: dp: 4 (over y, x), seq: 8 (over z, core).
Axes of the slice: x: 2, y: 2, z: 4, core: 2. Of those that a mesh axis runs over, the one named last changes fastest.
Arguments:
- tokens: bfloat16 [4, 2560, 2304], P('dp', 'seq'), may hold values from -6 to 6
- pre_attention: float32 [2304], replicated, may hold values from 0.25 to 1.75
- post_attention: float32 [2304], replicated, may hold values from 0.25 to 1.75
- pre_feedforward: float32 [2304], replicated, may hold values from 0.25 to 1.75
- post_feedforward: float32 [2304], replicated, may hold values from 0.25 to 1.75
- w_query: bfloat16 [2304, 2048], P(('dp', 'seq')), may hold values from -0.125 to 0.125
- key_weight: bfloat16 [2304, 1024], P(('dp', 'seq')), may hold values from -0.125 to 0.125
- value_weight: bfloat16 [2304, 1024], P(('dp', 'seq')), may hold values from -0.125 to 0.125
- w_output: bfloat16 [2048, 2304], P(('dp', 'seq')), may hold values from -0.125 to 0.125
- w_gate: bfloat16 [2304, 9216], P(('dp', 'seq')), may hold values from -0.125 to 0.125
- w_up: bfloat16 [2304, 9216], P(('dp', 'seq')), may hold values from -0.125 to 0.125
- w_down: bfloat16 [9216, 2304], P(('dp', 'seq')), may hold values from -0.0625 to 0.0625
- document_index: int32 [2, 5120], replicated, may hold values from 0 to 5, as said below
- token_padding_mask: int32 [2, 5120], replicated, may hold values 0 or 1
- cotangent: bfloat16 [4, 2560, 2304], P('dp', 'seq'), may hold values from -6 to 6
Outputs:
- output: float32 [4, 2560, 2304], P('dp', 'seq')
- tokens_grad: float32 [4, 2560, 2304], P('dp', 'seq')
- w_query_grad: float32 [2304, 2048], P(('dp', 'seq'))
- w_key_grad: float32 [2304, 1024], P(('dp', 'seq'))
- w_value_grad: float32 [2304, 1024], P(('dp', 'seq'))
- w_output_grad: float32 [2048, 2304], P(('dp', 'seq'))
- w_gate_grad: float32 [2304, 9216], P(('dp', 'seq'))
- w_up_grad: float32 [2304, 9216], P(('dp', 'seq'))
- w_down_grad: float32 [9216, 2304], P(('dp', 'seq'))
- pre_attention_grad: float32 [2304], P(('dp', 'seq'))
- post_attention_grad: float32 [2304], P(('dp', 'seq'))
- pre_feedforward_grad: float32 [2304], P(('dp', 'seq'))
- post_feedforward_grad: float32 [2304], P(('dp', 'seq'))
Inputs may be any that keep to these rules, and one draw needn't show every extreme that they name: `document_index`: along each sequence the segment numbers start at 0, never fall, and end at 5.
All inputs are finite; a program needn't handle non-finite values.
Results may differ from a plain program's by a relative error of at most 0.018.
Values may be sent and summed in bfloat16 or wider, within the bound.
No kernel may reach another device: no remote copies, remote signals or barrier semaphores. Data moves between devices by JAX's collectives and lax.ppermute only.
A program may use at most 768 MiB of HBM per device.

v0:
```python
import jax
import jax.numpy as jnp
from jax import lax
from jax.sharding import PartitionSpec as P

QUERY_HEADS = 8
KEY_VALUE_HEADS = 4
HEAD_DIM = 256
WINDOW = 4096


epsilon = 1e-06
softcap = 50.0
big_negative = -1e30


def shifted(block, axis, distance):
    devices = range(lax.axis_size(axis))
    route = [(i - distance, i) for i in devices if i - distance in devices]
    return lax.ppermute(block, axis, route)


def normed(values, gain_vec):
    inv_rms = lax.rsqrt(jnp.mean(values * values, axis=-1, keepdims=True) + epsilon)
    return values * inv_rms * gain_vec


def matmul(operand, other_operand):
    return jnp.dot(operand, other_operand, preferred_element_type=jnp.float32)


def matmul_t(operand, other_operand):
    return lax.dot_general(
        operand, other_operand, (((1,), (1,)), ((), ())), preferred_element_type=jnp.float32
    )


def inner_t(operand, other_operand):
    return lax.dot_general(
        operand, other_operand, (((0,), (0,)), ((), ())), preferred_element_type=jnp.float32
    )


def add_columns(operand, shard_piece):
    return matmul(operand, shard_piece)


def split_heads(query_batch, key_complete, value_complete):
    length_total = key_complete.shape[0]
    heads_of_query = query_batch.reshape(
        query_batch.shape[0], KEY_VALUE_HEADS, QUERY_HEADS // KEY_VALUE_HEADS, HEAD_DIM
    )
    return (
        heads_of_query,
        key_complete.reshape(length_total, KEY_VALUE_HEADS, HEAD_DIM),
        value_complete.reshape(length_total, KEY_VALUE_HEADS, HEAD_DIM),
    )


def scores_of(heads_of_query, heads_of_key):
    raw_scores = jnp.einsum(
        "qhgd,khd->hgqk", heads_of_query, heads_of_key, preferred_element_type=jnp.float32
    )
    capped = softcap * jnp.tanh(raw_scores * HEAD_DIM ** (-0.5) / softcap)
    return (raw_scores, capped)


def attention_forward(query_batch, key_complete, value_complete, allowed):
    heads_of_query, heads_of_key, heads_of_value = split_heads(
        query_batch, key_complete, value_complete
    )
    raw_scores, capped = scores_of(heads_of_query, heads_of_key)
    masked = jnp.where(allowed, capped, big_negative)
    row_max = jnp.max(masked, axis=-1, keepdims=True)
    weights = jnp.where(allowed, jnp.exp(masked - row_max), 0.0)
    row_total = jnp.sum(weights, axis=-1, keepdims=True)
    probabilities = (weights / row_total).astype(jnp.bfloat16)
    attended_output = jnp.einsum(
        "hgqk,khd->qhgd", probabilities, heads_of_value, preferred_element_type=jnp.float32
    )
    attended_output = attended_output.reshape(query_batch.shape[0], QUERY_HEADS * HEAD_DIM).astype(
        jnp.bfloat16
    )
    return (attended_output, row_max + jnp.log(row_total))


def attention_backward(query_batch, key_complete, value_complete, allowed, log_total, grad_b):
    heads_of_query, heads_of_key, heads_of_value = split_heads(
        query_batch, key_complete, value_complete
    )
    raw_scores, capped = scores_of(heads_of_query, heads_of_key)
    probabilities = jnp.where(allowed, jnp.exp(capped - log_total), 0.0)
    grad_heads = grad_b.reshape(heads_of_query.shape)
    grad_probs = jnp.einsum(
        "qhgd,khd->hgqk", grad_heads, heads_of_value, preferred_element_type=jnp.float32
    )
    value_gradient = jnp.einsum(
        "hgqk,qhgd->khd",
        probabilities.astype(jnp.bfloat16),
        grad_heads,
        preferred_element_type=jnp.float32,
    )
    delta = jnp.sum(probabilities * grad_probs, axis=-1, keepdims=True)
    grad_capped = probabilities * (grad_probs - delta)
    squashed = jnp.tanh(raw_scores * HEAD_DIM ** (-0.5) / softcap)
    grad_raw = (grad_capped * (1.0 - squashed * squashed) * HEAD_DIM ** (-0.5)).astype(jnp.bfloat16)
    grad_queries = jnp.einsum(
        "hgqk,khd->qhgd", grad_raw, heads_of_key, preferred_element_type=jnp.float32
    )
    key_gradient = jnp.einsum(
        "hgqk,qhgd->khd", grad_raw, heads_of_query, preferred_element_type=jnp.float32
    )
    length_total = key_complete.shape[0]
    return (
        grad_queries.reshape(query_batch.shape[0], QUERY_HEADS * HEAD_DIM),
        key_gradient.reshape(length_total, KEY_VALUE_HEADS * HEAD_DIM),
        value_gradient.reshape(length_total, KEY_VALUE_HEADS * HEAD_DIM),
    )


def body(
    tokens,
    pre_attention,
    post_attention,
    pre_feedforward,
    post_feedforward,
    w_query,
    key_weight,
    value_weight,
    w_output,
    w_gate,
    w_up,
    w_down,
    document_index,
    token_padding_mask,
    cotangent,
):
    inputs = tokens[0].astype(jnp.float32)
    token_count = inputs.shape[0]
    hidden_width = w_gate.shape[1]
    query_whole, key_whole, value_whole, output_whole = (
        lax.all_gather(w_query, ("dp", "seq"), axis=0, tiled=True),
        lax.all_gather(key_weight, ("dp", "seq"), axis=0, tiled=True),
        lax.all_gather(value_weight, ("dp", "seq"), axis=0, tiled=True),
        lax.all_gather(w_output, ("dp", "seq"), axis=0, tiled=True),
    )
    normed_in = normed(inputs, pre_attention).astype(jnp.bfloat16)
    query_batch = matmul(normed_in, query_whole).astype(jnp.bfloat16)
    key_b = matmul(normed_in, key_whole).astype(jnp.bfloat16)
    value_b = matmul(normed_in, value_whole).astype(jnp.bfloat16)
    key_half, value_half = (
        lax.all_gather(key_b, "seq", axis=0, tiled=True),
        lax.all_gather(value_b, "seq", axis=0, tiled=True),
    )
    half_length = key_half.shape[0]
    partner_key, partner_value = shifted((key_half, value_half), "dp", 1)
    key_complete = jnp.concatenate([partner_key, key_half], axis=0)
    value_complete = jnp.concatenate([partner_value, value_half], axis=0)
    row_index = lax.axis_index("dp")
    sequence_index = row_index // 2
    half_index = row_index % 2
    first_query = half_index * half_length + lax.axis_index("seq") * token_count
    segment_row = lax.dynamic_index_in_dim(document_index, sequence_index, 0, keepdims=False)
    padding_row = lax.dynamic_index_in_dim(token_padding_mask, sequence_index, 0, keepdims=False)
    query_segments = lax.dynamic_slice_in_dim(segment_row, first_query, token_count)
    padded_segments = jnp.concatenate([jnp.full((half_length,), -1, jnp.int32), segment_row])
    padded_padding = jnp.concatenate([jnp.zeros((half_length,), jnp.int32), padding_row])
    key_segments = lax.dynamic_slice_in_dim(
        padded_segments, half_index * half_length, 2 * half_length
    )
    key_padding = lax.dynamic_slice_in_dim(
        padded_padding, half_index * half_length, 2 * half_length
    )
    query_pos = first_query + jnp.arange(token_count, dtype=jnp.int32)
    key_pos = (half_index - 1) * half_length + jnp.arange(2 * half_length, dtype=jnp.int32)
    allowed = key_segments[None, :] == query_segments[:, None]
    allowed = allowed & (key_pos[None, :] <= query_pos[:, None])
    allowed = allowed & (query_pos[:, None] - key_pos[None, :] < WINDOW)
    allowed = allowed & ((key_padding[None, :] == 1) | (key_pos[None, :] == query_pos[:, None]))
    allowed = allowed[None, None]
    attended_b, log_total = attention_forward(query_batch, key_complete, value_complete, allowed)
    attn_out = matmul(attended_b, output_whole)
    residual = inputs + normed(attn_out, post_attention)
    normed_mid = normed(residual, pre_feedforward).astype(jnp.bfloat16)
    pieces = (
        lax.all_gather(w_gate, ("dp", "seq"), axis=0, tiled=True),
        lax.all_gather(w_up, ("dp", "seq"), axis=0, tiled=True),
    )
    gate_value = add_columns(normed_mid, pieces[0])
    up_value = add_columns(normed_mid, pieces[1])

    def activation(gate_in, up_in):
        return jax.nn.gelu(gate_in, approximate=True) * up_in

    hidden_b = activation(gate_value, up_value).astype(jnp.bfloat16)
    down_out = add_columns(hidden_b, lax.all_gather(w_down, ("dp", "seq"), axis=0, tiled=True))
    result = residual + normed(down_out, post_feedforward)
    grad_output = cotangent[0].astype(jnp.float32)
    post_ff_value, post_ff_back = jax.vjp(normed, down_out, post_feedforward)
    grad_down, grad_post_ff = post_ff_back(grad_output)
    grad_down_b = grad_down.astype(jnp.bfloat16)
    grad_hidden = matmul_t(grad_down_b, lax.all_gather(w_down, ("dp", "seq"), axis=0, tiled=True))
    down_shard = lax.psum_scatter(
        inner_t(hidden_b, grad_down_b), ("dp", "seq"), scatter_dimension=0, tiled=True
    )
    act_value, act_back = jax.vjp(activation, gate_value, up_value)
    grad_gate, grad_up = act_back(grad_hidden)
    grad_gate_b = grad_gate.astype(jnp.bfloat16)
    grad_up_b = grad_up.astype(jnp.bfloat16)
    pieces = lax.all_gather((w_gate, w_up), ("dp", "seq"), axis=0, tiled=True)
    grad_mid = matmul_t(grad_gate_b, pieces[0]) + matmul_t(grad_up_b, pieces[1])
    gate_up_shard = lax.psum_scatter(
        jnp.concatenate([inner_t(normed_mid, grad_gate_b), inner_t(normed_mid, grad_up_b)], axis=1),
        ("dp", "seq"),
        scatter_dimension=0,
        tiled=True,
    )
    pre_ff_value, pre_ff_back = jax.vjp(normed, residual, pre_feedforward)
    grad_residual_part, grad_pre_ff = pre_ff_back(grad_mid)
    grad_residual = grad_output + grad_residual_part
    post_attn_value, post_attn_back = jax.vjp(normed, attn_out, post_attention)
    grad_attn, grad_post_attn = post_attn_back(grad_residual)
    grad_attn_b = grad_attn.astype(jnp.bfloat16)
    grad_attended = matmul_t(grad_attn_b, output_whole)
    output_term = inner_t(attended_b, grad_attn_b)
    grad_attended_b = grad_attended.astype(jnp.bfloat16)
    grad_queries, grad_keys_all, grad_values_all = attention_backward(
        query_batch, key_complete, value_complete, allowed, log_total, grad_attended_b
    )
    returned_keys, returned_values = (
        shifted(grad_keys_all[:half_length].astype(jnp.bfloat16), "dp", -1).astype(jnp.float32),
        shifted(grad_values_all[:half_length].astype(jnp.bfloat16), "dp", -1).astype(jnp.float32),
    )
    key_gradient, value_gradient = (
        lax.psum_scatter(
            (grad_keys_all[half_length:] + returned_keys).astype(jnp.bfloat16),
            "seq",
            scatter_dimension=0,
            tiled=True,
        ).astype(jnp.float32),
        lax.psum_scatter(
            (grad_values_all[half_length:] + returned_values).astype(jnp.bfloat16),
            "seq",
            scatter_dimension=0,
            tiled=True,
        ).astype(jnp.float32),
    )
    grad_queries_b = grad_queries.astype(jnp.bfloat16)
    grad_keys_b = key_gradient.astype(jnp.bfloat16)
    grad_values_b = value_gradient.astype(jnp.bfloat16)
    grad_in = (
        matmul_t(grad_queries_b, query_whole)
        + matmul_t(grad_keys_b, key_whole)
        + matmul_t(grad_values_b, value_whole)
    )
    query_term = inner_t(normed_in, grad_queries_b)
    key_term = inner_t(normed_in, grad_keys_b)
    value_term = inner_t(normed_in, grad_values_b)
    pre_attn_value, pre_attn_back = jax.vjp(normed, inputs, pre_attention)
    grad_inputs, grad_pre_attn = pre_attn_back(grad_in)
    tokens_grad = grad_residual + grad_inputs
    gain_terms = jnp.stack([grad_pre_attn, grad_post_attn, grad_pre_ff, grad_post_ff], axis=1)
    query_shard, key_shard, value_shard, output_shard, gain_shard = (
        lax.psum_scatter(query_term, ("dp", "seq"), scatter_dimension=0, tiled=True),
        lax.psum_scatter(key_term, ("dp", "seq"), scatter_dimension=0, tiled=True),
        lax.psum_scatter(value_term, ("dp", "seq"), scatter_dimension=0, tiled=True),
        lax.psum_scatter(output_term, ("dp", "seq"), scatter_dimension=0, tiled=True),
        lax.psum_scatter(gain_terms, ("dp", "seq"), scatter_dimension=0, tiled=True),
    )
    return (
        result[None],
        tokens_grad[None],
        query_shard,
        key_shard,
        value_shard,
        output_shard,
        gate_up_shard[:, :hidden_width],
        gate_up_shard[:, hidden_width:],
        down_shard,
        gain_shard[:, 0],
        gain_shard[:, 1],
        gain_shard[:, 2],
        gain_shard[:, 3],
    )


def solution(mesh):
    placed = (
        P("dp", "seq", None),
        P(),
        P(),
        P(),
        P(),
        P(("dp", "seq"), None),
        P(("dp", "seq"), None),
        P(("dp", "seq"), None),
        P(("dp", "seq"), None),
        P(("dp", "seq"), None),
        P(("dp", "seq"), None),
        P(("dp", "seq"), None),
        P(),
        P(),
        P("dp", "seq", None),
    )
    return jax.shard_map(
        body,
        mesh=mesh,
        in_specs=placed,
        out_specs=(
            P("dp", "seq", None),
            P("dp", "seq", None),
            P(("dp", "seq"), None),
            P(("dp", "seq"), None),
            P(("dp", "seq"), None),
            P(("dp", "seq"), None),
            P(("dp", "seq"), None),
            P(("dp", "seq"), None),
            P(("dp", "seq"), None),
            P(("dp", "seq")),
            P(("dp", "seq")),
            P(("dp", "seq")),
            P(("dp", "seq")),
        ),
        check_vma=False,
    )
```

profile of v0, /device:TPU:0, one launch (start us, length us, event | category | flops | bytes accessed | tf_op | source)
XLA Modules:
  0.0 5610.1 jit_solution(14553944256693893840)
XLA Ops:
  11.0 66.4 %all-gather.10.cloned.1.call-done = bf16[2304,1024]{1,0:T(8,128)(2,1)} async-done(((bf16[72,1024]{1,0:T(8,128)(2,1)}), bf16[2304,1024]{1,0:T(8,128)(2,1)}) %all-gather.10.cloned.1.call-update) | async-done | bytes 4718608 | tf_op jit(solution)/shard_map/all_gather | solution.py:144
  82.9 60.1 %all-gather.14.cloned.1.call-done = bf16[2304,1024]{1,0:T(8,128)(2,1)} async-done(((bf16[72,1024]{1,0:T(8,128)(2,1)}), bf16[2304,1024]{1,0:T(8,128)(2,1)}) %all-gather.14.cloned.1.call-update) | async-done | bytes 4718608 | tf_op jit(solution)/shard_map/all_gather | solution.py:143
  151.3 48.7 all-gather.12.cloned.1.call-done
  205.8 51.2 all-gather.16.cloned.1.call-done
  266.2 102.3 %all-gather.18.cloned.1.call-done = bf16[2304,2048]{1,0:T(8,128)(2,1)} async-done(((bf16[72,2048]{1,0:T(8,128)(2,1)}), bf16[2304,2048]{1,0:T(8,128)(2,1)}) %all-gather.18.cloned.1.call-update) | async-done | bytes 9437200 | tf_op jit(solution)/shard_map/all_gather | solution.py:142
  411.3 72.2 %collective-permute-done.1 = bf16[2560,1024]{1,0:T(8,128)(2,1)} collective-permute-done((bf16[2560,1024]{1,0:T(8,128)(2,1)}, bf16[2560,1024]{1,0:T(8,128)(2,1)}, u32[]{:S(2)}, u32[]{:S(2)}) %collective-permute-start.1) | collective-permute-done | bytes 5242912 | tf_op jit(solution)/shard_map/ppermute | solution.py:20
  514.6 25.6 fusion.6
  540.2 26.7 fusion.8
  566.9 29.5 fusion.71
  610.8 108.0 %all-gather.22.cloned.1.call-done = bf16[2304,9216]{1,0:T(8,128)(2,1)} async-done(((bf16[72,9216]{1,0:T(8,128)(2,1)}), bf16[2304,9216]{1,0:T(8,128)(2,1)}) %all-gather.22.cloned.1.call-update) | async-done | bytes 42467344 | tf_op jit(solution)/shard_map/all_gather | solution.py:186
  718.8 24.8 fusion.102
  743.6 214.2 %all-gather.24.cloned.1.call-done = bf16[2304,9216]{1,0:T(8,128)(2,1)} async-done(((bf16[72,9216]{1,0:T(8,128)(2,1)}), bf16[2304,9216]{1,0:T(8,128)(2,1)}) %all-gather.24.cloned.1.call-update) | async-done | bytes 42467344 | tf_op jit(solution)/shard_map/all_gather | solution.py:187
  957.9 29.9 multiply_convert_fusion.1
  987.8 209.1 %all-gather.26.cloned.1.call-done = bf16[9216,2304]{1,0:T(8,128)(2,1)} async-done(((bf16[288,2304]{1,0:T(8,128)(2,1)}), bf16[9216,2304]{1,0:T(8,128)(2,1)}) %all-gather.26.cloned.1.call-update) | async-done | bytes 42467344 | tf_op jit(solution)/shard_map/all_gather | solution.py:196
  1224.4 32.0 multiply_convert_fusion
  1278.1 24.4 multiply_reduce_fusion
  1323.0 28.8 fusion.21
  1367.3 22.5 fusion.30
  1391.2 75.3 %fusion.2 = bf16[4,2,320,5120]{3,2,1,0:T(8,128)(2,1)} fusion(f32[4,5120,320,2]{1,2,3,0:T(8,128)} %fusion.30, f32[4,5120,320,2]{1,2,3,0:T(8,128)} %get-tuple-element.35, f32[4,2,320]{2,1,0:T(2,128)S(1)} %bitcast.191, pred[320,5120]{1,0:T(8,128)(4,1)S(1)} %copy-done.12), kind=kOutput, calls=%fused_computation.4 | output fusion | flops 209722880 | bytes 132720640 | tf_op jit(solution)/shard_map/sub | solution.py:104
  1466.5 40.8 collective-permute-done.3
  1555.9 34.2 fusion.107
  1598.8 33.6 fusion.106
  1632.4 39.4 collective-permute-done.2
  1689.2 111.8 %pad_maximum_fusion = f32[2304,18432]{1,0:T(8,128)} fusion(f32[2304,9216]{1,0:T(8,128)} %fusion.107, f32[2304,9216]{1,0:T(8,128)} %fusion.106), kind=kLoop, calls=%fused_computation.1 | loop fusion | flops 42467328 | bytes 339738624 | tf_op jit(solution)/shard_map/concatenate | solution.py:213
  1857.9 32.7 fusion.108
  1909.7 41.5 all-reduce.3
  1957.5 2209.0 %all-reduce.6.cloned.1.call-done = f32[2304,18432]{1,0:T(8,128)} async-done(((f32[2304,18432]{1,0:T(8,128)}), f32[2304,18432]{1,0:T(8,128)}) %all-reduce.6.cloned.1.call-update) | async-done | bytes 169869328
  4172.2 211.3 %reduce-scatter.19.cloned.1.call-done = f32[64,2304]{1,0:T(8,128)} async-done(((f32[2048,2304]{1,0:T(8,128)}), f32[64,2304]{1,0:T(8,128)}) %reduce-scatter.19.cloned.1.call-update) | async-done | bytes 589840 | tf_op jit(solution)/shard_map/reduce_scatter | solution.py:267
  4383.5 212.5 %reduce-scatter.13.cloned.1.call-done = f32[72,2048]{1,0:T(8,128)} async-done(((f32[2304,2048]{1,0:T(8,128)}), f32[72,2048]{1,0:T(8,128)}) %reduce-scatter.13.cloned.1.call-update) | async-done | bytes 589840 | tf_op jit(solution)/shard_map/reduce_scatter | solution.py:264
  4596.1 140.8 %reduce-scatter.17.cloned.1.call-done = f32[72,1024]{1,0:T(8,128)} async-done(((f32[2304,1024]{1,0:T(8,128)}), f32[72,1024]{1,0:T(8,128)}) %reduce-scatter.17.cloned.1.call-update) | async-done | bytes 294928 | tf_op jit(solution)/shard_map/reduce_scatter | solution.py:266
  4736.9 141.7 %reduce-scatter.15.cloned.1.call-done = f32[72,1024]{1,0:T(8,128)} async-done(((f32[2304,1024]{1,0:T(8,128)}), f32[72,1024]{1,0:T(8,128)}) %reduce-scatter.15.cloned.1.call-update) | async-done | bytes 294928 | tf_op jit(solution)/shard_map/reduce_scatter | solution.py:265
  4878.6 724.7 %reduce-scatter.21.cloned.1.call-done = f32[288,2304]{1,0:T(8,128)} async-done(((f32[9216,2304]{1,0:T(8,128)}), f32[288,2304]{1,0:T(8,128)}) %reduce-scatter.21.cloned.1.call-update) | async-done | bytes 2654224 | tf_op jit(solution)/shard_map/reduce_scatter | solution.py:203
  (206 shorter events, 369.5 us)
Async XLA Ops:
  7.2 70.2 %all-gather.10.cloned.1.call-start = ((), (), s32[]{:S(2)}) async-start(), calls=%async_computation.7 | async-start | bytes 4866048 | tf_op jit(solution)/shard_map/all_gather | solution.py:144
  7.9 135.0 %all-gather.14.cloned.1.call-start = ((), (), s32[]{:S(2)}) async-start(), calls=%async_computation.9 | async-start | bytes 4866048 | tf_op jit(solution)/shard_map/all_gather | solution.py:143
  8.7 191.4 %all-gather.12.cloned.1.call-start = ((), (), s32[]{:S(2)}) async-start(), calls=%async_computation.8 | async-start | bytes 5898240 | tf_op jit(solution)/shard_map/all_gather | solution.py:153
  11.0 357.5 %copy-start.26 = (f32[320]{0:T(512)}, f32[320]{0:T(512)S(1)}, u32[]{:S(2)}) copy-start(f32[320]{0:T(512)S(1)} %fusion.79) | copy-start | bytes 3844
  11.0 131.9 %copy-start = (bf16[1,320,2304]{2,1,0:T(8,128)(2,1)S(1)}, bf16[1,320,2304]{2,1,0:T(8,128)(2,1)}, u32[]{:S(2)}) copy-start(bf16[1,320,2304]{2,1,0:T(8,128)(2,1)} %param.15) | copy-start | bytes 4423684
  11.0 131.9 %copy-start.24 = (f32[2304]{0:T(1024)S(1)}, f32[2304]{0:T(1024)}, u32[]{:S(2)}) copy-start(f32[2304]{0:T(1024)} %param.16) | copy-start | bytes 27652
  82.8 174.1 %all-gather.16.cloned.1.call-start = ((), (), s32[]{:S(2)}) async-start(), calls=%async_computation.10 | async-start | bytes 5898240 | tf_op jit(solution)/shard_map/all_gather | solution.py:152
  147.9 114.9 %copy-start.45 = (s32[2,5120]{1,0:T(2,128)S(1)}, s32[2,5120]{1,0:T(2,128)}, u32[]{:S(2)}) copy-start(s32[2,5120]{1,0:T(2,128)} %param.27) | copy-start | bytes 122884
  147.9 115.1 %copy-start.46 = (s32[2,5120]{1,0:T(2,128)S(1)}, s32[2,5120]{1,0:T(2,128)}, u32[]{:S(2)}) copy-start(s32[2,5120]{1,0:T(2,128)} %param.28) | copy-start | bytes 122884
  147.9 220.6 %all-gather.18.cloned.1.call-start = ((), (), s32[]{:S(2)}) async-start(), calls=%async_computation.11 | async-start | bytes 9732096 | tf_op jit(solution)/shard_map/all_gather | solution.py:142
  148.5 452.0 %all-gather.20.cloned.1.call-start = ((), (), s32[]{:S(2)}) async-start(), calls=%async_computation.12 | async-start | bytes 9732096 | tf_op jit(solution)/shard_map/all_gather | solution.py:145
  149.1 569.8 %all-gather.22.cloned.1.call-start = ((), (), s32[]{:S(2)}) async-start(), calls=%async_computation.13 | async-start | bytes 43794432 | tf_op jit(solution)/shard_map/all_gather | solution.py:186
  149.8 808.0 %all-gather.24.cloned.1.call-start = ((), (), s32[]{:S(2)}) async-start(), calls=%async_computation.14 | async-start | bytes 43794432 | tf_op jit(solution)/shard_map/all_gather | solution.py:187
  150.6 1046.3 %all-gather.26.cloned.1.call-start = ((), (), s32[]{:S(2)}) async-start(), calls=%async_computation.15 | async-start | bytes 43794432 | tf_op jit(solution)/shard_map/all_gather | solution.py:196
  151.3 1692.1 %reduce-scatter.25.cloned.1.call-start = ((), (), s32[]{:S(2)}) async-start(), calls=%async_computation.22 | async-start | bytes 5898240
  200.1 180.0 %collective-permute-start = (bf16[2560,1024]{1,0:T(8,128)(2,1)}, bf16[2560,1024]{1,0:T(8,128)(2,1)}, u32[]{:S(2)}, u32[]{:S(2)}) collective-permute-start(bf16[2560,1024]{1,0:T(8,128)(2,1)} %all-gather.12.cloned.1.call-done), channel_id=1, source_target_pairs={{0,8},{8,16},{16,24},{1,9},{9,17},{17,25},{2,10},{10,18},{18,26},{... | collective-permute-start | bytes 15728648 | tf_op jit(solution)/shard_map/ppermute | solution.py:20
  257.0 226.6 %collective-permute-start.1 = (bf16[2560,1024]{1,0:T(8,128)(2,1)}, bf16[2560,1024]{1,0:T(8,128)(2,1)}, u32[]{:S(2)}, u32[]{:S(2)}) collective-permute-start(bf16[2560,1024]{1,0:T(8,128)(2,1)} %all-gather.16.cloned.1.call-done), channel_id=1, source_target_pairs={{0,8},{8,16},{16,24},{1,9},{9,17},{17,25},{2,10},{10,18},{18,26},{... | collective-permute-start | bytes 15728648 | tf_op jit(solution)/shard_map/ppermute | solution.py:20
  266.2 300.7 %copy-start.11 = (pred[320,5120]{1,0:T(8,128)(4,1)}, pred[320,5120]{1,0:T(8,128)(4,1)S(1)}, u32[]{:S(2)}) copy-start(pred[320,5120]{1,0:T(8,128)(4,1)S(1)} %fusion.34) | copy-start | bytes 4915204
  380.0 134.6 %copy-start.18 = (bf16[320,4,2,256]{3,2,1,0:T(2,128)(2,1)}, bf16[320,4,2,256]{3,2,1,0:T(2,128)(2,1)S(1)}, u32[]{:S(2)}) copy-start(bf16[320,4,2,256]{3,2,1,0:T(2,128)(2,1)S(1)} %reshape.309) | copy-start | bytes 3932164
  608.9 134.8 %copy-start.39 = (f32[320]{0:T(512)}, f32[320]{0:T(512)S(1)}, u32[]{:S(2)}) copy-start(f32[320]{0:T(512)S(1)} %get-tuple-element.22) | copy-start | bytes 3844
  608.9 134.8 %copy-start.41 = (f32[320]{0:T(512)}, f32[320]{0:T(512)S(1)}, u32[]{:S(2)}) copy-start(f32[320]{0:T(512)S(1)} %fusion.81) | copy-start | bytes 3844
  610.8 347.1 %copy-start.9 = (bf16[320,2304]{1,0:T(8,128)(2,1)}, bf16[320,2304]{1,0:T(8,128)(2,1)S(1)}, u32[]{:S(2)}) copy-start(bf16[320,2304]{1,0:T(8,128)(2,1)S(1)} %multiply_convert_fusion.2) | copy-start | bytes 4423684
  1389.9 117.4 %collective-permute-start.3 = (bf16[2560,1024]{0,1:T(8,128)(2,1)}, bf16[2560,1024]{0,1:T(8,128)(2,1)}, u32[]{:S(2)}, u32[]{:S(2)}) collective-permute-start(bf16[2560,1024]{0,1:T(8,128)(2,1)} %bitcast.185), channel_id=1, source_target_pairs={{8,0},{16,8},{24,16},{9,1},{17,9},{25,17},{10,2},{18,10},{26,18},{... | collective-permute-start | bytes 15728648 | tf_op jit(solution)/shard_map/ppermute | solution.py:20
  1524.7 325.2 %reduce-scatter.23.cloned.1.call-start = ((), (), s32[]{:S(2)}) async-start(), calls=%async_computation.21 | async-start | bytes 5898240
  1554.6 117.2 %collective-permute-start.2 = (bf16[2560,1024]{0,1:T(8,128)(2,1)}, bf16[2560,1024]{0,1:T(8,128)(2,1)}, u32[]{:S(2)}, u32[]{:S(2)}) collective-permute-start(bf16[2560,1024]{0,1:T(8,128)(2,1)} %bitcast.20), channel_id=1, source_target_pairs={{8,0},{16,8},{24,16},{9,1},{17,9},{25,17},{10,2},{18,10},{26,18},{... | collective-permute-start | bytes 15728648 | tf_op jit(solution)/shard_map/ppermute | solution.py:20
  1689.2 2477.3 %all-reduce.6.cloned.1.call-start = ((), (), s32[]{:S(2)}) async-start(), calls=%async_computation.23 | async-start | bytes 339738624
  1801.1 2582.4 %reduce-scatter.19.cloned.1.call-start = ((), (), s32[]{:S(2)}) async-start(), calls=%async_computation.19 | async-start | bytes 19464192 | tf_op jit(solution)/shard_map/reduce_scatter | solution.py:267
  1812.8 2783.2 %reduce-scatter.13.cloned.1.call-start = ((), (), s32[]{:S(2)}) async-start(), calls=%async_computation.16 | async-start | bytes 19464192 | tf_op jit(solution)/shard_map/reduce_scatter | solution.py:264
  1843.3 2893.6 %reduce-scatter.17.cloned.1.call-start = ((), (), s32[]{:S(2)}) async-start(), calls=%async_computation.18 | async-start | bytes 9732096 | tf_op jit(solution)/shard_map/reduce_scatter | solution.py:266
  1849.7 3028.8 %reduce-scatter.15.cloned.1.call-start = ((), (), s32[]{:S(2)}) async-start(), calls=%async_computation.17 | async-start | bytes 9732096 | tf_op jit(solution)/shard_map/reduce_scatter | solution.py:265
  1856.4 3746.9 %reduce-scatter.21.cloned.1.call-start = ((), (), s32[]{:S(2)}) async-start(), calls=%async_computation.20 | async-start | bytes 87588864 | tf_op jit(solution)/shard_map/reduce_scatter | solution.py:203
  1903.0 48.8 copy-start.38
  (38 other events, 288.5 us)
Sparse Core Ops, SparseCore 0:
  11.0 66.3 all-gather.9
  80.4 62.4 all-gather.13
  145.2 54.8 all-gather.11
  202.1 54.8 all-gather.15
  259.8 108.5 all-gather.17
  371.3 108.2 all-gather.19
  482.6 236.1 all-gather.21
  721.9 235.9 all-gather.23
  960.9 235.9 all-gather.25
  1524.8 58.9 reduce-scatter.24
  1689.3 59.1 reduce-scatter.22
  1801.2 2365.2 all-reduce.5
  4173.5 210.0 reduce-scatter.18
  4390.4 205.6 reduce-scatter.12
  4602.4 134.4 reduce-scatter.16
  4744.2 134.3 reduce-scatter.14
  4885.4 717.8 reduce-scatter.20
where the time goes:
time: 5620 us; the launch traced here: 5610 us
  waiting for transfers between devices  4660 us (83%)
  matrix products  481 us (9%)
  other arithmetic  283 us (5%)
  local copies, waits for them, and re-layouts  118 us (2%)
    unnamed x20, waiting for transfers between devices  2210 us
    reduce_scatter x1, waiting for transfers between devices, body(): lax.psum_scatter(inner_t(hidden_b, grad_down_b), ('dp', 'seq'), scatter_d...  725 us
    all_gather x1, waiting for transfers between devices, body(): lax.all_gather(w_up, ('dp', 'seq'), axis=0, tiled=True)  214 us
    reduce_scatter x1, waiting for transfers between devices, body(): lax.psum_scatter(query_term, ('dp', 'seq'), scatter_dimension=0, tiled=True)  213 us
    reduce_scatter x1, waiting for transfers between devices, body(): lax.psum_scatter(output_term, ('dp', 'seq'), scatter_dimension=0, tiled=T...  211 us
    all_gather x1, waiting for transfers between devices, body(): lax.all_gather(w_down, ('dp', 'seq'), axis=0, tiled=True)  209 us
    ppermute x4, waiting for transfers between devices, shifted(): return lax.ppermute(block, axis, route)  152 us
    reduce_scatter x1, waiting for transfers between devices, body(): lax.psum_scatter(key_term, ('dp', 'seq'), scatter_dimension=0, tiled=True)  142 us
  transfers between devices with their start and end apart: 21, of which 17 were waited for; matrix products, arithmetic and copies ran while one was open for 12% of the time, Pallas kernels for 0%

commit v1 on v0

v1 whole, which is shorter than its diff:
```python
import functools

import jax
import jax.numpy as jnp
from jax import lax
from jax.experimental import pallas as pl
from jax.experimental.pallas import tpu as pltpu
from jax.sharding import PartitionSpec as P

KEY_VALUE_HEADS = 4
HEAD_DIM = 256
GROUP = 2
WINDOW = 4096
CHUNKS = 2

epsilon = 1e-06
softcap = 50.0
score_scale = HEAD_DIM ** (-0.5) / softcap
log2_scale = softcap * 1.4426950408889634
VMEM_LIMIT = 56 * 1024 * 1024
ANYWHERE = pl.BlockSpec(memory_space=pl.ANY)


def normed(values, gain_vec):
    inv_rms = lax.rsqrt(jnp.mean(values * values, axis=-1, keepdims=True) + epsilon)
    return values * inv_rms * gain_vec


def matmul(a, b):
    return jnp.dot(a, b, preferred_element_type=jnp.float32)


def matmul_t(a, b):
    return lax.dot_general(a, b, (((1,), (1,)), ((), ())), preferred_element_type=jnp.float32)


def inner_t(a, b):
    return lax.dot_general(a, b, (((0,), (0,)), ((), ())), preferred_element_type=jnp.float32)


def across(x, bits):
    return lax.ppermute(x, "dp", [(i, i ^ bits) for i in range(lax.axis_size("dp"))])


def swap_core(x):
    return lax.ppermute(x, "seq", [(i, i ^ 1) for i in range(lax.axis_size("seq"))])


def line_groups():
    count = lax.axis_size("seq")
    return [list(range(core, count, 2)) for core in (0, 1)]


def gather_line(x):
    return lax.all_gather(x, "seq", axis=0, axis_index_groups=line_groups())


def exchange_line(x, place):
    line = x.shape[0]
    parts = x
    for k in range(1, line):
        route = [
            (2 * i + core, 2 * ((i + k) % line) + core) for i in range(line) for core in (0, 1)
        ]
        moved = lax.ppermute(pick(x, 0, (place + k) % line), "seq", route)
        parts = put(parts, moved, (place + line - k) % line)
    return parts


def scatter_line(x):
    return lax.psum_scatter(x, "seq", scatter_dimension=0, axis_index_groups=line_groups())


def gather_quad_near(x):
    return across(x, 1), across(x, 2)


def gather_quad_far(one, two):
    half = one.shape[0] // 2
    return jnp.concatenate([across(two[:half], 1), across(one[half:], 2)], axis=0)


def gather_quad(x):
    one, two = gather_quad_near(x)
    return [x, one, two, gather_quad_far(one, two)]


def scatter_quad(parts):
    half = parts[0].shape[0] // 2
    low, high = [p[:half] for p in parts], [p[half:] for p in parts]
    from_one = across(jnp.stack([low[1], low[3]]), 1)
    from_two = across(jnp.stack([high[2], high[3]]), 2)
    low_rest = across(low[2] + from_one[1], 2)
    high_rest = across(high[1] + from_two[1], 1)
    f32 = jnp.float32
    return jnp.concatenate(
        [
            low[0].astype(f32) + from_one[0].astype(f32) + low_rest.astype(f32),
            high[0].astype(f32) + from_two[0].astype(f32) + high_rest.astype(f32),
        ],
        axis=0,
    )


def flip_order(x, bits):
    pairs = x.reshape((2, 2) + x.shape[1:])
    pairs = jnp.where(bits % 2 == 1, pairs[:, ::-1], pairs)
    pairs = jnp.where(bits // 2 == 1, pairs[::-1], pairs)
    return pairs.reshape(x.shape)


def exchange_quad(x, place):
    parts = flip_order(x, place)
    return exchange_quad_end([parts[0]] + [across(parts[k], k) for k in (1, 2, 3)], place)


def exchange_quad_end(parts, place):
    return flip_order(jnp.stack(parts), place)


def pick(x, axis, index):
    return lax.dynamic_index_in_dim(x, index, axis, keepdims=False)


def put(x, part, *index):
    for _ in index:
        part = part[None]
    return lax.dynamic_update_slice(x, part, index + (0,) * (x.ndim - len(index)))


def after(x, *others):
    def kernel(x_ref, *rest):
        rest[-1][...] = x_ref[...]

    return pl.pallas_call(
        kernel,
        in_specs=[pl.BlockSpec(memory_space=pltpu.VMEM)] + [ANYWHERE] * len(others),
        out_specs=pl.BlockSpec(memory_space=pltpu.VMEM),
        out_shape=jax.ShapeDtypeStruct(x.shape, x.dtype),
    )(x, *others)


def empty(shape, dtype):
    return pl.pallas_call(
        lambda out_ref: None, out_specs=ANYWHERE, out_shape=jax.ShapeDtypeStruct(shape, dtype)
    )()


class Order:
    def __init__(self):
        self.token = jnp.zeros((8, 128), jnp.float32)

    def __call__(self, *trees):
        leaves, tree = jax.tree.flatten(trees)
        held = pl.pallas_call(
            lambda *refs: None,
            in_specs=[ANYWHERE] * (1 + len(leaves)),
            out_specs=[ANYWHERE] * (1 + len(leaves)),
            out_shape=[jax.ShapeDtypeStruct(x.shape, x.dtype) for x in [self.token, *leaves]],
            input_output_aliases={i: i for i in range(1 + len(leaves))},
        )(self.token, *leaves)
        self.token = held[0]
        out = jax.tree.unflatten(tree, held[1:])
        return out[0] if len(trees) == 1 else out


def split_columns(gate, up, dp, line):
    rows, ff = gate.shape
    rest = ff // (dp * line)

    def kernel(gate_ref, up_ref, out_ref):
        for which, ref in enumerate((gate_ref, up_ref)):
            for i in range(dp):
                for j in range(line):
                    first = (i * line + j) * rest
                    out_ref[j, which, :, i * rest : (i + 1) * rest] = ref[:, first : first + rest]

    return pl.pallas_call(
        kernel,
        out_shape=jax.ShapeDtypeStruct((line, 2, rows, dp * rest), gate.dtype),
        compiler_params=pltpu.CompilerParams(vmem_limit_bytes=VMEM_LIMIT),
    )(gate, up)


def join_columns(parts, dp):
    line, _, rows, part = parts.shape
    rest = part // dp

    def kernel(parts_ref, gate_ref, up_ref):
        for which, ref in enumerate((gate_ref, up_ref)):
            for i in range(dp):
                for j in range(line):
                    first = (i * line + j) * rest
                    ref[:, first : first + rest] = parts_ref[
                        j, which, :, i * rest : (i + 1) * rest
                    ].astype(jnp.float32)

    return pl.pallas_call(
        kernel,
        out_shape=[jax.ShapeDtypeStruct((rows, line * part), jnp.float32)] * 2,
        compiler_params=pltpu.CompilerParams(vmem_limit_bytes=VMEM_LIMIT),
    )(parts)


def tile_facts(place, span, tile):
    line = pl.num_programs(0) // 2
    row_tokens = line * 2 * span
    half = tile // line
    key_first = half * row_tokens + (tile % line) * 2 * span
    query_first = [(place[2] ^ j) * row_tokens + (2 * place[0] + place[1]) * span for j in (0, 1)]
    return key_first, query_first


def reach(key_first, keys, query_first, queries):
    key_last, query_last = key_first + keys - 1, query_first + queries - 1
    live = (key_first <= query_last) & (query_first - key_last < WINDOW)
    plain = (key_last < query_first) & (query_last - key_first < WINDOW)
    return live & plain, live & jnp.logical_not(plain)


def forward_kernel(place, query_ref, own_ref, other_ref, code_ref, segment_ref, *rest):
    out_ref, log_ref, acc, total = rest[-4:]
    tile = pl.program_id(0)
    span = query_ref.shape[1]
    key_first, query_first = tile_facts(place, span, tile)

    @pl.when(tile == 0)
    def _():
        acc[...] = jnp.zeros_like(acc)
        total[...] = jnp.zeros_like(total)

    def step(j, masked):
        keys = jnp.concatenate([own_ref[0, 0, :, :HEAD_DIM], other_ref[0, 0, :, :HEAD_DIM]], axis=0)
        values = jnp.concatenate(
            [own_ref[0, 0, :, HEAD_DIM:], other_ref[0, 0, :, HEAD_DIM:]], axis=0
        )
        allowed = code_ref[0, 0] == segment_ref[j]
        if masked:
            lane = lax.broadcasted_iota(jnp.int32, (1, 2 * span), 1)
            key_pos = key_first + lane + jnp.where(lane < span, place[1], -place[1]) * span
            query_pos = query_first[j] + lax.broadcasted_iota(jnp.int32, (span, 1), 0)
            back = query_pos - key_pos
            allowed = (allowed & (back > 0) & (back < WINDOW)) | (back == 0)
        for h in range(GROUP):
            query = query_ref[j, :, h * HEAD_DIM : (h + 1) * HEAD_DIM]
            scores = matmul_t(query, keys)
            weights = jnp.exp2(log2_scale * jnp.tanh(scores * score_scale))
            weights = jnp.where(allowed, weights, 0.0)
            total[j, h] += jnp.sum(weights, axis=-1, keepdims=True)
            acc[j, h] += matmul(weights.astype(jnp.bfloat16), values)

    for j in (0, 1):
        plain, masked = reach(key_first, 2 * span, query_first[j], span)
        pl.when(plain)(functools.partial(step, j, False))
        pl.when(masked)(functools.partial(step, j, True))

    @pl.when(tile == pl.num_programs(0) - 1)
    def _():
        for j in (0, 1):
            for h in range(GROUP):
                out_ref[j, :, h * HEAD_DIM : (h + 1) * HEAD_DIM] = (
                    acc[j, h] / total[j, h]
                ).astype(jnp.bfloat16)
        log_ref[...] = jnp.log2(total[...])


def backward_kernel(
    place, query_ref, grad_ref, own_ref, other_ref, code_ref, stats_ref, segment_ref, *rest
):
    query_grad_ref, own_grad_ref, other_grad_ref = rest[-8:-5]
    queries, grads, query_acc, key_acc, value_acc = rest[-5:]
    tile = pl.program_id(0)
    span = query_ref.shape[1]
    key_first, query_first = tile_facts(place, span, tile)

    @pl.when(tile == 0)
    def _():
        query_acc[...] = jnp.zeros_like(query_acc)
        for j in (0, 1):
            for h in range(GROUP):
                rows, columns = pl.ds(h * span, span), slice(h * HEAD_DIM, (h + 1) * HEAD_DIM)
                queries[j, rows, :] = query_ref[j, :, columns]
                grads[j, rows, :] = grad_ref[j, :, columns]

    def step(j, side, side_first, keys, values, masked):
        allowed = code_ref[0, 0, pl.ds(side * span, span), :] == segment_ref[j, 0:1, :]
        if masked:
            lane = lax.broadcasted_iota(jnp.int32, (1, GROUP * span), 1)
            query_pos = query_first[j] + jnp.where(lane < span, lane, lane - span)
            key_pos = side_first + lax.broadcasted_iota(jnp.int32, (span, 1), 0)
            back = query_pos - key_pos
            allowed = (allowed & (back > 0) & (back < WINDOW)) | (back == 0)
        squashed = jnp.tanh(matmul_t(keys, queries[j]) * score_scale)
        weights = jnp.exp2(log2_scale * squashed - stats_ref[j, 0:1, :])
        weights = jnp.where(allowed, weights, 0.0)
        grad_weights = matmul_t(values, grads[j])
        value_acc[side] += matmul(weights.astype(jnp.bfloat16), grads[j])
        grad_scores = weights * (grad_weights - stats_ref[j, 1:2, :]) * (1.0 - squashed * squashed)
        grad_scores = grad_scores.astype(jnp.bfloat16)
        key_acc[side] += matmul(grad_scores, queries[j])
        query_acc[j] += inner_t(grad_scores, keys)

    key_acc[...] = jnp.zeros_like(key_acc)
    value_acc[...] = jnp.zeros_like(value_acc)
    scale = HEAD_DIM ** (-0.5)
    for side, key_ref, grad_out in ((0, own_ref, own_grad_ref), (1, other_ref, other_grad_ref)):
        side_first = key_first + (place[1] if side == 0 else 1 - place[1]) * span

        def on_side(j, masked, side=side, side_first=side_first, key_ref=key_ref):
            keys, values = key_ref[0, 0, :, :HEAD_DIM], key_ref[0, 0, :, HEAD_DIM:]
            step(j, side, side_first, keys, values, masked)

        for j in (0, 1):
            plain, masked = reach(side_first, span, query_first[j], span)
            pl.when(plain)(functools.partial(on_side, j, False))
            pl.when(masked)(functools.partial(on_side, j, True))
        grad_out[0, 0, :, :HEAD_DIM] = (key_acc[side] * scale).astype(jnp.bfloat16)
        grad_out[0, 0, :, HEAD_DIM:] = value_acc[side].astype(jnp.bfloat16)

    @pl.when(tile == pl.num_programs(0) - 1)
    def _():
        for j in (0, 1):
            for h in range(GROUP):
                query_grad_ref[j, :, h * HEAD_DIM : (h + 1) * HEAD_DIM] = (
                    query_acc[j, h * span : (h + 1) * span, :] * scale
                ).astype(jnp.bfloat16)


def whole(*shape):
    return pl.BlockSpec(shape, lambda tile, place: (0,) * len(shape))


def tile_specs(line, span):
    def key_place(tile, place):
        return (tile % line, (tile // line) ^ place[2], 0, 0)

    def code_place(tile, place):
        return ((tile // line) ^ place[2], tile % line, 0, 0)

    return pl.BlockSpec((1, 1, span, 2 * HEAD_DIM), key_place), code_place


def attention_forward(place, queries, own, other, codes, segments, *first):
    line, _, span, width = own.shape
    tile_spec, code_place = tile_specs(line, span)
    pairs = 2 * span * line * 2 * span * GROUP
    return pl.pallas_call(
        forward_kernel,
        grid_spec=pltpu.PrefetchScalarGridSpec(
            num_scalar_prefetch=1,
            grid=(2 * line,),
            in_specs=[
                whole(2, span, width),
                tile_spec,
                tile_spec,
                pl.BlockSpec((1, 1, 1, 2 * span), code_place),
                whole(2, span, 1),
            ]
            + [ANYWHERE] * len(first),
            out_specs=[whole(2, span, width), whole(2, GROUP, span, 1)],
            scratch_shapes=[
                pltpu.VMEM((2, GROUP, span, HEAD_DIM), jnp.float32),
                pltpu.VMEM((2, GROUP, span, 1), jnp.float32),
            ],
        ),
        out_shape=[
            jax.ShapeDtypeStruct((2, span, width), jnp.bfloat16),
            jax.ShapeDtypeStruct((2, GROUP, span, 1), jnp.float32),
        ],
        compiler_params=pltpu.CompilerParams(vmem_limit_bytes=VMEM_LIMIT),
        cost_estimate=pl.CostEstimate(
            flops=4 * HEAD_DIM * pairs, bytes_accessed=12 << 20, transcendentals=2 * pairs
        ),
    )(place, queries, own, other, codes, segments, *first)


def attention_backward(place, queries, grads, own, other, codes, stats, segments, *first):
    line, _, span, width = own.shape
    tile_spec, code_place = tile_specs(line, span)
    pairs = 2 * span * line * 2 * span * GROUP
    return pl.pallas_call(
        backward_kernel,
        grid_spec=pltpu.PrefetchScalarGridSpec(
            num_scalar_prefetch=1,
            grid=(2 * line,),
            in_specs=[
                whole(2, span, width),
                whole(2, span, width),
                tile_spec,
                tile_spec,
                pl.BlockSpec((1, 1, 2 * span, 1), code_place),
                whole(2, 8, GROUP * span),
                whole(2, 8, GROUP * span),
            ]
            + [ANYWHERE] * len(first),
            out_specs=[whole(2, span, width), tile_spec, tile_spec],
            scratch_shapes=[
                pltpu.VMEM((2, GROUP * span, HEAD_DIM), jnp.bfloat16),
                pltpu.VMEM((2, GROUP * span, HEAD_DIM), jnp.bfloat16),
                pltpu.VMEM((2, GROUP * span, HEAD_DIM), jnp.float32),
                pltpu.VMEM((2, span, HEAD_DIM), jnp.float32),
                pltpu.VMEM((2, span, HEAD_DIM), jnp.float32),
            ],
        ),
        out_shape=[
            jax.ShapeDtypeStruct((2, span, width), jnp.bfloat16),
            jax.ShapeDtypeStruct(own.shape, jnp.bfloat16),
            jax.ShapeDtypeStruct(own.shape, jnp.bfloat16),
        ],
        compiler_params=pltpu.CompilerParams(vmem_limit_bytes=VMEM_LIMIT),
        cost_estimate=pl.CostEstimate(
            flops=10 * HEAD_DIM * pairs, bytes_accessed=20 << 20, transcendentals=2 * pairs
        ),
    )(place, queries, grads, own, other, codes, stats, segments, *first)


def body(
    tokens, pre_attention, post_attention, pre_feedforward, post_feedforward, w_query, key_weight,
    value_weight, w_output, w_gate, w_up, w_down, document_index, token_padding_mask, cotangent,
):
    bf16, f32 = jnp.bfloat16, jnp.float32
    dp, seq = lax.axis_size("dp"), lax.axis_size("seq")
    line, groups = seq // 2, dp // KEY_VALUE_HEADS
    dp_at, seq_at = lax.axis_index("dp"), lax.axis_index("seq")
    line_at, core = seq_at // 2, seq_at % 2
    head = dp_at % KEY_VALUE_HEADS
    half_bit = dp_at % 2
    _, span, model = tokens.shape
    rows = w_query.shape[0]
    ff = w_gate.shape[1]
    ff_rows = w_down.shape[0]
    ff_part = ff // line
    width = GROUP * HEAD_DIM

    order = Order()

    def attention_codes():
        sequence = dp_at // 2

        def by_pair(table):
            both = jnp.stack([pick(table, 0, sequence), pick(table, 0, sequence ^ 1)])
            both = both.reshape(2, 2, line, 2, span)
            both = jnp.where(half_bit == 1, both[:, ::-1], both)
            return jnp.where(core == 1, both[:, :, :, ::-1], both)

        segments = by_pair(document_index)
        codes = jnp.where(by_pair(token_padding_mask) == 1, segments, -1)
        return codes.reshape(2, 2, line, 2 * span), pick(segments[:, :, :, 0], 2, line_at)

    inputs = tokens[0].astype(f32)
    normed_in = normed(inputs, pre_attention).astype(bf16)
    blocks = jnp.concatenate(
        [
            w_query.reshape(rows, KEY_VALUE_HEADS, width),
            key_weight.reshape(rows, KEY_VALUE_HEADS, HEAD_DIM),
            value_weight.reshape(rows, KEY_VALUE_HEADS, HEAD_DIM),
        ],
        axis=2,
    ).transpose(1, 0, 2)

    if groups == 1:
        flipped = flip_order(blocks, head)
        normed_in, flipped = order(normed_in, flipped)
        near_normed = gather_quad_near(normed_in)
        mixed = [flipped[0]] + [across(flipped[k], k) for k in (1, 2, 3)]
        split = split_columns(w_gate, w_up, dp, line)
        mixed = exchange_quad_end(mixed, head)
        mixed, split = order(mixed, split)
        in_weight = lax.all_gather(mixed, "seq", axis=1).reshape(model, 2 * width)
    else:
        near_normed = gather_quad_near(normed_in)
        split = split_columns(w_gate, w_up, dp, line)
        in_weight = pick(lax.all_gather(blocks, ("dp", "seq"), axis=1, tiled=True), 0, head)

    per_device = line * rows
    gate_up = exchange_line(split.reshape(line, 2 * rows, ff_part), line_at)
    gate_up = gate_up.reshape(line, 2, rows, ff_part).transpose(1, 0, 2, 3)
    gate_up = gate_up.reshape(2 * per_device, ff_part)

    def near_blocks(own):
        return gather_quad_near(own) if groups == 1 else (lax.all_gather(own, "dp", axis=0),)

    def far_blocks(near):
        return (gather_quad_far(*near),) if groups == 1 else ()

    def swap_all(blocks):
        return [swap_core(block) for block in blocks]

    down_weight = empty((dp, 2, ff_rows, model), bf16)
    gate_weight = empty((dp, line, 2, rows, ff_part), bf16)
    up_weight = empty((dp, line, 2, rows, ff_part), bf16)

    def fill_down(weight, numbers, mine, swapped):
        for k, *sides in zip(numbers, mine, swapped):
            for block, side in zip(sides, (core, 1 - core)):
                at = head ^ k if groups == 1 else 0
                weight = lax.dynamic_update_slice(
                    weight, block.reshape(-1, 1, ff_rows, model), (at, side, 0, 0)
                )
        return weight

    def fill_in(gate, up, numbers, mine, swapped):
        for k, *sides in zip(numbers, mine, swapped):
            for block, side in zip(sides, (core, 1 - core)):
                at = head ^ k if groups == 1 else 0
                block = block.reshape(-1, 2, line, 1, rows, ff_part)
                gate = lax.dynamic_update_slice(gate, block[:, 0], (at, 0, side, 0, 0))
                up = lax.dynamic_update_slice(up, block[:, 1], (at, 0, side, 0, 0))
        return gate, up

    near_normed = order(near_normed)
    far_normed = gather_quad_far(*near_normed)
    first_rows = jnp.concatenate([normed_in, near_normed[0]], axis=0)
    far_normed, near_two, first_rows = order(far_normed, near_normed[1], first_rows)
    own_down = after(w_down, far_normed)
    near_down = near_blocks(own_down)
    second_rows = jnp.concatenate([near_two, far_normed], axis=0)
    second_rows, in_weight, first_rows = order(second_rows, in_weight, first_rows)

    def project(pair_rows):
        projected = matmul(pair_rows, in_weight).astype(bf16).reshape(2, span, 2 * width)
        return projected[..., :width], projected[..., width:]

    first_queries, first_keys = project(first_rows)
    first_queries, first_keys, second_rows, first_rows = order(
        first_queries, first_keys, second_rows, first_rows
    )
    first_own = gather_line(first_keys)
    second_queries, second_keys = project(second_rows)
    near_down, second_queries, second_keys = order(near_down, second_queries, second_keys)
    far_down = far_blocks(near_down)
    second_own = gather_line(second_keys)
    if groups == 1:
        out_weight = lax.all_gather(
            after(w_output, second_keys), "seq", axis=0, tiled=True
        )
    else:
        out_weight = lax.dynamic_slice_in_dim(
            lax.all_gather(w_output, ("dp", "seq"), axis=0, tiled=True), head * width, width
        )
    normed_rows = [first_rows, second_rows]

    gate_up, own_down, far_down = order(gate_up, own_down, far_down)
    near_in = near_blocks(gate_up)
    mine_down = ([own_down] if groups == 1 else []) + list(near_down) + list(far_down)
    swapped = swap_all(mine_down[:2])
    down_weight = fill_down(down_weight, (0, 1), mine_down[:2], swapped)
    first_own, down_weight = order(first_own, down_weight)
    first_other = swap_core(first_own)
    codes, own_segments = attention_codes()
    place = jnp.stack([line_at, core, half_bit]).astype(jnp.int32)
    row_codes = codes[:, :, :, None, :]
    column_segments = own_segments[..., None]
    first_other, place, row_codes, column_segments = order(
        first_other, place, row_codes, column_segments
    )
    swapped = swap_all(mine_down[2:])
    attended, log_total = [None, None], [None, None]
    attended[0], log_total[0] = attention_forward(
        place, first_queries, first_own, first_other, row_codes[0], column_segments[0]
    )
    attended[0], swapped = order(attended[0], swapped)
    down_weight = fill_down(down_weight, (2, 3), mine_down[2:], swapped)
    if groups == 1:
        swapped = swap_all([gate_up])
        gate_weight, up_weight = fill_in(gate_weight, up_weight, (0,), [gate_up], swapped)
    near_in, second_own, down_weight, gate_weight, up_weight = order(
        near_in, second_own, down_weight, gate_weight, up_weight
    )
    second_other = swap_core(second_own)
    far_in = far_blocks(near_in)
    second_other = order(second_other)
    swapped = swap_all(near_in)
    attended[1], log_total[1] = attention_forward(
        place, second_queries, second_own, second_other, row_codes[1], column_segments[1]
    )
    queries = [first_queries, second_queries]
    own_keys, other_keys = [first_own, second_own], [first_other, second_other]
    attended, log_total, out_weight, swapped, far_in = order(
        attended, log_total, out_weight, swapped, far_in
    )
    numbers = (1, 2, 3) if groups == 1 else (0,)

    def activation(gate_in, up_in):
        return jax.nn.gelu(gate_in, approximate=True) * up_in

    step = span // CHUNKS
    chunks = [slice(c * step, (c + 1) * step) for c in range(CHUNKS)]
    grad_output = cotangent[0].astype(f32)
    attn_outs, residuals, mids = [], [], []
    for c, part in enumerate(chunks):
        parts = []
        for pair in (0, 1):
            rows_of = attended[pair][:, part].reshape(2 * step, width)
            parts += list(matmul(rows_of, out_weight).astype(bf16).reshape(2, step, model))
        if c == 0:
            parts = order(parts)
        attn_outs.append(scatter_quad(parts))
        residuals.append(inputs[part] + normed(attn_outs[-1], post_attention))
        mids.append(normed(residuals[-1], pre_feedforward).astype(bf16))
        if c == 0:
            gate_weight, up_weight = fill_in(
                gate_weight, up_weight, numbers[:2], near_in, swapped
            )
            swapped = swap_all(far_in)
            mids[0], swapped, gate_weight, up_weight = order(
                mids[0], swapped, gate_weight, up_weight
            )
        if c == 1:
            gate_weight, up_weight = fill_in(gate_weight, up_weight, numbers[2:], far_in, swapped)
    down_weight = down_weight.reshape(ff_part, model)
    gate_weight = gate_weight.reshape(model, ff_part)
    up_weight = up_weight.reshape(model, ff_part)

    results, kept, grad_mids = [], [], []
    grad_post_ff = grad_pre_ff = grad_post_attn = 0.0
    for c, part in enumerate(chunks):
        mid_rows = gather_line(mids[c]).reshape(line * step, model)
        gate_value, up_value = matmul(mid_rows, gate_weight), matmul(mid_rows, up_weight)
        hidden = activation(gate_value, up_value).astype(bf16)
        down_part = matmul(hidden, down_weight).astype(bf16).reshape(line, step, model)
        down_out = scatter_line(down_part).astype(f32)
        normed_down, down_back = jax.vjp(normed, down_out, post_feedforward)
        results.append(residuals[c] + normed_down)
        grad_down, gain_part = down_back(grad_output[part])
        grad_post_ff += gain_part
        down_rows = gather_line(grad_down.astype(bf16)).reshape(line * step, model)
        grad_hidden = matmul_t(down_rows, down_weight)
        _, act_back = jax.vjp(activation, gate_value, up_value)
        grad_gate, grad_up = act_back(grad_hidden)
        grad_gate, grad_up = grad_gate.astype(bf16), grad_up.astype(bf16)
        mid_part = matmul_t(grad_gate, gate_weight) + matmul_t(grad_up, up_weight)
        mid_part = mid_part.astype(bf16).reshape(line, step, model)
        kept.append((mid_rows, hidden, down_rows, grad_gate, grad_up))
        if c == CHUNKS - 1:
            mid_part, kept = order(mid_part, kept)
        grad_mids.append(scatter_line(mid_part).astype(f32))
    result = jnp.concatenate(results, axis=0)

    mid_rows, hidden, down_rows, grad_gate, grad_up = (
        jnp.concatenate(parts, axis=0) for parts in zip(*kept)
    )
    down_term = inner_t(hidden, down_rows).astype(bf16).reshape(dp, 2, ff_rows, model)
    in_terms = [
        inner_t(mid_rows, grad).astype(bf16).reshape(dp, line, 2, rows, ff_part)
        for grad in (grad_gate, grad_up)
    ]
    *in_terms, down_term, grad_mids = order(*in_terms, down_term, grad_mids)
    in_swapped = [swap_core(pick(term, 2, 1 - core)) for term in in_terms]
    down_swapped = swap_core(pick(down_term, 1, 1 - core))

    grad_residuals, outputs_quad = [], []
    for c, part in enumerate(chunks):
        _, mid_back = jax.vjp(normed, residuals[c], pre_feedforward)
        grad_residual, gain_part = mid_back(grad_mids[c])
        grad_pre_ff += gain_part
        grad_residuals.append(grad_output[part] + grad_residual)
        _, attn_back = jax.vjp(normed, attn_outs[c], post_attention)
        grad_attn, gain_part = attn_back(grad_residuals[-1])
        grad_post_attn += gain_part
        outputs_quad.append(gather_quad(grad_attn.astype(bf16)))
    grad_residual = jnp.concatenate(grad_residuals, axis=0)

    def owned_gains(terms):
        terms = jnp.stack(terms, axis=1)
        count = terms.shape[1]
        if groups > 1:
            return lax.psum_scatter(terms, ("dp", "seq"), scatter_dimension=0, tiled=True)
        terms = terms.reshape(dp, line, 2, rows * count)
        terms = sum(
            (across(pick(terms, 0, head ^ k), k) for k in (1, 2, 3)), pick(terms, 0, head)
        )
        terms = pick(terms, 1, core) + swap_core(pick(terms, 1, 1 - core))
        return jnp.sum(exchange_line(terms, line_at), axis=0).reshape(rows, count)

    outputs_quad, in_swapped, down_swapped, in_terms, down_term = order(
        outputs_quad, in_swapped, down_swapped, in_terms, down_term
    )
    early_gains = owned_gains([grad_post_attn, grad_pre_ff, grad_post_ff])

    grad_attended, stats, output_term = [], [], 0.0
    for pair in (0, 1):
        attn_rows = jnp.concatenate(
            [quad[2 * pair + j] for j in (0, 1) for quad in outputs_quad], axis=0
        )
        output_term += inner_t(attended[pair].reshape(2 * span, width), attn_rows)
        grad_attended.append(matmul_t(attn_rows, out_weight).astype(bf16).reshape(2, span, width))
        delta = (grad_attended[pair].astype(f32) * attended[pair].astype(f32)).reshape(
            2, span, GROUP, HEAD_DIM
        )
        delta = jnp.sum(delta, axis=-1).transpose(0, 2, 1)
        stat = jnp.stack(
            [log_total[pair].reshape(2, GROUP * span), delta.reshape(2, GROUP * span)], axis=1
        )
        stats.append(jnp.pad(stat, ((0, 0), (0, 6), (0, 0))))
    output_term = output_term.astype(bf16)
    lane_segments = jnp.broadcast_to(
        own_segments[:, :, None, None, :], (2, 2, 8, GROUP, span)
    ).reshape(2, 2, 8, GROUP * span)
    column_codes = codes[..., None]
    output_term, early_gains, grad_attended, stats, lane_segments, column_codes = order(
        output_term, early_gains, grad_attended, stats, lane_segments, column_codes
    )
    if groups == 1:
        output_shard = lax.psum_scatter(output_term, "seq", scatter_dimension=0, tiled=True)
    else:
        spread = jnp.zeros((KEY_VALUE_HEADS, width, model), bf16).at[head].set(output_term)
        output_shard = lax.psum_scatter(
            spread.reshape(KEY_VALUE_HEADS * width, model),
            ("dp", "seq"),
            scatter_dimension=0,
            tiled=True,
        )

    def scatter_near(parts):
        half = parts[0].shape[0] // 2
        low, high = [p[:half] for p in parts], [p[half:] for p in parts]
        return across(jnp.stack([low[1], low[3]]), 1), across(jnp.stack([high[2], high[3]]), 2)

    def scatter_far(parts, from_one, from_two):
        half = parts[0].shape[0] // 2
        return across(parts[2][:half] + from_one[1], 2), across(parts[1][half:] + from_two[1], 1)

    def scatter_end(parts, from_one, from_two, low_rest, high_rest):
        half = parts[0].shape[0] // 2
        low = parts[0][:half].astype(f32) + from_one[0].astype(f32) + low_rest.astype(f32)
        high = parts[0][half:].astype(f32) + from_two[0].astype(f32) + high_rest.astype(f32)
        return jnp.concatenate([low, high], axis=0)

    def attend_back(pair):
        return attention_backward(
            place, queries[pair], grad_attended[pair], own_keys[pair], other_keys[pair],
            column_codes[pair], stats[pair], lane_segments[pair],
        )

    down_mine = pick(down_term, 1, core) + down_swapped
    in_mine = [
        (pick(term, 2, core) + swapped).reshape(dp, per_device, ff_part)
        for term, swapped in zip(in_terms, in_swapped)
    ]
    in_mine = jnp.concatenate(in_mine, axis=1)
    grad_queries, key_grads = [None, None], [None, None]
    if groups == 1:
        down_parts = [pick(down_mine, 0, head ^ k) for k in range(4)]
        in_parts = [pick(in_mine, 0, head ^ k) for k in range(4)]
        down_near = scatter_near(down_parts)
    grad_queries[0], own_grad, other_grad = attend_back(0)
    grad_queries[0], own_grad, other_grad = order(grad_queries[0], own_grad, other_grad)
    swapped = swap_core(other_grad)
    if groups == 1:
        in_near = scatter_near(in_parts)
    swapped = order(swapped)
    key_grads[0] = scatter_line(own_grad + swapped)
    grad_queries[1], own_grad, other_grad = attend_back(1)
    if groups == 1:
        down_near, grad_queries[1], own_grad, other_grad = order(
            down_near, grad_queries[1], own_grad, other_grad
        )
        down_far = scatter_far(down_parts, *down_near)
    swapped = order(swap_core(other_grad))
    key_grads[1] = scatter_line(own_grad + swapped)
    if groups == 1:
        in_near, down_far = order(in_near, down_far)
        down_shard = scatter_end(down_parts, *down_near, *down_far)
        in_far = scatter_far(in_parts, *in_near)
    else:
        down_shard = lax.psum_scatter(down_mine, "dp", scatter_dimension=0).astype(f32)
        in_shard = lax.psum_scatter(in_mine, "dp", scatter_dimension=0)

    def project_back(pair):
        grad_projected = jnp.concatenate([grad_queries[pair], key_grads[pair]], axis=2)
        grad_projected = grad_projected.reshape(2 * span, 2 * width)
        part = matmul_t(grad_projected, in_weight).astype(bf16).reshape(2, span, model)
        return grad_projected, list(part)

    key_grads[0] = order(key_grads[0])
    first_grad, first_parts = project_back(0)
    in_term = inner_t(normed_rows[0], first_grad)
    if groups == 1:
        in_far, first_grad, first_parts, in_term = order(in_far, first_grad, first_parts, in_term)
        in_shard = scatter_end(in_parts, *in_near, *in_far).astype(bf16)
    key_grads[1], in_shard, in_term = order(key_grads[1], in_shard, in_term)
    second_grad, second_parts = project_back(1)
    parts = order(first_parts + second_parts)
    in_near = scatter_near(parts)
    in_term = (in_term + inner_t(normed_rows[1], second_grad)).astype(bf16)
    in_shard = in_shard.reshape(2, line, rows, ff_part).transpose(1, 0, 2, 3)
    if groups == 1:
        in_part = lax.psum_scatter(
            in_term.reshape(KEY_VALUE_HEADS, seq, rows, 2 * width).transpose(1, 0, 2, 3), "seq"
        )
    in_shard = exchange_line(in_shard, line_at)
    in_near = order(in_near)
    in_far = scatter_far(parts, *in_near)
    grad_in = scatter_end(parts, *in_near, *in_far)
    _, in_back = jax.vjp(normed, inputs, pre_attention)
    grad_inputs, grad_pre_attn = in_back(grad_in)
    tokens_grad = grad_residual + grad_inputs
    late_gains = owned_gains([grad_pre_attn])
    gate_shard, up_shard = join_columns(in_shard, dp)
    if groups == 1:
        part_shard = exchange_quad(in_part, head)
    else:
        spread = jnp.zeros((KEY_VALUE_HEADS, model, 2 * width), bf16).at[head].set(in_term)
        part_shard = lax.psum_scatter(spread, ("dp", "seq"), scatter_dimension=1, tiled=True)
    part_shard = part_shard.astype(f32).transpose(1, 0, 2)
    query_shard = part_shard[..., :width].reshape(rows, KEY_VALUE_HEADS * width)
    key_shard = part_shard[..., width : width + HEAD_DIM].reshape(rows, KEY_VALUE_HEADS * HEAD_DIM)
    value_shard = part_shard[..., width + HEAD_DIM :].reshape(rows, KEY_VALUE_HEADS * HEAD_DIM)
    return (
        result[None],
        tokens_grad[None],
        query_shard,
        key_shard,
        value_shard,
        output_shard.astype(f32),
        gate_shard,
        up_shard,
        down_shard,
        late_gains[:, 0],
        early_gains[:, 0],
        early_gains[:, 1],
        early_gains[:, 2],
    )


def solution(mesh):
    tokens, weights, whole_copy = P("dp", "seq", None), P(("dp", "seq"), None), P()
    gains = P(("dp", "seq"))
    return jax.shard_map(
        body,
        mesh=mesh,
        in_specs=(tokens,) + (whole_copy,) * 4 + (weights,) * 7 + (whole_copy,) * 2 + (tokens,),
        out_specs=(tokens,) * 2 + (weights,) * 7 + (gains,) * 4,
        check_vma=False,
    )
```

time: 5620 us -> 1500 us (0.27)
  waiting for transfers between devices: 4660 us -> 696 us
  matrix products: 481 us -> 275 us
  other arithmetic: 283 us -> 146 us
  starting transfers between devices: 14.8 us -> 107 us
  Pallas kernels: 0 us -> 71.3 us
    unnamed x20 -> x17, waiting for transfers between devices: 2210 us -> 63.2 us
    reduce_scatter x5 -> x7, waiting for transfers between devices: 1430 us -> 143 us  [the longest x6 143 us: scatter_line(): lax.psum_scatter(x, 'seq', scatter_dimension=0, axis_index_groups=line_gr...]
    all_gather x9 -> x8, waiting for transfers between devices: 860 us -> 178 us  [the longest x6 157 us: gather_line(): return lax.all_gather(x, 'seq', axis=0, axis_index_groups=line_groups())]
    dot_general x27 -> x29, matrix products: 481 us -> 275 us  [the longest x10 108 us: matmul_t(): lax.dot_general(a, b, (((1,), (1,)), ((), ())), preferred_element_type=jn...]
    ppermute x4 -> x81, waiting for transfers between devices: 152 us -> 312 us  [the longest x52 279 us: across(): lax.ppermute(x, 'dp', [(i, i ^ bits) for i in range(lax.axis_size('dp'))])]
    concatenate x3 -> x12, other arithmetic: 138 us -> 23.9 us  [the longest x5 7.96 us: gather_quad_far(): jnp.concatenate([across(two[:half], 1), across(one[half:], 2)], axis=0)]
    ppermute x4 -> x81, starting transfers between devices: 14.1 us -> 105 us  [the longest x52 59.6 us: across(): lax.ppermute(x, 'dp', [(i, i ^ bits) for i in range(lax.axis_size('dp'))])]
    sub x1 -> x0, other arithmetic: 75.3 us -> none  [attention_backward(): grad_capped = probabilities * (grad_probs - delta)]
  transfers between devices with their start and end apart: 21 -> 97, of which waited for: 17 -> 47; matrix products, arithmetic and copies ran while one was open for 12% -> 27% of each run, Pallas kernels for 0% -> 5%
where the time goes in v1:
time: 1500 us; the launch traced here: 1490 us
  waiting for transfers between devices  696 us (46%)
  matrix products  275 us (18%)
  local copies, waits for them, and re-layouts  173 us (12%)
  other arithmetic  146 us (10%)
  starting transfers between devices  107 us (7%)
  Pallas kernels  71.3 us (5%)
  between operations  16.8 us (1%)
    ppermute x52, waiting for transfers between devices, across(): lax.ppermute(x, 'dp', [(i, i ^ bits) for i in range(lax.axis_size('dp'))])  279 us
    all_gather x6, waiting for transfers between devices, gather_line(): return lax.all_gather(x, 'seq', axis=0, axis_index_groups=line_groups())  157 us
    reduce_scatter x6, waiting for transfers between devices, scatter_line(): lax.psum_scatter(x, 'seq', scatter_dimension=0, axis_index_groups=line_gr...  143 us
    dot_general x10, matrix products, matmul_t(): lax.dot_general(a, b, (((1,), (1,)), ((), ())), preferred_element_type=jn...  108 us
    dot_general x12, matrix products, matmul(): return jnp.dot(a, b, preferred_element_type=jnp.float32)  87.7 us
    dot_general x7, matrix products, inner_t(): lax.dot_general(a, b, (((0,), (0,)), ((), ())), preferred_element_type=jn...  78.8 us
    unnamed x17, waiting for transfers between devices  63.2 us
    ppermute x52, starting transfers between devices, across(): lax.ppermute(x, 'dp', [(i, i ^ bits) for i in range(lax.axis_size('dp'))])  59.6 us
  transfers between devices with their start and end apart: 97, of which 47 were waited for; matrix products, arithmetic and copies ran while one was open for 27% of the time, Pallas kernels for 5%

profile of v1, /device:TPU:0, one launch (start us, length us, event | category | flops | bytes accessed | tf_op | source)
XLA Modules:
  0.0 1485.1 jit_solution(8988061522191363412)
XLA Ops:
  35.9 26.9 %collective-permute-done.3.refs_1_ = bf16[320,2304]{1,0:T(8,128)(2,1)} collective-permute-done((bf16[320,2304]{1,0:T(8,128)(2,1)S(1)}, bf16[320,2304]{1,0:T(8,128)(2,1)}, u32[]{:S(2)}, u32[]{:S(2)}) %collective-permute-start.3) | collective-permute-done | bytes 1474592 | tf_op jit(solution)/shard_map/ppermute | solution.py:42
  92.2 21.1 %all-gather.18.cloned.1.call-done = bf16[4,576,1024]{2,1,0:T(8,128)(2,1)} async-done(((bf16[4,72,1024]{2,1,0:T(8,128)(2,1)}), bf16[4,576,1024]{2,1,0:T(8,128)(2,1)}) %all-gather.18.cloned.1.call-update) | async-done | bytes 4718608 | tf_op jit(solution)/shard_map/all_gather | solution.py:469
  134.1 21.6 %collective-permute-done.7.refs_1_ = bf16[288,2304]{1,0:T(8,128)(2,1)} collective-permute-done((bf16[288,2304]{1,0:T(8,128)(2,1)}, bf16[288,2304]{1,0:T(8,128)(2,1)}, u32[]{:S(2)}, u32[]{:S(2)}) %collective-permute-start.7) | collective-permute-done | bytes 1327136 | tf_op jit(solution)/shard_map/ppermute | solution.py:42
  223.4 29.1 %collective-permute-done.19.refs_1_ = bf16[576,2304]{1,0:T(8,128)(2,1)} collective-permute-done((bf16[576,2304]{1,0:T(8,128)(2,1)S(1)}, bf16[576,2304]{1,0:T(8,128)(2,1)}, u32[]{:S(2)}, u32[]{:S(2)}) %collective-permute-start.19) | collective-permute-done | bytes 2654240 | tf_op jit(solution)/shard_map/ppermute | solution.py:42
  258.4 29.4 %collective-permute-done.25 = bf16[288,2304]{1,0:T(8,128)(2,1)S(1)} collective-permute-done((bf16[288,2304]{1,0:T(8,128)(2,1)S(1)}, bf16[288,2304]{1,0:T(8,128)(2,1)S(1)}, u32[]{:S(2)}, u32[]{:S(2)}) %collective-permute-start.25) | collective-permute-done | bytes 1327136 | tf_op jit(solution)/shard_map/ppermute | solution.py:42
  347.2 15.5 %collective-permute-done.29 = bf16[2,80,2304]{2,1,0:T(8,128)(2,1)S(1)} collective-permute-done((bf16[2,80,2304]{2,1,0:T(8,128)(2,1)S(1)}, bf16[2,80,2304]{2,1,0:T(8,128)(2,1)S(1)}, u32[]{:S(2)}, u32[]{:S(2)}) %collective-permute-start.29) | collective-permute-done | bytes 737312 | tf_op jit(solution)/shard_map/ppermute | solution.py:42
  400.7 40.3 %all-gather.26.cloned.1.call-done.refs_7_ = bf16[640,2304]{1,0:T(8,128)(2,1)} async-done(((bf16[160,2304]{1,0:T(8,128)(2,1)}), bf16[640,2304]{1,0:T(8,128)(2,1)}) %all-gather.26.cloned.1.call-update) | async-done | bytes 2949136 | tf_op jit(solution)/shard_map/all_gather | solution.py:55
  441.0 13.7 fusion.132
  475.8 25.6 %all-gather.24.cloned.1.call-done.refs_2_ = bf16[640,2304]{1,0:T(8,128)(2,1)} async-done(((bf16[160,2304]{1,0:T(8,128)(2,1)}), bf16[640,2304]{1,0:T(8,128)(2,1)}) %all-gather.24.cloned.1.call-update) | async-done | bytes 2949136 | tf_op jit(solution)/shard_map/all_gather | solution.py:55
  512.9 14.7 multiply_convert_fusion.3
  537.7 21.9 %reduce-scatter.11.cloned.1.call-done = bf16[1,160,2304]{2,1,0:T(8,128)(2,1)} async-done(((bf16[4,160,2304]{2,1,0:T(8,128)(2,1)}), bf16[1,160,2304]{2,1,0:T(8,128)(2,1)}) %reduce-scatter.11.cloned.1.call-update) | async-done | bytes 737296 | tf_op jit(solution)/shard_map/reduce_scatter | solution.py:71
  561.0 58.2 %reduce-scatter.9.cloned.1.call-done = bf16[1,160,2304]{2,1,0:T(8,128)(2,1)} async-done(((bf16[4,160,2304]{2,1,0:T(8,128)(2,1)}), bf16[1,160,2304]{2,1,0:T(8,128)(2,1)}) %reduce-scatter.9.cloned.1.call-update) | async-done | bytes 737296 | tf_op jit(solution)/shard_map/reduce_scatter | solution.py:71
  627.4 59.7 %all-gather.28.cloned.1.call-done.refs_9_ = bf16[640,2304]{1,0:T(8,128)(2,1)} async-done(((bf16[160,2304]{1,0:T(8,128)(2,1)}), bf16[640,2304]{1,0:T(8,128)(2,1)}) %all-gather.28.cloned.1.call-update) | async-done | bytes 2949136 | tf_op jit(solution)/shard_map/all_gather | solution.py:55
  687.1 19.1 %multiply_convert_fusion.1 = (bf16[640,2304]{1,0:T(8,128)(2,1)}, bf16[640,2304]{1,0:T(8,128)(2,1)}) fusion(f32[640,2304]{1,0:T(8,128)} %fusion.132, f32[640,2304]{1,0:T(8,128)} %get-tuple-element.498, bf16[640,2304]{1,0:T(8,128)(2,1)} %all-gather.28.cloned.1.call-done.refs_9_, bf16[2304,2304]{1,0:T(8,128)(2,1)} %bitcast.511), kind=kOutput, calls=%fused_computation.45 | convolution fusion | flops 6830161920 | bytes 31260672 | tf_op jit(solution)/shard_map/dot_general | solution.py:34
  716.5 31.5 %all-gather.30.cloned.1.call-done.refs_4_ = bf16[640,2304]{1,0:T(8,128)(2,1)} async-done(((bf16[160,2304]{1,0:T(8,128)(2,1)}), bf16[640,2304]{1,0:T(8,128)(2,1)}) %all-gather.30.cloned.1.call-update) | async-done | bytes 2949136 | tf_op jit(solution)/shard_map/all_gather | solution.py:55
  748.0 17.1 %multiply_convert_fusion = (bf16[640,2304]{1,0:T(8,128)(2,1)S(1)}, bf16[640,2304]{1,0:T(8,128)(2,1)S(1)}) fusion(f32[640,2304]{1,0:T(8,128)} %copy-done.150, f32[640,2304]{1,0:T(8,128)} %get-tuple-element.496, bf16[640,2304]{1,0:T(8,128)(2,1)} %all-gather.30.cloned.1.call-done.refs_4_, bf16[2304,2304]{1,0:T(8,128)(2,1)} %bitcast.512), kind=kOutput, calls=%fused_computation.43 | convolution fusion | flops 6830161920 | bytes 31260672 | tf_op jit(solution)/shard_map/dot_general | solution.py:34
  765.2 14.6 fusion.134
  779.8 15.5 %add_convert_fusion.2 = bf16[640,2304]{1,0:T(8,128)(2,1)} fusion(f32[640,2304]{1,0:T(8,128)} %fusion.133, bf16[640,2304]{1,0:T(8,128)(2,1)S(1)} %copy-done.79, bf16[2304,2304]{1,0:T(8,128)(2,1)} %bitcast.526), kind=kOutput, calls=%fused_computation.44 | convolution fusion | flops 6797721600 | bytes 22413312 | tf_op jit(solution)/shard_map/dot_general | solution.py:34
  795.3 15.5 %add_convert_fusion.1 = bf16[640,2304]{1,0:T(8,128)(2,1)} fusion(f32[640,2304]{1,0:T(8,128)} %fusion.134, bf16[640,2304]{1,0:T(8,128)(2,1)S(1)} %get-tuple-element.368.refs_6_, bf16[2304,2304]{1,0:T(8,128)(2,1)} %bitcast.527), kind=kOutput, calls=%fused_computation.42 | convolution fusion | flops 6797721600 | bytes 22413312 | tf_op jit(solution)/shard_map/dot_general | solution.py:34
  816.8 20.0 %convolution_convert_fusion = bf16[2304,2304]{1,0:T(8,128)(2,1)} fusion(bf16[640,2304]{1,0:T(8,128)(2,1)S(1)} %copy-done.77, bf16[640,2304]{1,0:T(8,128)(2,1)} %get-tuple-element.255, bf16[640,2304]{1,0:T(8,128)(2,1)} %get-tuple-element.258, bf16[640,2304]{1,0:T(8,128)(2,1)} %get-tuple-element.257), kind=kOutput, calls=%fused_computation | convolution fusion | flops 13618446336 | bytes 22413312 | tf_op jit(solution)/shard_map/dot_general | solution.py:38
  840.6 19.3 %convolution_convert_fusion.1 = bf16[2304,2304]{1,0:T(8,128)(2,1)} fusion(bf16[1280,2304]{1,0:T(8,128)(2,1)} %constant_dynamic-update-slice_fusion, bf16[640,2304]{1,0:T(8,128)(2,1)S(1)} %copy-done.80, bf16[640,2304]{1,0:T(8,128)(2,1)S(1)} %copy-done.83), kind=kOutput, calls=%fused_computation.1 | convolution fusion | flops 13606649856 | bytes 22413312 | tf_op jit(solution)/shard_map/dot_general | solution.py:38
  859.9 19.3 %convolution_convert_fusion.2 = bf16[2304,2304]{1,0:T(8,128)(2,1)} fusion(bf16[1280,2304]{1,0:T(8,128)(2,1)} %constant_dynamic-update-slice_fusion, bf16[640,2304]{1,0:T(8,128)(2,1)S(1)} %copy-done.81, bf16[640,2304]{1,0:T(8,128)(2,1)S(1)} %copy-done.85), kind=kOutput, calls=%fused_computation.2 | convolution fusion | flops 13606649856 | bytes 22413312 | tf_op jit(solution)/shard_map/dot_general | solution.py:38
  881.5 44.8 %reduce-scatter.13.cloned.1.call-done = bf16[1,160,2304]{2,1,0:T(8,128)(2,1)} async-done(((bf16[4,160,2304]{2,1,0:T(8,128)(2,1)}), bf16[1,160,2304]{2,1,0:T(8,128)(2,1)}) %reduce-scatter.13.cloned.1.call-update) | async-done | bytes 737296 | tf_op jit(solution)/shard_map/reduce_scatter | solution.py:71
  978.8 14.3 collective-permute-done.41.refs_7_
  996.2 13.5 collective-permute-done.37.refs_3_
  1070.8 18.2 %shard_map.274 = (bf16[2,320,512]{2,1,0:T(8,128)(2,1)}, bf16[4,2,320,512]{3,2,1,0:T(8,128)(2,1)}, bf16[4,2,320,512]{3,2,1,0:T(8,128)(2,1)}) custom-call(s32[3]{0:T(128)} %get-tuple-element.204.place, bf16[2,320,512]{2,1,0:T(8,128)(2,1)} %get-tuple-element.205.query_ref, bf16[2,320,512]{2,1,0:T(8,128)(2,1)} %get-tuple-element.278.grad_ref, ...), custom_call_target="tpu_custom_call" | custom-call | flops 8388608000 | bytes 20971520 | tf_op jit(solution)/shard_map/pallas_call | solution.py:381
  1124.6 18.3 %shard_map.277 = (bf16[2,320,512]{2,1,0:T(8,128)(2,1)}, bf16[4,2,320,512]{3,2,1,0:T(8,128)(2,1)}, bf16[4,2,320,512]{3,2,1,0:T(8,128)(2,1)}) custom-call(s32[3]{0:T(128)} %get-tuple-element.204.place, bf16[2,320,512]{2,1,0:T(8,128)(2,1)} %get-tuple-element.221.query_ref, bf16[2,320,512]{2,1,0:T(8,128)(2,1)} %get-tuple-element.290.grad_ref, ...), custom_call_target="tpu_custom_call" | custom-call | flops 8388608000 | bytes 20971520 | tf_op jit(solution)/shard_map/pallas_call | solution.py:381
  1157.2 29.7 %collective-permute-done.59.refs_2_ = bf16[2,288,2304]{2,1,0:T(8,128)(2,1)S(1)} collective-permute-done((bf16[2,288,2304]{2,1,0:T(8,128)(2,1)}, bf16[2,288,2304]{2,1,0:T(8,128)(2,1)S(1)}, u32[]{:S(2)}, u32[]{:S(2)}) %collective-permute-start.59) | collective-permute-done | bytes 2654240 | tf_op jit(solution)/shard_map/ppermute | solution.py:42
  1253.7 18.2 %reduce-scatter.19.cloned.1.call-done = bf16[1,2,320,512]{3,2,1,0:T(8,128)(2,1)} async-done(((bf16[4,2,320,512]{3,2,1,0:T(8,128)(2,1)}), bf16[1,2,320,512]{3,2,1,0:T(8,128)(2,1)}) %reduce-scatter.19.cloned.1.call-update) | async-done | bytes 655376 | tf_op jit(solution)/shard_map/reduce_scatter | solution.py:71
  1334.9 24.5 %collective-permute-done.72 = bf16[2,72,2304]{2,1,0:T(8,128)(2,1)} collective-permute-done((bf16[2,72,2304]{2,1,0:T(8,128)(2,1)}, bf16[2,72,2304]{2,1,0:T(8,128)(2,1)}, u32[]{:S(2)}, u32[]{:S(2)}) %collective-permute-start.72) | collective-permute-done | bytes 663584 | tf_op jit(solution)/shard_map/ppermute | solution.py:65
  1377.6 15.2 %collective-permute-start.78 = (f32[72]{0:T(128)}, f32[72]{0:T(128)}, u32[]{:S(2)}, u32[]{:S(2)}) collective-permute-start(f32[72]{0:T(128)} %get-tuple-element.494), channel_id=1, source_target_pairs={{0,2},{1,3},{2,4},{3,5},{4,6},{5,7},{6,0},{7,1},{8,10},{9,11},{10,... | collective-permute-start | bytes 872 | tf_op jit(solution)/shard_map/ppermute | solution.py:65
  1392.8 62.4 %all-reduce.5.cloned.1.call-done = bf16[8,4,72,1024]{3,2,0,1:T(8,128)(2,1)} async-done(((bf16[8,4,72,1024]{3,2,0,1:T(8,128)(2,1)}), bf16[8,4,72,1024]{3,2,0,1:T(8,128)(2,1)}) %all-reduce.5.cloned.1.call-update) | async-done | bytes 4718608
  (834 shorter events, 659.8 us)
Async XLA Ops:
  7.2 106.1 %all-gather.18.cloned.1.call-start = ((), (), s32[]{:S(2)}) async-start(), calls=%async_computation.15 | async-start | bytes 5308416 | tf_op jit(solution)/shard_map/all_gather | solution.py:469
  28.7 158.5 %all-gather.20.cloned.1.call-start = ((), (), s32[]{:S(2)}) async-start(), calls=%async_computation.16 | async-start | bytes 3276800 | tf_op jit(solution)/shard_map/all_gather | solution.py:55
  72.7 52.6 %collective-permute-start.10 = (bf16[144,2304]{1,0:T(8,128)(2,1)}, bf16[144,2304]{1,0:T(8,128)(2,1)}, u32[]{:S(2)}, u32[]{:S(2)}) collective-permute-start(bf16[144,2304]{1,0:T(8,128)(2,1)} %get-tuple-element.421), channel_id=1, source_target_pairs={{0,4},{1,5},{2,6},{3,7},{4,0},{5,1},{6,2},{7,3},{8,12},{9,13},{10,... | collective-permute-start | bytes 1990664 | tf_op jit(solution)/shard_map/ppermute | solution.py:65
  120.9 131.9 %all-gather.22.cloned.1.call-start = ((), (), s32[]{:S(2)}) async-start(), calls=%async_computation.17 | async-start | bytes 3276800 | tf_op jit(solution)/shard_map/all_gather | solution.py:55
  176.6 125.2 %all-gather.16.cloned.1.call-start = ((), (), s32[]{:S(2)}) async-start(), calls=%async_computation.7 | async-start | bytes 2654208 | tf_op jit(solution)/shard_map/all_gather | solution.py:534
  192.6 248.4 %all-gather.26.cloned.1.call-start = ((), (), s32[]{:S(2)}) async-start(), calls=%async_computation.19 | async-start | bytes 3686400 | tf_op jit(solution)/shard_map/all_gather | solution.py:55
  192.7 59.8 %collective-permute-start.19 = (bf16[576,2304]{1,0:T(8,128)(2,1)S(1)}, bf16[576,2304]{1,0:T(8,128)(2,1)}, u32[]{:S(2)}, u32[]{:S(2)}) collective-permute-start(bf16[576,2304]{1,0:T(8,128)(2,1)S(1)} %copy-done.10), channel_id=1, source_target_pairs={{0,8},{8,0},{16,24},{24,16},{1,9},{9,1},{17,25},{25,17},{2,10},{10... | collective-permute-start | bytes 7962632 | tf_op jit(solution)/shard_map/ppermute | solution.py:42
  193.4 59.5 %collective-permute-start.20 = (bf16[576,2304]{1,0:T(8,128)(2,1)S(1)}, bf16[576,2304]{1,0:T(8,128)(2,1)}, u32[]{:S(2)}, u32[]{:S(2)}) collective-permute-start(bf16[576,2304]{1,0:T(8,128)(2,1)S(1)} %copy-done.10), channel_id=1, source_target_pairs={{0,16},{8,24},{16,0},{24,8},{1,17},{9,25},{17,1},{25,9},{2,18},{10... | collective-permute-start | bytes 7962632 | tf_op jit(solution)/shard_map/ppermute | solution.py:42
  252.8 49.0 %collective-permute-start.23 = (bf16[576,2304]{1,0:T(8,128)(2,1)}, bf16[576,2304]{1,0:T(8,128)(2,1)S(1)}, u32[]{:S(2)}, u32[]{:S(2)}) collective-permute-start(bf16[576,2304]{1,0:T(8,128)(2,1)} %get-tuple-element.226), channel_id=1, source_target_pairs={{0,1},{1,0},{2,3},{3,2},{4,5},{5,4},{6,7},{7,6},{8,9},{9,8},{10,11... | collective-permute-start | bytes 7962632 | tf_op jit(solution)/shard_map/ppermute | solution.py:46
  253.4 48.5 %collective-permute-start.24 = (bf16[576,2304]{1,0:T(8,128)(2,1)}, bf16[576,2304]{1,0:T(8,128)(2,1)}, u32[]{:S(2)}, u32[]{:S(2)}) collective-permute-start(bf16[576,2304]{1,0:T(8,128)(2,1)} %get-tuple-element.227), channel_id=1, source_target_pairs={{0,1},{1,0},{2,3},{3,2},{4,5},{5,4},{6,7},{7,6},{8,9},{9,8},{10,11... | collective-permute-start | bytes 7962632 | tf_op jit(solution)/shard_map/ppermute | solution.py:46
  381.6 119.8 %all-gather.24.cloned.1.call-start = ((), (), s32[]{:S(2)}) async-start(), calls=%async_computation.18 | async-start | bytes 3686400 | tf_op jit(solution)/shard_map/all_gather | solution.py:55
  396.2 163.4 %reduce-scatter.11.cloned.1.call-start = ((), (), s32[]{:S(2)}) async-start(), calls=%async_computation.9 | async-start | bytes 3686400 | tf_op jit(solution)/shard_map/reduce_scatter | solution.py:71
  475.8 143.4 %reduce-scatter.9.cloned.1.call-start = ((), (), s32[]{:S(2)}) async-start(), calls=%async_computation.8 | async-start | bytes 3686400 | tf_op jit(solution)/shard_map/reduce_scatter | solution.py:71
  536.1 151.0 %all-gather.28.cloned.1.call-start = ((), (), s32[]{:S(2)}) async-start(), calls=%async_computation.20 | async-start | bytes 3686400 | tf_op jit(solution)/shard_map/all_gather | solution.py:55
  626.7 121.3 %all-gather.30.cloned.1.call-start = ((), (), s32[]{:S(2)}) async-start(), calls=%async_computation.21 | async-start | bytes 3686400 | tf_op jit(solution)/shard_map/all_gather | solution.py:55
  627.3 251.9 %reduce-scatter.15.cloned.1.call-start = ((), (), s32[]{:S(2)}) async-start(), calls=%async_computation.11 | async-start | bytes 3686400 | tf_op jit(solution)/shard_map/reduce_scatter | solution.py:71
  810.9 115.4 %reduce-scatter.13.cloned.1.call-start = ((), (), s32[]{:S(2)}) async-start(), calls=%async_computation.10 | async-start | bytes 3686400 | tf_op jit(solution)/shard_map/reduce_scatter | solution.py:71
  814.5 340.9 %reduce-scatter.21.cloned.1.call-start = ((), (), s32[]{:S(2)}) async-start(), calls=%async_computation.14 | async-start | bytes 2654208 | tf_op jit(solution)/shard_map/reduce_scatter | solution.py:705
  942.9 92.7 %collective-permute-start.44 = (bf16[4,4,72,2304]{3,2,1,0:T(8,128)(2,1)}, bf16[4,4,72,2304]{3,2,1,0:T(8,128)(2,1)}, u32[]{:S(2)}, u32[]{:S(2)}) collective-permute-start(bf16[4,4,72,2304]{3,2,1,0:T(8,128)(2,1)} %dynamic-slice_bitcast_fusion.2), channel_id=1, source_target_pairs={{0,1},{1,0},{2,3},{3,2},{4,5},{5,4},{6,7},{7,6},{8,9},{9,8},{10,11... | collective-permute-start | bytes 15925256 | tf_op jit(solution)/shard_map/ppermute | solution.py:46
  945.6 90.0 %collective-permute-start.45 = (bf16[4,4,72,2304]{3,2,1,0:T(8,128)(2,1)}, bf16[4,4,72,2304]{3,2,1,0:T(8,128)(2,1)}, u32[]{:S(2)}, u32[]{:S(2)}) collective-permute-start(bf16[4,4,72,2304]{3,2,1,0:T(8,128)(2,1)} %dynamic-slice_bitcast_fusion.1), channel_id=1, source_target_pairs={{0,1},{1,0},{2,3},{3,2},{4,5},{5,4},{6,7},{7,6},{8,9},{9,8},{10,11... | collective-permute-start | bytes 15925256 | tf_op jit(solution)/shard_map/ppermute | solution.py:46
  949.3 86.3 %collective-permute-start.46 = (bf16[4,288,2304]{2,1,0:T(8,128)(2,1)}, bf16[4,288,2304]{2,1,0:T(8,128)(2,1)}, u32[]{:S(2)}, u32[]{:S(2)}) collective-permute-start(bf16[4,288,2304]{2,1,0:T(8,128)(2,1)} %dynamic-slice_bitcast_fusion), channel_id=1, source_target_pairs={{0,1},{1,0},{2,3},{3,2},{4,5},{5,4},{6,7},{7,6},{8,9},{9,8},{10,11... | collective-permute-start | bytes 15925256 | tf_op jit(solution)/shard_map/ppermute | solution.py:46
  1070.5 148.8 %reduce-scatter.17.cloned.1.call-start = ((), (), s32[]{:S(2)}) async-start(), calls=%async_computation.12 | async-start | bytes 3276800 | tf_op jit(solution)/shard_map/reduce_scatter | solution.py:71
  1097.8 45.1 %collective-permute-start.56 = (bf16[2,144,2304]{2,1,0:T(8,128)(2,1)}, bf16[2,144,2304]{2,1,0:T(8,128)(2,1)}, u32[]{:S(2)}, u32[]{:S(2)}) collective-permute-start(bf16[2,144,2304]{2,1,0:T(8,128)(2,1)} %pad_maximum_fusion.15), channel_id=1, source_target_pairs={{0,16},{8,24},{16,0},{24,8},{1,17},{9,25},{17,1},{25,9},{2,18},{10... | collective-permute-start | bytes 3981320 | tf_op jit(solution)/shard_map/ppermute | solution.py:42
  1117.7 154.3 %reduce-scatter.19.cloned.1.call-start = ((), (), s32[]{:S(2)}) async-start(), calls=%async_computation.13 | async-start | bytes 3276800 | tf_op jit(solution)/shard_map/reduce_scatter | solution.py:71
  1121.6 65.2 %collective-permute-start.59 = (bf16[2,288,2304]{2,1,0:T(8,128)(2,1)}, bf16[2,288,2304]{2,1,0:T(8,128)(2,1)S(1)}, u32[]{:S(2)}, u32[]{:S(2)}) collective-permute-start(bf16[2,288,2304]{2,1,0:T(8,128)(2,1)} %pad_maximum_fusion.5), channel_id=1, source_target_pairs={{0,16},{8,24},{16,0},{24,8},{1,17},{9,25},{17,1},{25,9},{2,18},{10... | collective-permute-start | bytes 7962632 | tf_op jit(solution)/shard_map/ppermute | solution.py:42
  1124.5 64.8 %collective-permute-start.58 = (bf16[2,288,2304]{2,1,0:T(8,128)(2,1)}, bf16[2,288,2304]{2,1,0:T(8,128)(2,1)}, u32[]{:S(2)}, u32[]{:S(2)}) collective-permute-start(bf16[2,288,2304]{2,1,0:T(8,128)(2,1)} %pad_maximum_fusion.4), channel_id=1, source_target_pairs={{0,8},{8,0},{16,24},{24,16},{1,9},{9,1},{17,25},{25,17},{2,10},{10... | collective-permute-start | bytes 7962632 | tf_op jit(solution)/shard_map/ppermute | solution.py:42
  1147.9 52.6 %collective-permute-start.60 = (bf16[144,2304]{1,0:T(8,128)(2,1)}, bf16[144,2304]{1,0:T(8,128)(2,1)S(1)}, u32[]{:S(2)}, u32[]{:S(2)}) collective-permute-start(bf16[144,2304]{1,0:T(8,128)(2,1)} %get-tuple-element.379), channel_id=1, source_target_pairs={{0,16},{8,24},{16,0},{24,8},{1,17},{9,25},{17,1},{25,9},{2,18},{10... | collective-permute-start | bytes 1990664 | tf_op jit(solution)/shard_map/ppermute | solution.py:42
  1148.7 54.1 %collective-permute-start.61 = (bf16[144,2304]{1,0:T(8,128)(2,1)}, bf16[144,2304]{1,0:T(8,128)(2,1)}, u32[]{:S(2)}, u32[]{:S(2)}) collective-permute-start(bf16[144,2304]{1,0:T(8,128)(2,1)} %get-tuple-element.378), channel_id=1, source_target_pairs={{0,8},{8,0},{16,24},{24,16},{1,9},{9,1},{17,25},{25,17},{2,10},{10... | collective-permute-start | bytes 1990664 | tf_op jit(solution)/shard_map/ppermute | solution.py:42
  1212.0 243.2 %all-reduce.5.cloned.1.call-start = ((), (), s32[]{:S(2)}) async-start(), calls=%async_computation.22 | async-start | bytes 9437184
  1299.5 59.8 %collective-permute-start.72 = (bf16[2,72,2304]{2,1,0:T(8,128)(2,1)}, bf16[2,72,2304]{2,1,0:T(8,128)(2,1)}, u32[]{:S(2)}, u32[]{:S(2)}) collective-permute-start(bf16[2,72,2304]{2,1,0:T(8,128)(2,1)} %get-tuple-element.398), channel_id=1, source_target_pairs={{0,4},{1,5},{2,6},{3,7},{4,0},{5,1},{6,2},{7,3},{8,12},{9,13},{10,... | collective-permute-start | bytes 1990664 | tf_op jit(solution)/shard_map/ppermute | solution.py:65
  1301.5 67.7 %collective-permute-start.73 = (bf16[2,72,2304]{2,1,0:T(8,128)(2,1)}, bf16[2,72,2304]{2,1,0:T(8,128)(2,1)}, u32[]{:S(2)}, u32[]{:S(2)}) collective-permute-start(bf16[2,72,2304]{2,1,0:T(8,128)(2,1)} %get-tuple-element.397), channel_id=1, source_target_pairs={{0,6},{1,7},{2,0},{3,1},{4,2},{5,3},{6,4},{7,5},{8,14},{9,15},{10,... | collective-permute-start | bytes 1990664 | tf_op jit(solution)/shard_map/ppermute | solution.py:65
  1377.6 89.3 %collective-permute-start.78 = (f32[72]{0:T(128)}, f32[72]{0:T(128)}, u32[]{:S(2)}, u32[]{:S(2)}) collective-permute-start(f32[72]{0:T(128)} %get-tuple-element.494), channel_id=1, source_target_pairs={{0,2},{1,3},{2,4},{3,5},{4,6},{5,7},{6,0},{7,1},{8,10},{9,11},{10,... | collective-permute-start | bytes 872 | tf_op jit(solution)/shard_map/ppermute | solution.py:65
  (234 other events, 2956.5 us)
Sparse Core Ops, SparseCore 0:
  28.8 84.4 all-gather.17
  121.1 59.5 all-gather.19
  182.8 53.6 all-gather.21
  238.5 30.3 all-gather.15
  381.7 59.2 all-gather.25
  442.4 58.9 all-gather.23
  503.7 55.8 reduce-scatter.10
  562.0 57.0 reduce-scatter.8
  626.9 60.1 all-gather.27
  689.1 58.9 all-gather.29
  811.0 55.8 reduce-scatter.14
  869.2 57.0 reduce-scatter.12
  1070.7 35.2 reduce-scatter.20
  1117.8 59.5 reduce-scatter.16
  1212.1 59.7 reduce-scatter.18
  1314.5 140.6 all-reduce.4

commit v2 on v1

v2 whole, which is shorter than its diff:
```python
import functools
import math

import jax
import jax.numpy as jnp
from jax import lax
from jax.experimental import pallas as pl
from jax.experimental.pallas import tpu as pltpu
from jax.sharding import PartitionSpec as P

KEY_VALUE_HEADS = 4
HEAD_DIM = 256
GROUP = 2
WINDOW = 4096

epsilon = 1e-06
softcap = 50.0
score_scale = HEAD_DIM ** (-0.5) / softcap
log2_scale = softcap * 1.4426950408889634
VMEM_LIMIT = 56 * 1024 * 1024
ANYWHERE = pl.BlockSpec(memory_space=pl.ANY)


def normed(values, gain_vec):
    inv_rms = lax.rsqrt(jnp.mean(values * values, axis=-1, keepdims=True) + epsilon)
    return values * inv_rms * gain_vec


def matmul(a, b):
    return jnp.dot(a, b, preferred_element_type=jnp.float32)


def matmul_t(a, b):
    return lax.dot_general(a, b, (((1,), (1,)), ((), ())), preferred_element_type=jnp.float32)


def inner_t(a, b):
    return lax.dot_general(a, b, (((0,), (0,)), ((), ())), preferred_element_type=jnp.float32)


def across(x, bits):
    return lax.ppermute(x, "dp", [(i, i ^ bits) for i in range(lax.axis_size("dp"))])


def swap_core(x):
    return lax.ppermute(x, "seq", [(i, i ^ 1) for i in range(lax.axis_size("seq"))])


def line_groups():
    count = lax.axis_size("seq")
    return [list(range(core, count, 2)) for core in (0, 1)]


def gather_line(x):
    return lax.all_gather(x, "seq", axis=0, axis_index_groups=line_groups())


def line_route(line, distance):
    return [
        (2 * i + core, 2 * ((i + distance) % line) + core) for i in range(line) for core in (0, 1)
    ]


def exchange_line_parts(parts):
    line = len(parts)
    return [parts[0]] + [lax.ppermute(parts[k], "seq", line_route(line, k)) for k in range(1, line)]


def exchange_line(x, place):
    line = x.shape[0]
    parts = exchange_line_parts([pick(x, 0, (place + k) % line) for k in range(line)])
    for k in range(1, line):
        x = put(x, parts[k], (place + line - k) % line)
    return x


def scatter_line(x):
    return lax.psum_scatter(x, "seq", scatter_dimension=0, axis_index_groups=line_groups())


def scatter_line_steps(x, place):
    line = x.shape[0]
    right = left = None
    for step in range(1, line):
        going = pick(x, 0, jnp.clip(line - step + place, 0, line - 1))
        coming = pick(x, 0, jnp.clip(step - line + place, 0, line - 1))
        right = going if right is None else going + right
        left = coming if left is None else coming + left
        right_route = [(2 * i + c, 2 * i + 2 + c) for i in range(step) for c in (0, 1)]
        left_route = [
            (2 * (line - 1 - i) + c, 2 * (line - 2 - i) + c) for i in range(step) for c in (0, 1)
        ]
        right = lax.ppermute(right, "seq", right_route)
        left = lax.ppermute(left, "seq", left_route)
    f32 = jnp.float32
    return pick(x, 0, place).astype(f32) + right.astype(f32) + left.astype(f32)


def gather_quad_near(x):
    return across(x, 1), across(x, 2)


def gather_quad_far_parts(one, two):
    half = one.shape[0] // 2
    return across(two[:half], 1), across(one[half:], 2)


def gather_quad_far(one, two):
    return jnp.concatenate(gather_quad_far_parts(one, two), axis=0)


def gather_quad(x):
    one, two = gather_quad_near(x)
    return [x, one, two, gather_quad_far(one, two)]


def scatter_quad_near(sent):
    return across(sent[0], 1), across(sent[1], 2)


def scatter_quad_far(kept, near):
    return across(kept[1] + near[0][1], 2), across(kept[2] + near[1][1], 1)


def scatter_quad_end(kept, near, far):
    half = kept[0].shape[0] // 2
    f32 = jnp.float32
    low = kept[0][:half].astype(f32) + near[0][0].astype(f32) + far[0].astype(f32)
    high = kept[0][half:].astype(f32) + near[1][0].astype(f32) + far[1].astype(f32)
    return jnp.concatenate([low, high], axis=0)


def flip_order(x, bits):
    pairs = x.reshape((2, 2) + x.shape[1:])
    pairs = jnp.where(bits % 2 == 1, pairs[:, ::-1], pairs)
    pairs = jnp.where(bits // 2 == 1, pairs[::-1], pairs)
    return pairs.reshape(x.shape)


def exchange_quad(x, place):
    parts = flip_order(x, place)
    return exchange_quad_end([parts[0]] + [across(parts[k], k) for k in (1, 2, 3)], place)


def exchange_quad_end(parts, place):
    return flip_order(jnp.stack(parts), place)


def pick(x, axis, index):
    return lax.dynamic_index_in_dim(x, index, axis, keepdims=False)


def put(x, part, *index):
    for _ in index:
        part = part[None]
    return lax.dynamic_update_slice(x, part, index + (0,) * (x.ndim - len(index)))


def after(x, *others):
    def kernel(x_ref, *rest):
        rest[-1][...] = x_ref[...]

    return pl.pallas_call(
        kernel,
        in_specs=[pl.BlockSpec(memory_space=pltpu.VMEM)] + [ANYWHERE] * len(others),
        out_specs=pl.BlockSpec(memory_space=pltpu.VMEM),
        out_shape=jax.ShapeDtypeStruct(x.shape, x.dtype),
    )(x, *others)


def empty(shape, dtype):
    return pl.pallas_call(
        lambda out_ref: None, out_specs=ANYWHERE, out_shape=jax.ShapeDtypeStruct(shape, dtype)
    )()


class Order:
    def __init__(self):
        self.token = jnp.zeros((8, 128), jnp.float32)

    def __call__(self, *trees):
        leaves, tree = jax.tree.flatten(trees)
        held = pl.pallas_call(
            lambda *refs: None,
            in_specs=[ANYWHERE] * (1 + len(leaves)),
            out_specs=[ANYWHERE] * (1 + len(leaves)),
            out_shape=[jax.ShapeDtypeStruct(x.shape, x.dtype) for x in [self.token, *leaves]],
            input_output_aliases={i: i for i in range(1 + len(leaves))},
        )(self.token, *leaves)
        self.token = held[0]
        out = jax.tree.unflatten(tree, held[1:])
        return out[0] if len(trees) == 1 else out


FREE = pl.CostEstimate(flops=0, bytes_accessed=0, transcendentals=0)


def cost(us):
    return pl.CostEstimate(flops=0, bytes_accessed=int(us * 3.5e6), transcendentals=0)


def deposit(place, targets, sources, moves):
    count = len(targets)

    def kernel(place_ref, *refs):
        source_refs = refs[count : count + len(sources)]
        target_refs, sems = refs[count + len(sources) : -1], refs[-1]
        copies = []
        for n, (source, source_at, target, target_at) in enumerate(moves):
            source_ref, target_ref = source_refs[source], target_refs[target]
            if source_at is not None:
                source_ref = source_ref.at[source_at(place_ref)]
            copies.append(
                pltpu.make_async_copy(source_ref, target_ref.at[target_at(place_ref)], sems.at[n])
            )
            copies[-1].start()
        for copy in copies:
            copy.wait()

    return pl.pallas_call(
        kernel,
        in_specs=[pl.BlockSpec(memory_space=pltpu.SMEM)]
        + [ANYWHERE] * count
        + [pl.BlockSpec(memory_space=pltpu.VMEM)] * len(sources),
        out_specs=[ANYWHERE] * count,
        out_shape=[jax.ShapeDtypeStruct(x.shape, x.dtype) for x in targets],
        scratch_shapes=[pltpu.SemaphoreType.DMA((len(moves),))],
        input_output_aliases={1 + i: i for i in range(count)},
        compiler_params=pltpu.CompilerParams(vmem_limit_bytes=VMEM_LIMIT),
        cost_estimate=FREE,
    )(place, *targets, *sources)


LINE_AT, CORE_AT, HALF_AT, HEAD_AT = range(4)


def pack_heads(place, query, key, value):
    rows, width = query.shape[0], GROUP * HEAD_DIM

    def kernel(place_ref, query_ref, key_ref, value_ref, *out_refs):
        for k, out_ref in enumerate(out_refs):
            head = place_ref[HEAD_AT] ^ k
            first = pl.multiple_of(head * width, width)
            out_ref[:, :width] = query_ref[:, pl.ds(first, width)]
            first = pl.multiple_of(head * HEAD_DIM, HEAD_DIM)
            out_ref[:, width : width + HEAD_DIM] = key_ref[:, pl.ds(first, HEAD_DIM)]
            out_ref[:, width + HEAD_DIM :] = value_ref[:, pl.ds(first, HEAD_DIM)]

    return pl.pallas_call(
        kernel,
        in_specs=[pl.BlockSpec(memory_space=pltpu.SMEM)]
        + [pl.BlockSpec(memory_space=pltpu.VMEM)] * 3,
        out_shape=[jax.ShapeDtypeStruct((rows, 2 * width), query.dtype)] * KEY_VALUE_HEADS,
        compiler_params=pltpu.CompilerParams(vmem_limit_bytes=VMEM_LIMIT),
        cost_estimate=FREE,
    )(place, query, key, value)


def order_heads(place, parts):
    def kernel(place_ref, *refs):
        for k in range(KEY_VALUE_HEADS):
            refs[-1][place_ref[HEAD_AT] ^ k] = refs[k][...]

    return pl.pallas_call(
        kernel,
        in_specs=[pl.BlockSpec(memory_space=pltpu.SMEM)]
        + [pl.BlockSpec(memory_space=pltpu.VMEM)] * KEY_VALUE_HEADS,
        out_shape=jax.ShapeDtypeStruct((KEY_VALUE_HEADS,) + parts[0].shape, parts[0].dtype),
        compiler_params=pltpu.CompilerParams(vmem_limit_bytes=VMEM_LIMIT),
        cost_estimate=FREE,
    )(place, *parts)


def weight_halves(place, lefts, rights, inner):
    rows, model = lefts[0].shape
    columns = rights[0].shape[1]
    block, strip = math.gcd(model, 1152), math.gcd(columns, 256)
    groups = block // (2 * inner)

    def kernel(place_ref, left_a, left_b, right_a, right_b, own_ref, other_ref, turned):
        turned[:, :rows] = left_a[...].T
        turned[:, rows:] = left_b[...].T
        core_here = place_ref[CORE_AT]

        def body(n, carry):
            at = pl.ds(pl.multiple_of(n * strip, strip), strip)
            term = matmul(turned[:, :rows], right_a[:, at])
            term = (term + matmul(turned[:, rows:], right_b[:, at])).astype(jnp.bfloat16)
            term = term.reshape(groups, 2, inner, strip)
            own_ref[:, :, at] = jnp.where(core_here == 0, term[:, 0], term[:, 1])
            other_ref[:, :, at] = jnp.where(core_here == 0, term[:, 1], term[:, 0])
            return carry

        lax.fori_loop(0, columns // strip, body, 0)

    half = pl.BlockSpec((groups, inner, columns), lambda i: (i, 0, 0))
    shape = jax.ShapeDtypeStruct((model // (2 * inner), inner, columns), jnp.bfloat16)
    left_spec = pl.BlockSpec((rows, block), lambda i: (0, i))
    right_spec = pl.BlockSpec((rows, columns), lambda i: (0, 0))
    return pl.pallas_call(
        kernel,
        grid=(model // block,),
        in_specs=[pl.BlockSpec(memory_space=pltpu.SMEM)] + [left_spec] * 2 + [right_spec] * 2,
        out_specs=[half, half],
        out_shape=[shape, shape],
        scratch_shapes=[pltpu.VMEM((block, 2 * rows), jnp.bfloat16)],
        compiler_params=pltpu.CompilerParams(vmem_limit_bytes=VMEM_LIMIT),
        cost_estimate=FREE,
    )(place, *lefts, *rights)


def quad_terms(lefts, weight, part, turned):
    first, count = part.start, part.stop - part.start
    half = count // 2
    model = weight.shape[0] if turned else weight.shape[1]

    def kernel(a_ref, b_ref, weight_ref, one_ref, two_ref, own_ref, low_ref, high_ref):
        for k in range(4):
            ref = (a_ref, b_ref)[k // 2]
            rows = ref[k % 2, first : first + count, :]
            product = matmul_t if turned else matmul
            term = product(rows, weight_ref[...]).astype(jnp.bfloat16)
            if k == 0:
                own_ref[...] = term
            if k % 2 == 1:
                one_ref[k // 2] = term[:half]
            if k == 2:
                low_ref[...] = term[:half]
            if k >= 2:
                two_ref[k - 2] = term[half:]
            if k == 1:
                high_ref[...] = term[half:]

    def shape(*lead):
        return jax.ShapeDtypeStruct(lead + (model,), jnp.bfloat16)

    one, two, own, low, high = pl.pallas_call(
        kernel,
        out_shape=[shape(2, half), shape(2, half), shape(count), shape(half), shape(half)],
        compiler_params=pltpu.CompilerParams(vmem_limit_bytes=VMEM_LIMIT),
        cost_estimate=FREE,
    )(*lefts, weight)
    return (one, two), (own, low, high)


def split_columns(place, gate, up, dp, line):
    rows, ff = gate.shape
    rest = ff // (dp * line)

    def kernel(place_ref, gate_ref, up_ref, *out_refs):
        def fill(j, k):
            for which, ref in enumerate((gate_ref, up_ref)):
                for i in range(dp):
                    first = (i * line + j) * rest
                    out_refs[k][which, :, i * rest : (i + 1) * rest] = ref[:, first : first + rest]

        for j in range(line):
            for k in range(line):
                there = lax.rem(place_ref[LINE_AT] + k, line) == j
                pl.when(there)(functools.partial(fill, j, k))

    return pl.pallas_call(
        kernel,
        in_specs=[pl.BlockSpec(memory_space=pltpu.SMEM)]
        + [pl.BlockSpec(memory_space=pltpu.VMEM)] * 2,
        out_shape=[jax.ShapeDtypeStruct((2, rows, dp * rest), gate.dtype)] * line,
        compiler_params=pltpu.CompilerParams(vmem_limit_bytes=VMEM_LIMIT),
        cost_estimate=FREE,
    )(place, gate, up)


def join_columns(place, parts, dp):
    line = len(parts)
    rows, part = parts[0].shape
    rest = part // dp

    def kernel(place_ref, *refs):
        def fill(j, k):
            for i in range(dp):
                first = (i * line + j) * rest
                refs[line][:, first : first + rest] = refs[k][
                    :, i * rest : (i + 1) * rest
                ].astype(jnp.float32)

        for j in range(line):
            for k in range(line):
                there = lax.rem(place_ref[LINE_AT] + line - k, line) == j
                pl.when(there)(functools.partial(fill, j, k))

    return pl.pallas_call(
        kernel,
        in_specs=[pl.BlockSpec(memory_space=pltpu.SMEM)]
        + [pl.BlockSpec(memory_space=pltpu.VMEM)] * line,
        out_shape=jax.ShapeDtypeStruct((rows, line * part), jnp.float32),
        compiler_params=pltpu.CompilerParams(vmem_limit_bytes=VMEM_LIMIT),
        cost_estimate=FREE,
    )(place, *parts)


def add_second(term, pair):
    rows, columns = term.shape

    def kernel(term_ref, pair_ref, out_ref):
        total = term_ref[...].astype(jnp.float32) + pair_ref[0].astype(jnp.float32)
        out_ref[...] = total.astype(jnp.bfloat16)

    return pl.pallas_call(
        kernel,
        grid=(1,),
        in_specs=[
            pl.BlockSpec((rows, columns), lambda i: (0, 0)),
            pl.BlockSpec((1, rows, columns), lambda i: (1, 0, 0)),
        ],
        out_specs=pl.BlockSpec((rows, columns), lambda i: (0, 0)),
        out_shape=jax.ShapeDtypeStruct((rows, columns), jnp.bfloat16),
        compiler_params=pltpu.CompilerParams(vmem_limit_bytes=VMEM_LIMIT),
        cost_estimate=FREE,
    )(term, pair)


def combine_quad(place, own, other, shapes, plan):
    _, inner, columns = own.shape
    spec = pl.BlockSpec((1, inner, columns), lambda k, place: (place[HEAD_AT] ^ k, 0, 0))

    def kernel(place_ref, own_ref, other_ref, *out_refs):
        total = own_ref[0].astype(jnp.float32) + other_ref[0].astype(jnp.float32)
        total = total.astype(jnp.bfloat16)

        def write(k):
            for out, at, taken in plan[k]:
                if at is None:
                    out_refs[out][...] = total[taken]
                else:
                    out_refs[out][at] = total[taken]

        for k in range(4):
            pl.when(pl.program_id(0) == k)(functools.partial(write, k))

    return pl.pallas_call(
        kernel,
        grid_spec=pltpu.PrefetchScalarGridSpec(
            num_scalar_prefetch=1,
            grid=(4,),
            in_specs=[spec, spec],
            out_specs=[
                pl.BlockSpec(shape, lambda k, place, rank=len(shape): (0,) * rank)
                for shape in shapes
            ],
        ),
        out_shape=[jax.ShapeDtypeStruct(shape, jnp.bfloat16) for shape in shapes],
        compiler_params=pltpu.CompilerParams(vmem_limit_bytes=VMEM_LIMIT),
        cost_estimate=cost(4),
    )(place, own, other)


def to_line(place, kept, near, far, line):
    count, columns = kept.shape
    rows, half = count // line, count // 2
    alone = pl.BlockSpec((count, columns), lambda i, place: (0, 0))
    first = pl.BlockSpec((1, half, columns), lambda i, place: (0, 0, 0))
    last = pl.BlockSpec((half, columns), lambda i, place: (0, 0))
    part = pl.BlockSpec((rows, columns), lambda i, place: (0, 0))

    def kernel(place_ref, kept_ref, near_one, near_two, far_one, far_two, *out_refs):
        def fill(j, k):
            start = j * rows % half
            near_ref, far_ref = ((near_one, far_one), (near_two, far_two))[j * rows // half]
            total = kept_ref[j * rows : (j + 1) * rows].astype(jnp.float32)
            total = total + near_ref[0, start : start + rows].astype(jnp.float32)
            total = total + far_ref[start : start + rows].astype(jnp.float32)
            out_refs[k][...] = total.astype(jnp.bfloat16)

        for j in range(line):
            for k in range(line):
                there = lax.rem(place_ref[LINE_AT] + k, line) == j
                pl.when(there)(functools.partial(fill, j, k))

    return pl.pallas_call(
        kernel,
        grid_spec=pltpu.PrefetchScalarGridSpec(
            num_scalar_prefetch=1,
            grid=(1,),
            in_specs=[alone, first, first, last, last],
            out_specs=[part] * line,
        ),
        out_shape=[jax.ShapeDtypeStruct((rows, columns), jnp.bfloat16)] * line,
        compiler_params=pltpu.CompilerParams(vmem_limit_bytes=VMEM_LIMIT),
        cost_estimate=FREE,
    )(place, kept, *near, *far)


def input_terms(lefts, rights, dp, seq):
    count, model = lefts[0].shape
    columns = rights[0].shape[1]
    rest = model // (dp * seq)
    block, strip = model // 2, math.gcd(columns, 256)
    halves = dp // 2

    def kernel(left_a, left_b, right_a, right_b, out_ref, turned):
        turned[:, :count] = left_a[...].T
        turned[:, count:] = left_b[...].T

        def body(n, carry):
            at = pl.ds(pl.multiple_of(n * strip, strip), strip)
            term = matmul(turned[:, :count], right_a[:, at])
            term = (term + matmul(turned[:, count:], right_b[:, at])).astype(jnp.bfloat16)
            term = term.reshape(halves, seq, rest, strip)
            for i in range(halves):
                out_ref[:, i, :, at] = term[i]
            return carry

        lax.fori_loop(0, columns // strip, body, 0)

    left_spec = pl.BlockSpec((count, block), lambda i: (0, i))
    right_spec = pl.BlockSpec((count, columns), lambda i: (0, 0))
    return pl.pallas_call(
        kernel,
        grid=(2,),
        in_specs=[left_spec] * 2 + [right_spec] * 2,
        out_specs=pl.BlockSpec((seq, halves, rest, columns), lambda i: (0, i, 0, 0)),
        out_shape=jax.ShapeDtypeStruct((seq, dp, rest, columns), jnp.bfloat16),
        scratch_shapes=[pltpu.VMEM((block, 2 * count), jnp.bfloat16)],
        compiler_params=pltpu.CompilerParams(vmem_limit_bytes=VMEM_LIMIT),
        cost_estimate=cost(6),
    )(*lefts, *rights)


def tile_facts(place, span, tile):
    line = pl.num_programs(0) // 2
    row_tokens = line * 2 * span
    half = tile // line
    key_first = half * row_tokens + (tile % line) * 2 * span
    query_first = [(place[2] ^ j) * row_tokens + (2 * place[0] + place[1]) * span for j in (0, 1)]
    return key_first, query_first


def reach(key_first, keys, query_first, queries):
    key_last, query_last = key_first + keys - 1, query_first + queries - 1
    live = (key_first <= query_last) & (query_first - key_last < WINDOW)
    plain = (key_last < query_first) & (query_last - key_first < WINDOW)
    return live & plain, live & jnp.logical_not(plain)


def row_of(columns, scale):
    ones = jnp.full((8, columns.shape[1]), scale, jnp.float32)
    return lax.dot_general(
        ones,
        columns,
        (((1,), (1,)), ((), ())),
        precision=lax.Precision.HIGHEST,
        preferred_element_type=jnp.float32,
    )


def forward_kernel(
    place, query_ref, own_ref, other_ref, code_ref, segment_ref, out_ref, log_ref, acc, total
):
    tile = pl.program_id(0)
    span = query_ref.shape[1]
    key_first, query_first = tile_facts(place, span, tile)

    @pl.when(tile == 0)
    def _():
        acc[...] = jnp.zeros_like(acc)
        total[...] = jnp.zeros_like(total)

    def step(j, masked):
        keys = jnp.concatenate([own_ref[0, 0, :, :HEAD_DIM], other_ref[0, 0, :, :HEAD_DIM]], axis=0)
        values = jnp.concatenate(
            [own_ref[0, 0, :, HEAD_DIM:], other_ref[0, 0, :, HEAD_DIM:]], axis=0
        )
        allowed = code_ref[0, 0] == segment_ref[j]
        if masked:
            lane = lax.broadcasted_iota(jnp.int32, (1, 2 * span), 1)
            key_pos = key_first + lane + jnp.where(lane < span, place[1], -place[1]) * span
            query_pos = query_first[j] + lax.broadcasted_iota(jnp.int32, (span, 1), 0)
            back = query_pos - key_pos
            allowed = (allowed & (back > 0) & (back < WINDOW)) | (back == 0)
        for h in range(GROUP):
            query = query_ref[j, :, h * HEAD_DIM : (h + 1) * HEAD_DIM]
            scores = matmul_t(query, keys)
            weights = jnp.exp2(log2_scale * jnp.tanh(scores * score_scale))
            weights = jnp.where(allowed, weights, 0.0)
            total[j, h] += jnp.sum(weights, axis=-1, keepdims=True)
            acc[j, h] += matmul(weights.astype(jnp.bfloat16), values)

    for j in (0, 1):
        plain, masked = reach(key_first, 2 * span, query_first[j], span)
        pl.when(plain)(functools.partial(step, j, False))
        pl.when(masked)(functools.partial(step, j, True))

    @pl.when(tile == pl.num_programs(0) - 1)
    def _():
        for j in (0, 1):
            for h in range(GROUP):
                out_ref[j, :, h * HEAD_DIM : (h + 1) * HEAD_DIM] = (
                    acc[j, h] / total[j, h]
                ).astype(jnp.bfloat16)
                column = jnp.broadcast_to(jnp.log2(total[j, h]), (span, 128))
                log_ref[j, :, h * span : (h + 1) * span] = row_of(column, 1.0 / 128)


def backward_kernel(
    place, query_ref, grad_ref, attended_ref, own_ref, other_ref, code_ref, log_ref, segment_ref,
    query_grad_ref, own_grad_ref, other_grad_ref,
    queries, grads, query_acc, key_acc, value_acc, delta,
):
    tile = pl.program_id(0)
    span = query_ref.shape[1]
    key_first, query_first = tile_facts(place, span, tile)

    @pl.when(tile == 0)
    def _():
        query_acc[...] = jnp.zeros_like(query_acc)
        for j in (0, 1):
            for h in range(GROUP):
                rows, columns = pl.ds(h * span, span), slice(h * HEAD_DIM, (h + 1) * HEAD_DIM)
                queries[j, rows, :] = query_ref[j, :, columns]
                grads[j, rows, :] = grad_ref[j, :, columns]
                products = grad_ref[j, :, columns].astype(jnp.float32) * attended_ref[
                    j, :, columns
                ].astype(jnp.float32)
                delta[j, :, h * span : (h + 1) * span] = row_of(products, 1.0)

    def step(j, side, side_first, keys, values, masked):
        allowed = code_ref[0, 0, pl.ds(side * span, span), :] == segment_ref[j, 0:1, :]
        if masked:
            lane = lax.broadcasted_iota(jnp.int32, (1, GROUP * span), 1)
            query_pos = query_first[j] + jnp.where(lane < span, lane, lane - span)
            key_pos = side_first + lax.broadcasted_iota(jnp.int32, (span, 1), 0)
            back = query_pos - key_pos
            allowed = (allowed & (back > 0) & (back < WINDOW)) | (back == 0)
        squashed = jnp.tanh(matmul_t(keys, queries[j]) * score_scale)
        weights = jnp.exp2(log2_scale * squashed - log_ref[j, 0:1, :])
        weights = jnp.where(allowed, weights, 0.0)
        grad_weights = matmul_t(values, grads[j])
        value_acc[side] += matmul(weights.astype(jnp.bfloat16), grads[j])
        grad_scores = weights * (grad_weights - delta[j, 0:1, :]) * (1.0 - squashed * squashed)
        grad_scores = grad_scores.astype(jnp.bfloat16)
        key_acc[side] += matmul(grad_scores, queries[j])
        query_acc[j] += inner_t(grad_scores, keys)

    key_acc[...] = jnp.zeros_like(key_acc)
    value_acc[...] = jnp.zeros_like(value_acc)
    scale = HEAD_DIM ** (-0.5)
    for side, key_ref, grad_out in ((0, own_ref, own_grad_ref), (1, other_ref, other_grad_ref)):
        side_first = key_first + (place[1] if side == 0 else 1 - place[1]) * span

        def on_side(j, masked, side=side, side_first=side_first, key_ref=key_ref):
            keys, values = key_ref[0, 0, :, :HEAD_DIM], key_ref[0, 0, :, HEAD_DIM:]
            step(j, side, side_first, keys, values, masked)

        for j in (0, 1):
            plain, masked = reach(side_first, span, query_first[j], span)
            pl.when(plain)(functools.partial(on_side, j, False))
            pl.when(masked)(functools.partial(on_side, j, True))
        grad_out[0, 0, :, :HEAD_DIM] = (key_acc[side] * scale).astype(jnp.bfloat16)
        grad_out[0, 0, :, HEAD_DIM:] = value_acc[side].astype(jnp.bfloat16)

    @pl.when(tile == pl.num_programs(0) - 1)
    def _():
        for j in (0, 1):
            for h in range(GROUP):
                query_grad_ref[j, :, h * HEAD_DIM : (h + 1) * HEAD_DIM] = (
                    query_acc[j, h * span : (h + 1) * span, :] * scale
                ).astype(jnp.bfloat16)


def whole(*shape):
    return pl.BlockSpec(shape, lambda tile, place: (0,) * len(shape))


def tile_specs(line, span):
    def key_place(tile, place):
        return (tile % line, (tile // line) ^ place[2], 0, 0)

    def code_place(tile, place):
        return ((tile // line) ^ place[2], tile % line, 0, 0)

    return pl.BlockSpec((1, 1, span, 2 * HEAD_DIM), key_place), code_place


def attention_forward(place, queries, own, other, codes, segments):
    line, _, span, width = own.shape
    tile_spec, code_place = tile_specs(line, span)
    return pl.pallas_call(
        forward_kernel,
        grid_spec=pltpu.PrefetchScalarGridSpec(
            num_scalar_prefetch=1,
            grid=(2 * line,),
            in_specs=[
                whole(2, span, width),
                tile_spec,
                tile_spec,
                pl.BlockSpec((1, 1, 1, 2 * span), code_place),
                whole(2, span, 1),
            ],
            out_specs=[whole(2, span, width), whole(2, 8, GROUP * span)],
            scratch_shapes=[
                pltpu.VMEM((2, GROUP, span, HEAD_DIM), jnp.float32),
                pltpu.VMEM((2, GROUP, span, 1), jnp.float32),
            ],
        ),
        out_shape=[
            jax.ShapeDtypeStruct((2, span, width), jnp.bfloat16),
            jax.ShapeDtypeStruct((2, 8, GROUP * span), jnp.float32),
        ],
        compiler_params=pltpu.CompilerParams(vmem_limit_bytes=VMEM_LIMIT),
        cost_estimate=cost(6),
    )(place, queries, own, other, codes, segments)


def attention_backward(place, queries, grads, attended, own, other, codes, logs, segments):
    line, _, span, width = own.shape
    tile_spec, code_place = tile_specs(line, span)
    return pl.pallas_call(
        backward_kernel,
        grid_spec=pltpu.PrefetchScalarGridSpec(
            num_scalar_prefetch=1,
            grid=(2 * line,),
            in_specs=[
                whole(2, span, width),
                whole(2, span, width),
                whole(2, span, width),
                tile_spec,
                tile_spec,
                pl.BlockSpec((1, 1, 2 * span, 1), code_place),
                whole(2, 8, GROUP * span),
                whole(2, 8, GROUP * span),
            ],
            out_specs=[whole(2, span, width), tile_spec, tile_spec],
            scratch_shapes=[
                pltpu.VMEM((2, GROUP * span, HEAD_DIM), jnp.bfloat16),
                pltpu.VMEM((2, GROUP * span, HEAD_DIM), jnp.bfloat16),
                pltpu.VMEM((2, GROUP * span, HEAD_DIM), jnp.float32),
                pltpu.VMEM((2, span, HEAD_DIM), jnp.float32),
                pltpu.VMEM((2, span, HEAD_DIM), jnp.float32),
                pltpu.VMEM((2, 8, GROUP * span), jnp.float32),
            ],
        ),
        out_shape=[
            jax.ShapeDtypeStruct((2, span, width), jnp.bfloat16),
            jax.ShapeDtypeStruct(own.shape, jnp.bfloat16),
            jax.ShapeDtypeStruct(own.shape, jnp.bfloat16),
        ],
        compiler_params=pltpu.CompilerParams(vmem_limit_bytes=VMEM_LIMIT),
        cost_estimate=cost(12),
    )(place, queries, grads, attended, own, other, codes, logs, segments)


def body(
    tokens, pre_attention, post_attention, pre_feedforward, post_feedforward, w_query, key_weight,
    value_weight, w_output, w_gate, w_up, w_down, document_index, token_padding_mask, cotangent,
):
    bf16, f32 = jnp.bfloat16, jnp.float32
    dp, seq = lax.axis_size("dp"), lax.axis_size("seq")
    line, groups = seq // 2, dp // KEY_VALUE_HEADS
    dp_at, seq_at = lax.axis_index("dp"), lax.axis_index("seq")
    line_at, core = seq_at // 2, seq_at % 2
    head = dp_at % KEY_VALUE_HEADS
    half_bit = dp_at % 2
    _, span, model = tokens.shape
    rows = w_query.shape[0]
    ff = w_gate.shape[1]
    ff_rows = w_down.shape[0]
    ff_part = ff // line
    width = GROUP * HEAD_DIM

    order = Order()

    def attention_codes():
        sequence = dp_at // 2

        def by_pair(table):
            both = jnp.stack([pick(table, 0, sequence), pick(table, 0, sequence ^ 1)])
            both = both.reshape(2, 2, line, 2, span)
            both = jnp.where(half_bit == 1, both[:, ::-1], both)
            return jnp.where(core == 1, both[:, :, :, ::-1], both)

        segments = by_pair(document_index)
        codes = jnp.where(by_pair(token_padding_mask) == 1, segments, -1)
        return codes.reshape(2, 2, line, 2 * span), pick(segments[:, :, :, 0], 2, line_at)

    quad = groups == 1
    place = jnp.stack([line_at, core, half_bit, head]).astype(jnp.int32)
    inputs = tokens[0].astype(f32)
    flipped = pack_heads(place, w_query, key_weight, value_weight)
    split = split_columns(place, w_gate, w_up, dp, line)
    if quad:
        flipped, split, place = order(flipped, split, place)
        mixed = [flipped[0]] + [across(flipped[k], k) for k in (1, 2, 3)]
        normed_in = normed(inputs, pre_attention).astype(bf16)
        mixed, normed_in, split = order(order_heads(place, mixed), normed_in, split)
        near_normed = gather_quad_near(normed_in)
        in_weight = lax.all_gather(mixed, "seq", axis=1).reshape(model, 2 * width)
    else:
        normed_in = normed(inputs, pre_attention).astype(bf16)
        near_normed = gather_quad_near(normed_in)
        blocks = lax.all_gather(order_heads(place, flipped), ("dp", "seq"), axis=1, tiled=True)
        in_weight = pick(blocks, 0, head)

    per_device = line * rows
    split = exchange_line_parts(split)

    def ordered_split(split):
        (whole,) = deposit(
            place,
            [empty((2, line, rows, ff_part), bf16)],
            split,
            [
                (k, lambda at, w=w: (w,), 0, lambda at, w=w, k=k: (w, (at[LINE_AT] + line - k) % line))
                for k in range(line)
                for w in (0, 1)
            ],
        )
        return whole.reshape(2 * per_device, ff_part)

    def near_blocks(own):
        return gather_quad_near(own) if quad else (lax.all_gather(own, "dp", axis=0),)

    def far_blocks(near):
        return (gather_quad_far(*near),) if quad else ()

    def swap_all(blocks):
        return [swap_core(block) for block in blocks]

    down_weight = empty((dp, 2, ff_rows, model), bf16)
    gate_weight = empty((dp, line, 2, rows, ff_part), bf16)
    up_weight = empty((dp, line, 2, rows, ff_part), bf16)

    def sides(numbers, mine, swapped):
        for k, *blocks in zip(numbers, mine, swapped):
            for other, block in enumerate(blocks):
                yield k, other, block

    def at_dp(at, k):
        return at[HEAD_AT] ^ k if quad else pl.ds(0, dp)

    def fill_down(weight, numbers, mine, swapped):
        sources, moves = [], []
        for k, other, block in sides(numbers, mine, swapped):
            target = lambda at, k=k, other=other: (at_dp(at, k), at[CORE_AT] ^ other)
            moves.append((len(sources), None, 0, target))
            sources.append(block)
        return deposit(place, [weight], sources, moves)[0] if sources else weight

    def fill_in(gate, up, numbers, mine, swapped):
        sources, moves = [], []
        for k, other, block in sides(numbers, mine, swapped):
            for which in (0, 1):
                source = lambda at, which=which: (slice(None),) * (not quad) + (which,)
                target = lambda at, k=k, other=other: (
                    at_dp(at, k), slice(None), at[CORE_AT] ^ other
                )
                moves.append((len(sources), source, which, target))
            lead = () if quad else (dp,)
            sources.append(block.reshape(lead + (2, line, rows, ff_part)))
        return deposit(place, [gate, up], sources, moves) if sources else (gate, up)

    def project(pair_rows):
        projected = matmul(pair_rows, in_weight).astype(bf16).reshape(2, span, 2 * width)
        return projected[..., :width], projected[..., width:]

    codes, own_segments = attention_codes()
    row_codes = codes[:, :, :, None, :]
    column_segments = own_segments[..., None]
    near_normed, in_weight, split, row_codes, column_segments = order(
        near_normed, in_weight, split, row_codes, column_segments
    )
    far_normed = gather_quad_far_parts(*near_normed)
    first_rows = jnp.concatenate([normed_in, near_normed[0]], axis=0)
    first_queries, first_keys = project(first_rows)
    first_queries, first_keys, first_rows, far_normed = order(
        first_queries, first_keys, first_rows, far_normed
    )
    first_own = gather_line(first_keys)
    gate_up = ordered_split(split)
    second_rows = jnp.concatenate([near_normed[1], *far_normed], axis=0)
    second_queries, second_keys = project(second_rows)
    second_queries, second_keys, second_rows, gate_up = order(
        second_queries, second_keys, second_rows, gate_up
    )
    second_own = gather_line(second_keys)
    normed_rows = [first_rows, second_rows]
    near_in = near_blocks(gate_up)
    swapped = swap_all([gate_up] if quad else [])
    column_codes = [codes[pair][..., None] for pair in (0, 1)]
    lane_segments = jnp.broadcast_to(
        own_segments[:, :, None, None, :], (2, 2, 8, GROUP, span)
    ).reshape(2, 2, 8, GROUP * span)
    lane_segments = [lane_segments[0], lane_segments[1]]
    swapped, first_own, column_codes, lane_segments = order(
        swapped, first_own, column_codes, lane_segments
    )
    first_other = order(swap_core(first_own))
    attended, log_total = [None, None], [None, None]
    attended[0], log_total[0] = attention_forward(
        place, first_queries, first_own, first_other, row_codes[0], column_segments[0]
    )
    if quad:
        gate_weight, up_weight = fill_in(gate_weight, up_weight, (0,), [gate_up], swapped)
    attended[0], log_total[0], gate_weight, up_weight, near_in = order(
        attended[0], log_total[0], gate_weight, up_weight, near_in
    )
    far_in = far_blocks(near_in)
    swapped = swap_all(near_in)
    second_own, swapped, far_in = order(second_own, swapped, far_in)
    second_other = swap_core(second_own)
    if quad:
        out_weight = lax.all_gather(after(w_output, second_own), "seq", axis=0, tiled=True)
    else:
        out_weight = lax.dynamic_slice_in_dim(
            lax.all_gather(w_output, ("dp", "seq"), axis=0, tiled=True), head * width, width
        )
    numbers = (1, 2, 3) if quad else (0,)
    near_swapped = swapped
    second_other = order(second_other)
    swapped = swap_all(far_in)
    attended[1], log_total[1] = attention_forward(
        place, second_queries, second_own, second_other, row_codes[1], column_segments[1]
    )
    attended, log_total, out_weight, swapped = order(attended, log_total, out_weight, swapped)
    in_blocks, swapped = list(near_in) + list(far_in), near_swapped + swapped
    queries = [first_queries, second_queries]
    own_keys, other_keys = [first_own, second_own], [first_other, second_other]

    def activation(gate_in, up_in):
        return jax.nn.gelu(gate_in, approximate=True) * up_in

    step = span // 2
    chunks = [slice(0, step), slice(step, 2 * step)]
    grad_output = cotangent[0].astype(f32)

    def into_feedforward(part, kept, near, far):
        attn_out = scatter_quad_end(kept, near, far)
        residual = inputs[part] + normed(attn_out, post_attention)
        return attn_out, residual, normed(residual, pre_feedforward).astype(bf16)

    sent_a, kept_a = order(quad_terms(attended, out_weight, chunks[0], False))
    near_a = scatter_quad_near(sent_a)
    sent_b, kept_b = quad_terms(attended, out_weight, chunks[1], False)
    near_a, sent_b, kept_b = order(near_a, sent_b, kept_b)
    far_a = scatter_quad_far(kept_a, near_a)
    far_a, sent_b = order(far_a, sent_b)
    near_b = scatter_quad_near(sent_b)
    attn_out_a, residual_a, mid_a = order(into_feedforward(chunks[0], kept_a, near_a, far_a))
    mid_rows_a = gather_line(mid_a).reshape(line * step, model)
    near_b = order(near_b)
    far_b = order(scatter_quad_far(kept_b, near_b))
    attn_out_b, residual_b, mid_b = order(into_feedforward(chunks[1], kept_b, near_b, far_b))
    mid_rows_b = gather_line(mid_b).reshape(line * step, model)
    own_down = after(w_down, far_b[0])
    near_down = near_blocks(own_down)
    gate_weight, up_weight = fill_in(gate_weight, up_weight, numbers, in_blocks, swapped)
    mid_rows_a, gate_weight, up_weight = order(mid_rows_a, gate_weight, up_weight)
    gate_weight = gate_weight.reshape(model, ff_part)
    up_weight = up_weight.reshape(model, ff_part)
    gate_a = matmul(mid_rows_a, gate_weight)
    gate_a, mid_rows_a, near_down = order(gate_a, mid_rows_a, near_down)
    far_down = far_blocks(near_down)
    down_blocks = ([own_down] if quad else []) + list(near_down)
    swapped = swap_all(down_blocks)
    up_a = matmul(mid_rows_a, up_weight)
    gate_a, up_a, far_down, swapped = order(gate_a, up_a, far_down, swapped)
    down_weight = fill_down(down_weight, range(3), down_blocks, swapped)
    swapped = swap_all(far_down)
    down_weight, swapped = order(down_weight, swapped)
    down_weight = fill_down(down_weight, (3,), far_down, swapped)
    down_weight = down_weight.reshape(ff_part, model)

    def feedforward(gate_value, up_value):
        hidden = activation(gate_value, up_value).astype(bf16)
        down_part = matmul(hidden, down_weight).astype(bf16).reshape(line, step, model)
        return gate_value, up_value, hidden, down_part

    def output_of(part, residual, down_out):
        down_out = down_out.astype(f32)
        normed_down, down_back = jax.vjp(normed, down_out, post_feedforward)
        grad_down, gain_part = down_back(grad_output[part])
        return residual + normed_down, grad_down.astype(bf16), gain_part

    def feedforward_back(down_rows, gate_value, up_value):
        grad_hidden = matmul_t(down_rows, down_weight)
        _, act_back = jax.vjp(activation, gate_value, up_value)
        grad_gate, grad_up = act_back(grad_hidden)
        grad_gate, grad_up = grad_gate.astype(bf16), grad_up.astype(bf16)
        mid_part = matmul_t(grad_gate, gate_weight) + matmul_t(grad_up, up_weight)
        return grad_gate, grad_up, mid_part.astype(bf16).reshape(line, step, model)

    def attention_grad(part, residual, attn_out, grad_mid):
        _, mid_back = jax.vjp(normed, residual, pre_feedforward)
        grad_residual, grad_pre = mid_back(grad_mid.astype(f32))
        grad_residual = grad_output[part] + grad_residual
        _, attn_back = jax.vjp(normed, attn_out, post_attention)
        grad_attn, grad_post = attn_back(grad_residual)
        return grad_residual, grad_attn.astype(bf16), grad_pre, grad_post

    gate_a, up_a, hidden_a, down_a = order(feedforward(gate_a, up_a))
    down_a = scatter_line(down_a)
    mid_rows_b = order(mid_rows_b)
    gate_b, up_b, hidden_b, down_b = order(
        feedforward(matmul(mid_rows_b, gate_weight), matmul(mid_rows_b, up_weight))
    )
    down_b = scatter_line(down_b)
    down_a = order(down_a)
    result_a, grad_down_a, post_ff_a = order(output_of(chunks[0], residual_a, down_a))
    down_rows_a = gather_line(grad_down_a).reshape(line * step, model)
    down_b = order(down_b)
    result_b, grad_down_b, post_ff_b = order(output_of(chunks[1], residual_b, down_b))
    down_rows_b = gather_line(grad_down_b).reshape(line * step, model)
    down_rows_a = order(down_rows_a)
    grad_gate_a, grad_up_a, mid_part = order(feedforward_back(down_rows_a, gate_a, up_a))
    grad_mid_a = scatter_line(mid_part)
    down_rows_b = order(down_rows_b)
    grad_gate_b, grad_up_b, mid_part = order(feedforward_back(down_rows_b, gate_b, up_b))
    grad_mid_b = scatter_line(mid_part)
    result = jnp.concatenate([result_a, result_b], axis=0)

    def halves(lefts, rights, inner):
        if inner % 8 == 0:
            return weight_halves(place, lefts, rights, inner)
        term = sum(inner_t(left, right) for left, right in zip(lefts, rights))
        term = term.astype(bf16).reshape(-1, 2, inner, rights[0].shape[1])
        return pick(term, 1, core), pick(term, 1, 1 - core)

    def from_cores(own, moved, inner, plan, *shapes):
        own, moved = own.reshape(dp, inner, -1), moved.reshape(dp, inner, -1)
        if not quad:
            return own + moved
        shapes = [tuple(shape) + (own.shape[-1],) for shape in shapes]
        return combine_quad(place, own, moved, shapes, plan)

    def quad_plan(inner):
        low, high = slice(0, inner // 2), slice(inner // 2, inner)
        plan = [
            [(2, None, slice(0, inner))],
            [(0, 0, low), (4, None, high)],
            [(1, 0, high), (3, None, low)],
            [(0, 1, low), (1, 1, high)],
        ]
        half = inner // 2
        return plan, (2, half), (2, half), (inner,), (half,), (half,)

    def combine(own, moved, inner):
        parts = from_cores(own, moved, inner, *quad_plan(inner))
        return (parts[:2], parts[2:]) if quad else (parts, ())

    def near_sums(sent):
        return scatter_quad_near(sent) if quad else ()

    def far_sums(kept, near):
        if not quad:
            return ()
        return across(add_second(kept[1], near[0]), 2), across(add_second(kept[2], near[1]), 1)

    def line_parts(sent, kept, near, far):
        if quad:
            return to_line(place, kept[0], near, far, line)
        total = lax.psum_scatter(sent, "dp", scatter_dimension=0).reshape(line, rows, ff_part)
        return [pick(total, 0, (line_at + k) % line) for k in range(line)]

    mid_rows, hiddens, down_rows = (mid_rows_a, mid_rows_b), (hidden_a, hidden_b), (
        down_rows_a, down_rows_b
    )
    grad_gates, grad_ups = (grad_gate_a, grad_gate_b), (grad_up_a, grad_up_b)
    gate_own, gate_other = halves(mid_rows, grad_gates, rows)
    grad_mid_a, gate_own, gate_other = order(grad_mid_a, gate_own, gate_other)
    gate_other = swap_core(gate_other)
    grad_residual_a, grad_attn, pre_ff_a, post_attn_a = attention_grad(
        chunks[0], residual_a, attn_out_a, grad_mid_a
    )
    grad_residual_a, grad_attn, pre_ff_a, post_attn_a, gate_other = order(
        grad_residual_a, grad_attn, pre_ff_a, post_attn_a, gate_other
    )
    near_a = gather_quad_near(grad_attn)
    gate_sent, gate_kept = combine(gate_own, gate_other, per_device)
    near_a, gate_sent, gate_kept, mid_rows, grad_ups = order(
        near_a, gate_sent, gate_kept, mid_rows, grad_ups
    )
    far_a = gather_quad_far_parts(*near_a)
    gate_near = near_sums(gate_sent)
    up_own, up_other = halves(mid_rows, grad_ups, rows)
    far_a, gate_near, up_own, up_other = order(far_a, gate_near, up_own, up_other)
    quad_a = [grad_attn, *near_a, jnp.concatenate(far_a, axis=0)]
    gate_far = far_sums(gate_kept, gate_near)
    up_other = swap_core(up_other)
    grad_mid_b = order(grad_mid_b)
    grad_residual_b, grad_attn, pre_ff_b, post_attn_b = order(
        attention_grad(chunks[1], residual_b, attn_out_b, grad_mid_b)
    )
    near_b = gather_quad_near(grad_attn)
    up_sent, up_kept = combine(up_own, up_other, per_device)
    near_b, up_sent, up_kept, gate_far, quad_a = order(near_b, up_sent, up_kept, gate_far, quad_a)
    far_b = gather_quad_far_parts(*near_b)
    grad_residual = jnp.concatenate([grad_residual_a, grad_residual_b], axis=0)

    def attention_rows(blocks_a, blocks_b):
        return jnp.concatenate(
            [block for pair in zip(blocks_a, blocks_b) for block in pair], axis=0
        )

    def attended_grad(attn_rows):
        return matmul_t(attn_rows, out_weight).astype(bf16).reshape(2, span, width)

    def attend_back(pair, grad_attended):
        return attention_backward(
            place, queries[pair], grad_attended, attended[pair], own_keys[pair], other_keys[pair],
            column_codes[pair], log_total[pair], lane_segments[pair],
        )

    def owned_gains(terms):
        terms = jnp.stack(terms, axis=1)
        count = terms.shape[1]
        if not quad:
            return lax.psum_scatter(terms, ("dp", "seq"), scatter_dimension=0, tiled=True)
        terms = terms.reshape(dp, line, 2, rows * count)
        terms = sum(
            (across(pick(terms, 0, head ^ k), k) for k in (1, 2, 3)), pick(terms, 0, head)
        )
        terms = pick(terms, 1, core) + swap_core(pick(terms, 1, 1 - core))
        return jnp.sum(exchange_line(terms, line_at), axis=0).reshape(rows, count)

    def project_back(grad_queries, key_grads):
        grad_projected = jnp.concatenate([grad_queries, key_grads], axis=2)
        return grad_projected, grad_projected.reshape(2 * span, 2 * width)

    first_attn = attention_rows(quad_a[:2], [grad_attn, near_b[0]])
    gate_line = line_parts(gate_sent, gate_kept, gate_near, gate_far)
    far_b, grad_attended, gate_line = order(far_b, attended_grad(first_attn), gate_line)
    gate_line = exchange_line_parts(gate_line)
    up_near = near_sums(up_sent)
    first_grads, own_grad, other_grad, far_b, gate_line = order(
        *attend_back(0, grad_attended), far_b, gate_line
    )
    swapped = swap_core(other_grad)
    second_attn = attention_rows(quad_a[2:], [near_b[1], jnp.concatenate(far_b, axis=0)])
    grad_attended = attended_grad(second_attn)
    swapped, grad_attended = order(swapped, grad_attended)
    first_key_grads, up_near = order(own_grad + swapped, up_near)
    first_key_grads = scatter_line(first_key_grads)
    up_far = far_sums(up_kept, up_near)
    second_grads, own_grad, other_grad, up_far = order(*attend_back(1, grad_attended), up_far)
    swapped = swap_core(other_grad)
    up_line = line_parts(up_sent, up_kept, up_near, up_far)
    swapped, up_line = order(swapped, up_line)
    second_key_grads, first_key_grads, hiddens, down_rows = order(
        own_grad + swapped, first_key_grads, hiddens, down_rows
    )
    second_key_grads = scatter_line(second_key_grads)

    down_own, down_other = halves(hiddens, down_rows, ff_rows)
    output_term = inner_t(attended[0].reshape(2 * span, width), first_attn)
    output_term += inner_t(attended[1].reshape(2 * span, width), second_attn)
    output_term = output_term.astype(bf16)
    second_key_grads, up_line, down_own, down_other, output_term = order(
        second_key_grads, up_line, down_own, down_other, output_term
    )

    first_grad, first_rows = project_back(first_grads, first_key_grads)
    second_grad, second_rows = project_back(second_grads, second_key_grads)
    sent, kept = quad_terms((first_grad, second_grad), in_weight, slice(0, span), True)
    sent, kept, first_rows, second_rows = order(sent, kept, first_rows, second_rows)
    near = scatter_quad_near(sent)
    if quad:
        output_shard = lax.psum_scatter(output_term, "seq", scatter_dimension=0, tiled=True)
    else:
        spread = jnp.zeros((KEY_VALUE_HEADS, width, model), bf16).at[head].set(output_term)
        output_shard = lax.psum_scatter(
            spread.reshape(KEY_VALUE_HEADS * width, model),
            ("dp", "seq"),
            scatter_dimension=0,
            tiled=True,
        )
    up_line = exchange_line_parts(up_line)
    down_other = swap_core(down_other)
    if quad:
        in_term = order(input_terms(normed_rows, (first_rows, second_rows), dp, seq))
        in_part = lax.psum_scatter(
            in_term.reshape(model, 2 * width), "seq", scatter_dimension=0, tiled=True
        )
        near, up_line = order(near, up_line)
        far = scatter_quad_far(kept, near)
        down_sent, down_kept = combine(down_own, down_other, ff_rows)
        far, down_sent, down_kept = order(far, down_sent, down_kept)
        down_near = scatter_quad_near(down_sent)
    else:
        in_term = inner_t(normed_rows[0], first_rows) + inner_t(normed_rows[1], second_rows)
        near, in_term = order(near, in_term.astype(bf16))
        far = order(scatter_quad_far(kept, near))
        down_mine, _ = combine(down_own, down_other, ff_rows)
        down_shard = lax.psum_scatter(down_mine, "dp", scatter_dimension=0).astype(f32)
    grad_in = scatter_quad_end(kept, near, far)
    _, in_back = jax.vjp(normed, inputs, pre_attention)
    grad_inputs, grad_pre_attn = in_back(grad_in)
    grad_pre_attn, grad_inputs = order(grad_pre_attn, grad_inputs)
    gains = owned_gains(
        [grad_pre_attn, post_attn_a + post_attn_b, pre_ff_a + pre_ff_b, post_ff_a + post_ff_b]
    )
    tokens_grad = grad_residual + grad_inputs
    if quad:
        gains, down_near, in_part = order(gains, down_near, in_part)
        down_far = scatter_quad_far(down_kept, down_near)
        down_shard = scatter_quad_end(down_kept, down_near, down_far)
    gate_shard, up_shard = join_columns(place, gate_line, dp), join_columns(place, up_line, dp)
    if quad:
        part_shard = exchange_quad(in_part.reshape(dp, rows, 2 * width), head)
    else:
        spread = jnp.zeros((KEY_VALUE_HEADS, model, 2 * width), bf16).at[head].set(in_term)
        part_shard = lax.psum_scatter(spread, ("dp", "seq"), scatter_dimension=1, tiled=True)
    part_shard = part_shard.astype(f32).transpose(1, 0, 2)
    query_shard = part_shard[..., :width].reshape(rows, KEY_VALUE_HEADS * width)
    key_shard = part_shard[..., width : width + HEAD_DIM].reshape(rows, KEY_VALUE_HEADS * HEAD_DIM)
    value_shard = part_shard[..., width + HEAD_DIM :].reshape(rows, KEY_VALUE_HEADS * HEAD_DIM)
    return (
        result[None],
        tokens_grad[None],
        query_shard,
        key_shard,
        value_shard,
        output_shard.astype(f32),
        gate_shard,
        up_shard,
        down_shard,
        gains[:, 0],
        gains[:, 1],
        gains[:, 2],
        gains[:, 3],
    )


def solution(mesh):
    tokens, weights, whole_copy = P("dp", "seq", None), P(("dp", "seq"), None), P()
    gains = P(("dp", "seq"))
    return jax.shard_map(
        body,
        mesh=mesh,
        in_specs=(tokens,) + (whole_copy,) * 4 + (weights,) * 7 + (whole_copy,) * 2 + (tokens,),
        out_specs=(tokens,) * 2 + (weights,) * 7 + (gains,) * 4,
        check_vma=False,
    )
```

time: 1500 us -> 1280 us (0.85)
  Pallas kernels: 71.3 us -> 274 us
  waiting for transfers between devices: 696 us -> 522 us
  matrix products: 275 us -> 183 us
  local copies, waits for them, and re-layouts: 173 us -> 83.5 us
  other arithmetic: 146 us -> 91.2 us
    pallas_call x2 -> x26, Pallas kernels: 8.38 us -> 208 us  [the longest x3 81.1 us: weight_halves(): pl.pallas_call(kernel, grid=(model // block,), in_specs=[pl.BlockSpec(mem...]
    ppermute x52 -> x53, waiting for transfers between devices: 279 us -> 145 us  [across(): lax.ppermute(x, 'dp', [(i, i ^ bits) for i in range(lax.axis_size('dp'))])]
    ppermute x12, waiting for transfers between devices: 30.7 us -> 112 us  [exchange_line_parts(): lax.ppermute(parts[k], 'seq', line_route(line, k))]
    dot_general x7 -> x2, matrix products: 78.8 us -> 7.45 us  [inner_t(): lax.dot_general(a, b, (((0,), (0,)), ((), ())), preferred_element_type=jn...]
    unnamed x17 -> x16, waiting for transfers between devices: 63.2 us -> 0.26 us
    dynamic_update_slice x16 -> x0, local copies, waits for them, and re-layouts: 39.3 us -> none  [the longest x8 18.5 us: fill_down(): lax.dynamic_update_slice(weight, block.reshape(-1, 1, ff_rows, model), (a...]
    reduce_scatter x6, waiting for transfers between devices: 143 us -> 108 us  [scatter_line(): lax.psum_scatter(x, 'seq', scatter_dimension=0, axis_index_groups=line_gr...]
    all_gather x6, waiting for transfers between devices: 157 us -> 128 us  [gather_line(): return lax.all_gather(x, 'seq', axis=0, axis_index_groups=line_groups())]
  transfers between devices with their start and end apart: 97 -> 97, of which waited for: 47 -> 46; matrix products, arithmetic and copies ran while one was open for 27% -> 24% of each run, Pallas kernels for 5% -> 21%
where the time goes in v2:
time: 1280 us; the launch traced here: 1260 us
  waiting for transfers between devices  522 us (41%)
  Pallas kernels  274 us (21%)
  matrix products  183 us (14%)
  starting transfers between devices  94 us (7%)
  other arithmetic  91.2 us (7%)
  local copies, waits for them, and re-layouts  83.5 us (7%)
  between operations  16.1 us (1%)
    ppermute x53, waiting for transfers between devices, across(): lax.ppermute(x, 'dp', [(i, i ^ bits) for i in range(lax.axis_size('dp'))])  145 us
    all_gather x6, waiting for transfers between devices, gather_line(): return lax.all_gather(x, 'seq', axis=0, axis_index_groups=line_groups())  128 us
    ppermute x12, waiting for transfers between devices, exchange_line_parts(): lax.ppermute(parts[k], 'seq', line_route(line, k))  112 us
    reduce_scatter x6, waiting for transfers between devices, scatter_line(): lax.psum_scatter(x, 'seq', scatter_dimension=0, axis_index_groups=line_gr...  108 us
    dot_general x8, matrix products, matmul_t(): lax.dot_general(a, b, (((1,), (1,)), ((), ())), preferred_element_type=jn...  91.1 us
    dot_general x8, matrix products, matmul(): return jnp.dot(a, b, preferred_element_type=jnp.float32)  84 us
    pallas_call x3, Pallas kernels, weight_halves(): pl.pallas_call(kernel, grid=(model // block,), in_specs=[pl.BlockSpec(mem...  81.1 us
    ppermute x53, starting transfers between devices, across(): lax.ppermute(x, 'dp', [(i, i ^ bits) for i in range(lax.axis_size('dp'))])  60.6 us
  transfers between devices with their start and end apart: 97, of which 46 were waited for; matrix products, arithmetic and copies ran while one was open for 24% of the time, Pallas kernels for 21%

profile of v2, /device:TPU:0, one launch (start us, length us, event | category | flops | bytes accessed | tf_op | source)
XLA Modules:
  0.0 1263.7 jit_solution(8499316459926429810)
XLA Ops:
  41.8 20.9 %collective-permute-done.5.refs_5_ = bf16[2,72,2304]{2,1,0:T(8,128)(2,1)} collective-permute-done((bf16[2,72,2304]{2,1,0:T(8,128)(2,1)}, bf16[2,72,2304]{2,1,0:T(8,128)(2,1)}, u32[]{:S(2)}, u32[]{:S(2)}) %collective-permute-start.5) | collective-permute-done | bytes 663584 | tf_op jit(solution)/shard_map/ppermute | solution.py:66
  62.8 46.9 %collective-permute-done.6.refs_6_ = bf16[2,72,2304]{2,1,0:T(8,128)(2,1)} collective-permute-done((bf16[2,72,2304]{2,1,0:T(8,128)(2,1)}, bf16[2,72,2304]{2,1,0:T(8,128)(2,1)}, u32[]{:S(2)}, u32[]{:S(2)}) %collective-permute-start.6) | collective-permute-done | bytes 663584 | tf_op jit(solution)/shard_map/ppermute | solution.py:66
  168.3 38.7 %all-gather.20.cloned.1.call-done = bf16[8,320,512]{2,1,0:T(8,128)(2,1)} async-done(((bf16[2,320,512]{2,1,0:T(8,128)(2,1)}), bf16[8,320,512]{2,1,0:T(8,128)(2,1)}) %all-gather.20.cloned.1.call-update) | async-done | bytes 2621456 | tf_op jit(solution)/shard_map/all_gather | solution.py:55
  235.1 28.6 %collective-permute-done.16 = bf16[288,2304]{1,0:T(8,128)(2,1)S(1)} collective-permute-done((bf16[288,2304]{1,0:T(8,128)(2,1)S(1)}, bf16[288,2304]{1,0:T(8,128)(2,1)S(1)}, u32[]{:S(2)}, u32[]{:S(2)}) %collective-permute-start.16) | collective-permute-done | bytes 1327136 | tf_op jit(solution)/shard_map/ppermute | solution.py:42
  291.8 11.7 all-gather.16.cloned.1.call-done.refs_5_
  349.9 12.8 %collective-permute-done.24.refs_1_ = bf16[2,80,2304]{2,1,0:T(8,128)(2,1)} collective-permute-done((bf16[2,80,2304]{2,1,0:T(8,128)(2,1)S(1)}, bf16[2,80,2304]{2,1,0:T(8,128)(2,1)}, u32[]{:S(2)}, u32[]{:S(2)}) %collective-permute-start.24) | collective-permute-done | bytes 737312 | tf_op jit(solution)/shard_map/ppermute | solution.py:42
  389.3 18.5 %all-gather.24.cloned.1.call-done.refs_1_ = bf16[640,2304]{1,0:T(8,128)(2,1)} async-done(((bf16[160,2304]{1,0:T(8,128)(2,1)}), bf16[640,2304]{1,0:T(8,128)(2,1)}) %all-gather.24.cloned.1.call-update) | async-done | bytes 2949136 | tf_op jit(solution)/shard_map/all_gather | solution.py:55
  407.8 13.3 %fusion.93.refs_1_ = f32[640,2304]{1,0:T(8,128)} fusion(bf16[640,2304]{1,0:T(8,128)(2,1)} %get-tuple-element.485.refs_2_, bf16[2304,2304]{1,0:T(8,128)(2,1)} %bitcast.230), kind=kOutput, calls=%fused_computation.256 | convolution fusion | flops 6794772480 | bytes 19464192 | tf_op jit(solution)/shard_map/dot_general | solution.py:30
  428.1 13.3 %fusion.94.refs_2_ = f32[640,2304]{1,0:T(8,128)} fusion(bf16[640,2304]{1,0:T(8,128)(2,1)} %get-tuple-element.489.left_a.refs_8_, bf16[2304,2304]{1,0:T(8,128)(2,1)} %bitcast.224), kind=kOutput, calls=%fused_computation.257 | convolution fusion | flops 6794772480 | bytes 19464192 | tf_op jit(solution)/shard_map/dot_general | solution.py:30
  462.0 12.4 convolution_convert_fusion.1
  474.9 14.0 %fusion.95.refs_1_ = f32[640,2304]{1,0:T(8,128)} fusion(bf16[640,2304]{1,0:T(8,128)(2,1)} %get-tuple-element.506.left_b.refs_9_, bf16[2304,2304]{1,0:T(8,128)(2,1)} %bitcast.231), kind=kOutput, calls=%fused_computation.258 | convolution fusion | flops 6794772480 | bytes 19464192 | tf_op jit(solution)/shard_map/dot_general | solution.py:30
  513.3 16.4 %reduce-scatter.9.cloned.1.call-done = bf16[1,160,2304]{2,1,0:T(8,128)(2,1)} async-done(((bf16[4,160,2304]{2,1,0:T(8,128)(2,1)}), bf16[1,160,2304]{2,1,0:T(8,128)(2,1)}) %reduce-scatter.9.cloned.1.call-update) | async-done | bytes 737296 | tf_op jit(solution)/shard_map/reduce_scatter | solution.py:78
  537.7 51.5 %reduce-scatter.11.cloned.1.call-done = bf16[1,160,2304]{2,1,0:T(8,128)(2,1)} async-done(((bf16[4,160,2304]{2,1,0:T(8,128)(2,1)}), bf16[1,160,2304]{2,1,0:T(8,128)(2,1)}) %reduce-scatter.11.cloned.1.call-update) | async-done | bytes 737296 | tf_op jit(solution)/shard_map/reduce_scatter | solution.py:78
  597.9 53.1 %all-gather.28.cloned.1.call-done.refs_1_ = bf16[640,2304]{1,0:T(8,128)(2,1)} async-done(((bf16[160,2304]{1,0:T(8,128)(2,1)}), bf16[640,2304]{1,0:T(8,128)(2,1)}) %all-gather.28.cloned.1.call-update) | async-done | bytes 2949136 | tf_op jit(solution)/shard_map/all_gather | solution.py:55
  651.0 18.9 %multiply_convert_fusion.1 = (bf16[640,2304]{1,0:T(8,128)(2,1)}, bf16[640,2304]{1,0:T(8,128)(2,1)}) fusion(f32[640,2304]{1,0:T(8,128)} %get-tuple-element.524, f32[640,2304]{1,0:T(8,128)} %get-tuple-element.523, bf16[640,2304]{1,0:T(8,128)(2,1)} %get-tuple-element.522.refs_5_, bf16[2304,2304]{1,0:T(8,128)(2,1)} %bitcast.239), kind=kOutput, calls=%fused_computation.41 | convolution fusion | flops 6830161920 | bytes 31260672 | tf_op jit(solution)/shard_map/dot_general | solution.py:34
  680.1 13.8 %add_convert_fusion.1 = bf16[640,2304]{1,0:T(8,128)(2,1)} fusion(f32[640,2304]{1,0:T(8,128)} %fusion.96, bf16[640,2304]{1,0:T(8,128)(2,1)} %get-tuple-element.758.refs_2_, bf16[2304,2304]{1,0:T(8,128)(2,1)} %bitcast.225), kind=kOutput, calls=%fused_computation.40 | convolution fusion | flops 6797721600 | bytes 22413312 | tf_op jit(solution)/shard_map/dot_general | solution.py:34
  694.2 17.1 %all-gather.30.cloned.1.call-done.refs_1_ = bf16[640,2304]{1,0:T(8,128)(2,1)} async-done(((bf16[160,2304]{1,0:T(8,128)(2,1)}), bf16[640,2304]{1,0:T(8,128)(2,1)}) %all-gather.30.cloned.1.call-update) | async-done | bytes 2949136 | tf_op jit(solution)/shard_map/all_gather | solution.py:55
  711.3 18.9 %multiply_convert_fusion = (bf16[640,2304]{1,0:T(8,128)(2,1)}, bf16[640,2304]{1,0:T(8,128)(2,1)}) fusion(f32[640,2304]{1,0:T(8,128)} %get-tuple-element.530, f32[640,2304]{1,0:T(8,128)} %get-tuple-element.529, bf16[640,2304]{1,0:T(8,128)(2,1)} %get-tuple-element.528.refs_6_, bf16[2304,2304]{1,0:T(8,128)(2,1)} %bitcast.240), kind=kOutput, calls=%fused_computation.39 | convolution fusion | flops 6830161920 | bytes 31260672 | tf_op jit(solution)/shard_map/dot_general | solution.py:34
  740.6 13.8 %add_convert_fusion = bf16[640,2304]{1,0:T(8,128)(2,1)} fusion(f32[640,2304]{1,0:T(8,128)} %fusion.97, bf16[640,2304]{1,0:T(8,128)(2,1)} %get-tuple-element.756.refs_2_, bf16[2304,2304]{1,0:T(8,128)(2,1)} %bitcast.226), kind=kOutput, calls=%fused_computation.38 | convolution fusion | flops 6797721600 | bytes 22413312 | tf_op jit(solution)/shard_map/dot_general | solution.py:34
  754.4 27.0 %shard_map.297 = (bf16[16,72,2304]{2,1,0:T(8,128)(2,1)}, bf16[16,72,2304]{2,1,0:T(8,128)(2,1)}) custom-call(s32[4]{0:T(128)} %get-tuple-element.379.place_ref.place, bf16[640,2304]{1,0:T(8,128)(2,1)} %get-tuple-element.489.left_a.refs_8_, bf16[640,2304]{1,0:T(8,128)(2,1)} %get-tuple-element.506.left_b.refs_9_, bf16[640,2304]{1,0:T(8,128)(2,1)} %get-tuple-element.533.right_a, ...), custom_call_target="tpu_custom_call" | custom-call | tf_op jit(solution)/shard_map/pallas_call | solution.py:300
  817.7 27.0 %shard_map.302 = (bf16[16,72,2304]{2,1,0:T(8,128)(2,1)}, bf16[16,72,2304]{2,1,0:T(8,128)(2,1)}) custom-call(s32[4]{0:T(128)} %get-tuple-element.379.place_ref.place, bf16[640,2304]{1,0:T(8,128)(2,1)} %get-tuple-element.558.left_a, bf16[640,2304]{1,0:T(8,128)(2,1)} %get-tuple-element.559.left_b, bf16[640,2304]{1,0:T(8,128)(2,1)} %get-tuple-element.560.right_a, ...), custom_call_target="tpu_custom_call" | custom-call | tf_op jit(solution)/shard_map/pallas_call | solution.py:300
  878.9 13.2 %collective-permute-done.47.refs_9_ = bf16[144,2304]{1,0:T(8,128)(2,1)S(1)} collective-permute-done((bf16[144,2304]{1,0:T(8,128)(2,1)}, bf16[144,2304]{1,0:T(8,128)(2,1)S(1)}, u32[]{:S(2)}, u32[]{:S(2)}) %collective-permute-start.47) | collective-permute-done | bytes 663584 | tf_op jit(solution)/shard_map/ppermute | solution.py:42
  911.6 19.6 %shard_map.312 = (bf16[2,320,512]{2,1,0:T(8,128)(2,1)}, bf16[4,2,320,512]{3,2,1,0:T(8,128)(2,1)}, bf16[4,2,320,512]{3,2,1,0:T(8,128)(2,1)}) custom-call(s32[4]{0:T(128)} %get-tuple-element.379.place_ref.place, bf16[2,320,512]{2,1,0:T(8,128)(2,1)} %get-tuple-element.412.query_ref, bf16[2,320,512]{2,1,0:T(8,128)(2,1)} %get-tuple-element.598.grad_ref, ...), custom_call_target="tpu_custom_call" | custom-call | bytes 42000000 | tf_op jit(solution)/shard_map/pallas_call | solution.py:716
  943.8 20.3 %collective-permute-done.54.refs_2_ = bf16[2,144,2304]{2,1,0:T(8,128)(2,1)} collective-permute-done((bf16[2,144,2304]{2,1,0:T(8,128)(2,1)}, bf16[2,144,2304]{2,1,0:T(8,128)(2,1)}, u32[]{:S(2)}, u32[]{:S(2)}) %collective-permute-start.54) | collective-permute-done | bytes 1327136 | tf_op jit(solution)/shard_map/ppermute | solution.py:42
  971.4 19.6 %shard_map.316 = (bf16[2,320,512]{2,1,0:T(8,128)(2,1)}, bf16[4,2,320,512]{3,2,1,0:T(8,128)(2,1)}, bf16[4,2,320,512]{3,2,1,0:T(8,128)(2,1)}) custom-call(s32[4]{0:T(128)} %get-tuple-element.379.place_ref.place, bf16[2,320,512]{2,1,0:T(8,128)(2,1)} %get-tuple-element.429.query_ref, bf16[2,320,512]{2,1,0:T(8,128)(2,1)} %get-tuple-element.623.grad_ref, ...), custom_call_target="tpu_custom_call" | custom-call | bytes 42000000 | tf_op jit(solution)/shard_map/pallas_call | solution.py:716
  1003.6 20.8 %reduce-scatter.17.cloned.1.call-done = bf16[1,2,320,512]{3,2,1,0:T(8,128)(2,1)} async-done(((bf16[4,2,320,512]{3,2,1,0:T(8,128)(2,1)}), bf16[1,2,320,512]{3,2,1,0:T(8,128)(2,1)}) %reduce-scatter.17.cloned.1.call-update) | async-done | bytes 655376 | tf_op jit(solution)/shard_map/reduce_scatter | solution.py:78
  1033.0 27.1 %shard_map.323 = (bf16[4,288,2304]{2,1,0:T(8,128)(2,1)}, bf16[4,288,2304]{2,1,0:T(8,128)(2,1)}) custom-call(s32[4]{0:T(128)} %get-tuple-element.379.place_ref.place, bf16[640,2304]{1,0:T(8,128)(2,1)} %get-tuple-element.655.left_a, bf16[640,2304]{1,0:T(8,128)(2,1)} %get-tuple-element.656.left_b, bf16[640,2304]{1,0:T(8,128)(2,1)} %get-tuple-element.657.right_a, ...), custom_call_target="tpu_custom_call" | custom-call | tf_op jit(solution)/shard_map/pallas_call | solution.py:300
  1060.0 18.9 %reduce-scatter.19.cloned.1.call-done = bf16[1,2,320,512]{3,2,1,0:T(8,128)(2,1)} async-done(((bf16[4,2,320,512]{3,2,1,0:T(8,128)(2,1)}), bf16[1,2,320,512]{3,2,1,0:T(8,128)(2,1)}) %reduce-scatter.19.cloned.1.call-update) | async-done | bytes 655376 | tf_op jit(solution)/shard_map/reduce_scatter | solution.py:78
  1095.6 14.4 %shard_map.327.refs_1_ = bf16[8,4,72,1024]{3,2,1,0:T(8,128)(2,1)} custom-call(bf16[640,2304]{1,0:T(8,128)(2,1)} %get-tuple-element.672.left_a, bf16[640,2304]{1,0:T(8,128)(2,1)} %get-tuple-element.673.left_b, bf16[640,1024]{1,0:T(8,128)(2,1)} %get-tuple-element.674.right_a, bf16[640,1024]{1,0:T(8,128)(2,1)} %get-tuple-element.675.right_b), custom_call_target="tpu_custom_call" | custom-call | bytes 21000000 | tf_op jit(solution)/shard_map/pallas_call | solution.py:516
  1125.9 21.3 %collective-permute-done.62.refs_5_ = bf16[72,2304]{1,0:T(8,128)(2,1)S(1)} collective-permute-done((bf16[72,2304]{1,0:T(8,128)(2,1)}, bf16[72,2304]{1,0:T(8,128)(2,1)S(1)}, u32[]{:S(2)}, u32[]{:S(2)}) %collective-permute-start.62) | collective-permute-done | bytes 331808 | tf_op jit(solution)/shard_map/ppermute | solution.py:66
  1204.1 12.3 collective-permute-start.71
  1234.3 11.7 collective-permute-done.76
  (741 shorter events, 559.9 us)
Async XLA Ops:
  7.2 115.0 %all-gather.18.cloned.1.call-start = ((), (), s32[]{:S(2)}) async-start(), calls=%async_computation.17 | async-start | bytes 5308416 | tf_op jit(solution)/shard_map/all_gather | solution.py:795
  29.1 177.9 %all-gather.20.cloned.1.call-start = ((), (), s32[]{:S(2)}) async-start(), calls=%async_computation.18 | async-start | bytes 3276800 | tf_op jit(solution)/shard_map/all_gather | solution.py:55
  30.1 83.0 %collective-permute-start.3 = (bf16[320,2304]{1,0:T(8,128)(2,1)}, bf16[320,2304]{1,0:T(8,128)(2,1)}, u32[]{:S(2)}, u32[]{:S(2)}) collective-permute-start(bf16[320,2304]{1,0:T(8,128)(2,1)} %get-tuple-element.389), channel_id=1, source_target_pairs={{0,8},{8,0},{16,24},{24,16},{1,9},{9,1},{17,25},{25,17},{2,10},{10... | collective-permute-start | bytes 4423688 | tf_op jit(solution)/shard_map/ppermute | solution.py:42
  31.3 81.7 %collective-permute-start.4 = (bf16[320,2304]{1,0:T(8,128)(2,1)}, bf16[320,2304]{1,0:T(8,128)(2,1)}, u32[]{:S(2)}, u32[]{:S(2)}) collective-permute-start(bf16[320,2304]{1,0:T(8,128)(2,1)} %get-tuple-element.389), channel_id=1, source_target_pairs={{0,16},{8,24},{16,0},{24,8},{1,17},{9,25},{17,1},{25,9},{2,18},{10... | collective-permute-start | bytes 4423688 | tf_op jit(solution)/shard_map/ppermute | solution.py:42
  34.0 75.6 %collective-permute-start.6 = (bf16[2,72,2304]{2,1,0:T(8,128)(2,1)}, bf16[2,72,2304]{2,1,0:T(8,128)(2,1)}, u32[]{:S(2)}, u32[]{:S(2)}) collective-permute-start(bf16[2,72,2304]{2,1,0:T(8,128)(2,1)} %get-tuple-element.393), channel_id=1, source_target_pairs={{0,4},{1,5},{2,6},{3,7},{4,0},{5,1},{6,2},{7,3},{8,12},{9,13},{10,... | collective-permute-start | bytes 1990664 | tf_op jit(solution)/shard_map/ppermute | solution.py:66
  36.6 76.5 %collective-permute-start.7 = (bf16[2,72,2304]{2,1,0:T(8,128)(2,1)}, bf16[2,72,2304]{2,1,0:T(8,128)(2,1)}, u32[]{:S(2)}, u32[]{:S(2)}) collective-permute-start(bf16[2,72,2304]{2,1,0:T(8,128)(2,1)} %get-tuple-element.394), channel_id=1, source_target_pairs={{0,6},{1,7},{2,0},{3,1},{4,2},{5,3},{6,4},{7,5},{8,14},{9,15},{10,... | collective-permute-start | bytes 1990664 | tf_op jit(solution)/shard_map/ppermute | solution.py:66
  147.2 119.3 %all-gather.22.cloned.1.call-start = ((), (), s32[]{:S(2)}) async-start(), calls=%async_computation.19 | async-start | bytes 3276800 | tf_op jit(solution)/shard_map/all_gather | solution.py:55
  158.0 70.6 %collective-permute-start.12 = (bf16[576,2304]{1,0:T(8,128)(2,1)}, bf16[576,2304]{1,0:T(8,128)(2,1)}, u32[]{:S(2)}, u32[]{:S(2)}) collective-permute-start(bf16[576,2304]{1,0:T(8,128)(2,1)} %get-tuple-element.407), channel_id=1, source_target_pairs={{0,8},{8,0},{16,24},{24,16},{1,9},{9,1},{17,25},{25,17},{2,10},{10... | collective-permute-start | bytes 7962632 | tf_op jit(solution)/shard_map/ppermute | solution.py:42
  158.4 70.1 %collective-permute-start.13 = (bf16[576,2304]{1,0:T(8,128)(2,1)}, bf16[576,2304]{1,0:T(8,128)(2,1)}, u32[]{:S(2)}, u32[]{:S(2)}) collective-permute-start(bf16[576,2304]{1,0:T(8,128)(2,1)} %get-tuple-element.407), channel_id=1, source_target_pairs={{0,16},{8,24},{16,0},{24,8},{1,17},{9,25},{17,1},{25,9},{2,18},{10... | collective-permute-start | bytes 7962632 | tf_op jit(solution)/shard_map/ppermute | solution.py:42
  208.3 95.2 %all-gather.16.cloned.1.call-start = ((), (), s32[]{:S(2)}) async-start(), calls=%async_computation.8 | async-start | bytes 2654208 | tf_op jit(solution)/shard_map/all_gather | solution.py:910
  228.6 38.0 %collective-permute-start.14 = (bf16[576,2304]{1,0:T(8,128)(2,1)}, bf16[576,2304]{1,0:T(8,128)(2,1)S(1)}, u32[]{:S(2)}, u32[]{:S(2)}) collective-permute-start(bf16[576,2304]{1,0:T(8,128)(2,1)} %get-tuple-element.423), channel_id=1, source_target_pairs={{0,1},{1,0},{2,3},{3,2},{4,5},{5,4},{6,7},{7,6},{8,9},{9,8},{10,11... | collective-permute-start | bytes 7962632 | tf_op jit(solution)/shard_map/ppermute | solution.py:46
  229.2 37.4 %collective-permute-start.15 = (bf16[576,2304]{1,0:T(8,128)(2,1)}, bf16[576,2304]{1,0:T(8,128)(2,1)}, u32[]{:S(2)}, u32[]{:S(2)}) collective-permute-start(bf16[576,2304]{1,0:T(8,128)(2,1)} %get-tuple-element.424), channel_id=1, source_target_pairs={{0,1},{1,0},{2,3},{3,2},{4,5},{5,4},{6,7},{7,6},{8,9},{9,8},{10,11... | collective-permute-start | bytes 7962632 | tf_op jit(solution)/shard_map/ppermute | solution.py:46
  269.9 137.9 %all-gather.24.cloned.1.call-start = ((), (), s32[]{:S(2)}) async-start(), calls=%async_computation.20 | async-start | bytes 3686400 | tf_op jit(solution)/shard_map/all_gather | solution.py:55
  349.8 125.0 %all-gather.26.cloned.1.call-start = ((), (), s32[]{:S(2)}) async-start(), calls=%async_computation.21 | async-start | bytes 3686400 | tf_op jit(solution)/shard_map/all_gather | solution.py:55
  383.1 38.1 %collective-permute-start.28 = (bf16[288,2304]{1,0:T(8,128)(2,1)}, bf16[288,2304]{1,0:T(8,128)(2,1)S(1)}, u32[]{:S(2)}, u32[]{:S(2)}) collective-permute-start(bf16[288,2304]{1,0:T(8,128)(2,1)} %shard_map.279.refs_1_), channel_id=1, source_target_pairs={{0,8},{8,0},{16,24},{24,16},{1,9},{9,1},{17,25},{25,17},{2,10},{10... | collective-permute-start | bytes 3981320 | tf_op jit(solution)/shard_map/ppermute | solution.py:42
  384.1 37.1 %collective-permute-start.29 = (bf16[288,2304]{1,0:T(8,128)(2,1)}, bf16[288,2304]{1,0:T(8,128)(2,1)}, u32[]{:S(2)}, u32[]{:S(2)}) collective-permute-start(bf16[288,2304]{1,0:T(8,128)(2,1)} %shard_map.279.refs_1_), channel_id=1, source_target_pairs={{0,16},{8,24},{16,0},{24,8},{1,17},{9,25},{17,1},{25,9},{2,18},{10... | collective-permute-start | bytes 3981320 | tf_op jit(solution)/shard_map/ppermute | solution.py:42
  384.5 59.8 %collective-permute-start.32 = (bf16[288,2304]{1,0:T(8,128)(2,1)}, bf16[288,2304]{1,0:T(8,128)(2,1)}, u32[]{:S(2)}, u32[]{:S(2)}) collective-permute-start(bf16[288,2304]{1,0:T(8,128)(2,1)} %shard_map.279.refs_1_), channel_id=1, source_target_pairs={{0,1},{1,0},{2,3},{3,2},{4,5},{5,4},{6,7},{7,6},{8,9},{9,8},{10,11... | collective-permute-start | bytes 3981320 | tf_op jit(solution)/shard_map/ppermute | solution.py:46
  389.0 140.6 %reduce-scatter.9.cloned.1.call-start = ((), (), s32[]{:S(2)}) async-start(), calls=%async_computation.9 | async-start | bytes 3686400 | tf_op jit(solution)/shard_map/reduce_scatter | solution.py:78
  474.4 114.8 %reduce-scatter.11.cloned.1.call-start = ((), (), s32[]{:S(2)}) async-start(), calls=%async_computation.10 | async-start | bytes 3686400 | tf_op jit(solution)/shard_map/reduce_scatter | solution.py:78
  510.1 140.8 %all-gather.28.cloned.1.call-start = ((), (), s32[]{:S(2)}) async-start(), calls=%async_computation.22 | async-start | bytes 3686400 | tf_op jit(solution)/shard_map/all_gather | solution.py:55
  537.6 173.7 %all-gather.30.cloned.1.call-start = ((), (), s32[]{:S(2)}) async-start(), calls=%async_computation.23 | async-start | bytes 3686400 | tf_op jit(solution)/shard_map/all_gather | solution.py:55
  597.6 183.8 %reduce-scatter.13.cloned.1.call-start = ((), (), s32[]{:S(2)}) async-start(), calls=%async_computation.11 | async-start | bytes 3686400 | tf_op jit(solution)/shard_map/reduce_scatter | solution.py:78
  693.9 159.6 %reduce-scatter.15.cloned.1.call-start = ((), (), s32[]{:S(2)}) async-start(), calls=%async_computation.12 | async-start | bytes 3686400 | tf_op jit(solution)/shard_map/reduce_scatter | solution.py:78
  783.1 241.4 %reduce-scatter.17.cloned.1.call-start = ((), (), s32[]{:S(2)}) async-start(), calls=%async_computation.13 | async-start | bytes 3276800 | tf_op jit(solution)/shard_map/reduce_scatter | solution.py:78
  811.4 38.9 %collective-permute-start.41 = (bf16[2,144,2304]{2,1,0:T(8,128)(2,1)}, bf16[2,144,2304]{2,1,0:T(8,128)(2,1)S(1)}, u32[]{:S(2)}, u32[]{:S(2)}) collective-permute-start(bf16[2,144,2304]{2,1,0:T(8,128)(2,1)} %get-tuple-element.556), channel_id=1, source_target_pairs={{0,8},{8,0},{16,24},{24,16},{1,9},{9,1},{17,25},{25,17},{2,10},{10... | collective-permute-start | bytes 3981320 | tf_op jit(solution)/shard_map/ppermute | solution.py:42
  812.0 38.3 %collective-permute-start.42 = (bf16[2,144,2304]{2,1,0:T(8,128)(2,1)}, bf16[2,144,2304]{2,1,0:T(8,128)(2,1)S(1)}, u32[]{:S(2)}, u32[]{:S(2)}) collective-permute-start(bf16[2,144,2304]{2,1,0:T(8,128)(2,1)} %get-tuple-element.557), channel_id=1, source_target_pairs={{0,16},{8,24},{16,0},{24,8},{1,17},{9,25},{17,1},{25,9},{2,18},{10... | collective-permute-start | bytes 3981320 | tf_op jit(solution)/shard_map/ppermute | solution.py:42
  965.0 113.9 %reduce-scatter.19.cloned.1.call-start = ((), (), s32[]{:S(2)}) async-start(), calls=%async_computation.14 | async-start | bytes 3276800 | tf_op jit(solution)/shard_map/reduce_scatter | solution.py:78
  1024.5 177.8 %reduce-scatter.23.cloned.1.call-start = ((), (), s32[]{:S(2)}) async-start(), calls=%async_computation.16 | async-start | bytes 2654208 | tf_op jit(solution)/shard_map/reduce_scatter | solution.py:1165
  1079.0 144.8 %reduce-scatter.21.cloned.1.call-start = ((), (), s32[]{:S(2)}) async-start(), calls=%async_computation.15 | async-start | bytes 5308416 | tf_op jit(solution)/shard_map/reduce_scatter | solution.py:1178
  1079.2 83.4 %collective-permute-start.66 = (bf16[4,288,2304]{2,1,0:T(8,128)(2,1)}, bf16[4,288,2304]{2,1,0:T(8,128)(2,1)}, u32[]{:S(2)}, u32[]{:S(2)}) collective-permute-start(bf16[4,288,2304]{2,1,0:T(8,128)(2,1)} %get-tuple-element.689), channel_id=1, source_target_pairs={{0,1},{1,0},{2,3},{3,2},{4,5},{5,4},{6,7},{7,6},{8,9},{9,8},{10,11... | collective-permute-start | bytes 15925256 | tf_op jit(solution)/shard_map/ppermute | solution.py:46
  1110.0 46.8 %collective-permute-start.59 = (bf16[2,160,2304]{2,1,0:T(8,128)(2,1)}, bf16[2,160,2304]{2,1,0:T(8,128)(2,1)S(1)}, u32[]{:S(2)}, u32[]{:S(2)}) collective-permute-start(bf16[2,160,2304]{2,1,0:T(8,128)(2,1)} %get-tuple-element.677), channel_id=1, source_target_pairs={{0,8},{8,0},{16,24},{24,16},{1,9},{9,1},{17,25},{25,17},{2,10},{10... | collective-permute-start | bytes 4423688 | tf_op jit(solution)/shard_map/ppermute | solution.py:42
  1111.6 45.3 %collective-permute-start.60 = (bf16[2,160,2304]{2,1,0:T(8,128)(2,1)}, bf16[2,160,2304]{2,1,0:T(8,128)(2,1)S(1)}, u32[]{:S(2)}, u32[]{:S(2)}) collective-permute-start(bf16[2,160,2304]{2,1,0:T(8,128)(2,1)} %get-tuple-element.678), channel_id=1, source_target_pairs={{0,16},{8,24},{16,0},{24,8},{1,17},{9,25},{17,1},{25,9},{2,18},{10... | collective-permute-start | bytes 4423688 | tf_op jit(solution)/shard_map/ppermute | solution.py:42
  (208 other events, 2078.9 us)
Sparse Core Ops, SparseCore 0:
  29.2 92.9 all-gather.17
  147.3 59.6 all-gather.19
  208.6 53.5 all-gather.21
  270.0 33.3 all-gather.15
  349.9 57.8 all-gather.23
  409.2 58.9 all-gather.25
  474.5 55.0 reduce-scatter.8
  532.0 57.0 reduce-scatter.10
  590.8 60.1 all-gather.27
  652.4 58.9 all-gather.29
  713.7 55.8 reduce-scatter.12
  783.2 55.8 reduce-scatter.14
  965.1 59.2 reduce-scatter.16
  1027.2 51.7 reduce-scatter.18
  1081.7 36.3 reduce-scatter.22
  1120.3 68.3 reduce-scatter.20

commit v3 on v2

--- a/solution.py
+++ b/solution.py
@@ -309,38 +309,48 @@
     )(place, *lefts, *rights)
 
 
-def quad_terms(lefts, weight, part, turned):
+def quad_terms(lefts, weight, part, turned, sent):
     first, count = part.start, part.stop - part.start
     half = count // 2
     model = weight.shape[0] if turned else weight.shape[1]
-
-    def kernel(a_ref, b_ref, weight_ref, one_ref, two_ref, own_ref, low_ref, high_ref):
-        for k in range(4):
-            ref = (a_ref, b_ref)[k // 2]
-            rows = ref[k % 2, first : first + count, :]
-            product = matmul_t if turned else matmul
-            term = product(rows, weight_ref[...]).astype(jnp.bfloat16)
-            if k == 0:
-                own_ref[...] = term
-            if k % 2 == 1:
-                one_ref[k // 2] = term[:half]
-            if k == 2:
-                low_ref[...] = term[:half]
-            if k >= 2:
-                two_ref[k - 2] = term[half:]
-            if k == 1:
-                high_ref[...] = term[half:]
-
-    def shape(*lead):
-        return jax.ShapeDtypeStruct(lead + (model,), jnp.bfloat16)
-
-    one, two, own, low, high = pl.pallas_call(
+    if sent:
+        plan = [(1, 0, half, 0, 0), (3, 0, half, 0, 1), (2, half, half, 1, 0), (3, half, half, 1, 1)]
+        shapes = [(2, half, model), (2, half, model)]
+    else:
+        plan = [(0, 0, count, 0, None), (2, 0, half, 1, None), (1, half, half, 2, None)]
+        shapes = [(count, model), (half, model), (half, model)]
+    widths = [pair[0].shape[2] for pair in lefts]
+
+    def kernel(*refs):
+        weight_ref, scratch = refs[2 * len(lefts)], refs[-1]
+        out_refs = refs[2 * len(lefts) + 1 : -1]
+        row = 0
+        for k, start, size, _, _ in plan:
+            column = 0
+            for n, width in enumerate(widths):
+                ref = refs[2 * n + k // 2]
+                scratch[row : row + size, column : column + width] = ref[
+                    k % 2, first + start : first + start + size, :
+                ]
+                column += width
+            row += size
+        product = matmul_t if turned else matmul
+        term = product(scratch[...], weight_ref[...]).astype(jnp.bfloat16)
+        row = 0
+        for _, _, size, out, at in plan:
+            if at is None:
+                out_refs[out][...] = term[row : row + size]
+            else:
+                out_refs[out][at] = term[row : row + size]
+            row += size
+
+    return pl.pallas_call(
         kernel,
-        out_shape=[shape(2, half), shape(2, half), shape(count), shape(half), shape(half)],
+        out_shape=[jax.ShapeDtypeStruct(shape, jnp.bfloat16) for shape in shapes],
+        scratch_shapes=[pltpu.VMEM((2 * count, sum(widths)), jnp.bfloat16)],
         compiler_params=pltpu.CompilerParams(vmem_limit_bytes=VMEM_LIMIT),
-        cost_estimate=FREE,
-    )(*lefts, weight)
-    return (one, two), (own, low, high)
+        cost_estimate=cost(1),
+    )(*[x for pair in lefts for x in pair], weight)
 
 
 def split_columns(place, gate, up, dp, line):
@@ -369,9 +379,9 @@
     )(place, gate, up)
 
 
-def join_columns(place, parts, dp):
+def join_columns(place, parts, which, dp):
     line = len(parts)
-    rows, part = parts[0].shape
+    _, rows, part = parts[0].shape
     rest = part // dp
 
     def kernel(place_ref, *refs):
@@ -379,7 +389,7 @@
             for i in range(dp):
                 first = (i * line + j) * rest
                 refs[line][:, first : first + rest] = refs[k][
-                    :, i * rest : (i + 1) * rest
+                    0, :, i * rest : (i + 1) * rest
                 ].astype(jnp.float32)
 
         for j in range(line):
@@ -389,8 +399,12 @@
 
     return pl.pallas_call(
         kernel,
-        in_specs=[pl.BlockSpec(memory_space=pltpu.SMEM)]
-        + [pl.BlockSpec(memory_space=pltpu.VMEM)] * line,
+        grid_spec=pltpu.PrefetchScalarGridSpec(
+            num_scalar_prefetch=1,
+            grid=(1,),
+            in_specs=[pl.BlockSpec((1, rows, part), lambda i, place: (which, 0, 0))] * line,
+            out_specs=pl.BlockSpec((rows, line * part), lambda i, place: (0, 0)),
+        ),
         out_shape=jax.ShapeDtypeStruct((rows, line * part), jnp.float32),
         compiler_params=pltpu.CompilerParams(vmem_limit_bytes=VMEM_LIMIT),
         cost_estimate=FREE,
@@ -449,26 +463,28 @@
         ),
         out_shape=[jax.ShapeDtypeStruct(shape, jnp.bfloat16) for shape in shapes],
         compiler_params=pltpu.CompilerParams(vmem_limit_bytes=VMEM_LIMIT),
-        cost_estimate=cost(4),
+        cost_estimate=FREE,
     )(place, own, other)
 
 
-def to_line(place, kept, near, far, line):
-    count, columns = kept.shape
+def to_line(place, terms, line):
+    count, columns = terms[0][0].shape
     rows, half = count // line, count // 2
     alone = pl.BlockSpec((count, columns), lambda i, place: (0, 0))
     first = pl.BlockSpec((1, half, columns), lambda i, place: (0, 0, 0))
     last = pl.BlockSpec((half, columns), lambda i, place: (0, 0))
-    part = pl.BlockSpec((rows, columns), lambda i, place: (0, 0))
-
-    def kernel(place_ref, kept_ref, near_one, near_two, far_one, far_two, *out_refs):
+    part = pl.BlockSpec((len(terms), rows, columns), lambda i, place: (0, 0, 0))
+
+    def kernel(place_ref, *refs):
         def fill(j, k):
-            start = j * rows % half
-            near_ref, far_ref = ((near_one, far_one), (near_two, far_two))[j * rows // half]
-            total = kept_ref[j * rows : (j + 1) * rows].astype(jnp.float32)
-            total = total + near_ref[0, start : start + rows].astype(jnp.float32)
-            total = total + far_ref[start : start + rows].astype(jnp.float32)
-            out_refs[k][...] = total.astype(jnp.bfloat16)
+            start, high = j * rows % half, j * rows // half
+            for which in range(len(terms)):
+                kept_ref, *near_refs = refs[5 * which : 5 * which + 3]
+                far_ref = refs[5 * which + 3 + high]
+                total = kept_ref[j * rows : (j + 1) * rows].astype(jnp.float32)
+                total = total + near_refs[high][0, start : start + rows].astype(jnp.float32)
+                total = total + far_ref[start : start + rows].astype(jnp.float32)
+                refs[5 * len(terms) + k][which] = total.astype(jnp.bfloat16)
 
         for j in range(line):
             for k in range(line):
@@ -480,49 +496,55 @@
         grid_spec=pltpu.PrefetchScalarGridSpec(
             num_scalar_prefetch=1,
             grid=(1,),
-            in_specs=[alone, first, first, last, last],
+            in_specs=[alone, first, first, last, last] * len(terms),
             out_specs=[part] * line,
         ),
-        out_shape=[jax.ShapeDtypeStruct((rows, columns), jnp.bfloat16)] * line,
+        out_shape=[jax.ShapeDtypeStruct((len(terms), rows, columns), jnp.bfloat16)] * line,
         compiler_params=pltpu.CompilerParams(vmem_limit_bytes=VMEM_LIMIT),
         cost_estimate=FREE,
-    )(place, kept, *near, *far)
+    )(place, *[x for kept, near, far in terms for x in (kept, *near, *far)])
 
 
 def input_terms(lefts, rights, dp, seq):
     count, model = lefts[0].shape
-    columns = rights[0].shape[1]
+    widths = [pair[0].shape[1] for pair in rights]
     rest = model // (dp * seq)
-    block, strip = model // 2, math.gcd(columns, 256)
+    block, strip = model // 2, math.gcd(*widths, 256)
     halves = dp // 2
 
-    def kernel(left_a, left_b, right_a, right_b, out_ref, turned):
+    def kernel(left_a, left_b, *refs):
+        out_ref, turned = refs[-2:]
         turned[:, :count] = left_a[...].T
         turned[:, count:] = left_b[...].T
-
-        def body(n, carry):
-            at = pl.ds(pl.multiple_of(n * strip, strip), strip)
-            term = matmul(turned[:, :count], right_a[:, at])
-            term = (term + matmul(turned[:, count:], right_b[:, at])).astype(jnp.bfloat16)
-            term = term.reshape(halves, seq, rest, strip)
-            for i in range(halves):
-                out_ref[:, i, :, at] = term[i]
-            return carry
-
-        lax.fori_loop(0, columns // strip, body, 0)
+        column = 0
+        for n, width in enumerate(widths):
+
+            def body(m, carry, right_a=refs[2 * n], right_b=refs[2 * n + 1], column=column):
+                at = pl.ds(pl.multiple_of(m * strip, strip), strip)
+                to = pl.ds(pl.multiple_of(column + m * strip, strip), strip)
+                term = matmul(turned[:, :count], right_a[:, at])
+                term = (term + matmul(turned[:, count:], right_b[:, at])).astype(jnp.bfloat16)
+                term = term.reshape(halves, seq, rest, strip)
+                for i in range(halves):
+                    out_ref[:, i, :, to] = term[i]
+                return carry
+
+            lax.fori_loop(0, width // strip, body, 0)
+            column += width
 
     left_spec = pl.BlockSpec((count, block), lambda i: (0, i))
-    right_spec = pl.BlockSpec((count, columns), lambda i: (0, 0))
+    columns = sum(widths)
     return pl.pallas_call(
         kernel,
         grid=(2,),
-        in_specs=[left_spec] * 2 + [right_spec] * 2,
+        in_specs=[left_spec] * 2
+        + [pl.BlockSpec((count, width), lambda i: (0, 0)) for width in widths for _ in (0, 1)],
         out_specs=pl.BlockSpec((seq, halves, rest, columns), lambda i: (0, i, 0, 0)),
         out_shape=jax.ShapeDtypeStruct((seq, dp, rest, columns), jnp.bfloat16),
         scratch_shapes=[pltpu.VMEM((block, 2 * count), jnp.bfloat16)],
         compiler_params=pltpu.CompilerParams(vmem_limit_bytes=VMEM_LIMIT),
         cost_estimate=cost(6),
-    )(*lefts, *rights)
+    )(*lefts, *[x for pair in rights for x in pair])
 
 
 def tile_facts(place, span, tile):
@@ -744,7 +766,7 @@
             jax.ShapeDtypeStruct(own.shape, jnp.bfloat16),
         ],
         compiler_params=pltpu.CompilerParams(vmem_limit_bytes=VMEM_LIMIT),
-        cost_estimate=cost(12),
+        cost_estimate=cost(6),
     )(place, queries, grads, attended, own, other, codes, logs, segments)
 
 
@@ -864,18 +886,19 @@
     codes, own_segments = attention_codes()
     row_codes = codes[:, :, :, None, :]
     column_segments = own_segments[..., None]
-    near_normed, in_weight, split, row_codes, column_segments = order(
-        near_normed, in_weight, split, row_codes, column_segments
-    )
-    far_normed = gather_quad_far_parts(*near_normed)
     first_rows = jnp.concatenate([normed_in, near_normed[0]], axis=0)
+    halfway = span // 2
+    far_normed = near_normed[1][:halfway], near_normed[0][halfway:]
+    near_two, far_normed, first_rows, in_weight, split, row_codes, column_segments = order(
+        near_normed[1], far_normed, first_rows, in_weight, split, row_codes, column_segments
+    )
+    far_normed = across(far_normed[0], 1), across(far_normed[1], 2)
     first_queries, first_keys = project(first_rows)
-    first_queries, first_keys, first_rows, far_normed = order(
-        first_queries, first_keys, first_rows, far_normed
-    )
+    first_queries, first_keys, first_rows = order(first_queries, first_keys, first_rows)
     first_own = gather_line(first_keys)
     gate_up = ordered_split(split)
-    second_rows = jnp.concatenate([near_normed[1], *far_normed], axis=0)
+    far_normed, gate_up = order(far_normed, gate_up)
+    second_rows = jnp.concatenate([near_two, *far_normed], axis=0)
     second_queries, second_keys = project(second_rows)
     second_queries, second_keys, second_rows, gate_up = order(
         second_queries, second_keys, second_rows, gate_up
@@ -884,14 +907,7 @@
     normed_rows = [first_rows, second_rows]
     near_in = near_blocks(gate_up)
     swapped = swap_all([gate_up] if quad else [])
-    column_codes = [codes[pair][..., None] for pair in (0, 1)]
-    lane_segments = jnp.broadcast_to(
-        own_segments[:, :, None, None, :], (2, 2, 8, GROUP, span)
-    ).reshape(2, 2, 8, GROUP * span)
-    lane_segments = [lane_segments[0], lane_segments[1]]
-    swapped, first_own, column_codes, lane_segments = order(
-        swapped, first_own, column_codes, lane_segments
-    )
+    swapped, first_own = order(swapped, first_own)
     first_other = order(swap_core(first_own))
     attended, log_total = [None, None], [None, None]
     attended[0], log_total[0] = attention_forward(
@@ -936,16 +952,18 @@
         residual = inputs[part] + normed(attn_out, post_attention)
         return attn_out, residual, normed(residual, pre_feedforward).astype(bf16)
 
-    sent_a, kept_a = order(quad_terms(attended, out_weight, chunks[0], False))
+    sent_a = order(quad_terms([attended], out_weight, chunks[0], False, True))
     near_a = scatter_quad_near(sent_a)
-    sent_b, kept_b = quad_terms(attended, out_weight, chunks[1], False)
-    near_a, sent_b, kept_b = order(near_a, sent_b, kept_b)
+    kept_a = quad_terms([attended], out_weight, chunks[0], False, False)
+    near_a, kept_a = order(near_a, kept_a)
     far_a = scatter_quad_far(kept_a, near_a)
+    sent_b = quad_terms([attended], out_weight, chunks[1], False, True)
     far_a, sent_b = order(far_a, sent_b)
     near_b = scatter_quad_near(sent_b)
     attn_out_a, residual_a, mid_a = order(into_feedforward(chunks[0], kept_a, near_a, far_a))
     mid_rows_a = gather_line(mid_a).reshape(line * step, model)
-    near_b = order(near_b)
+    kept_b = quad_terms([attended], out_weight, chunks[1], False, False)
+    near_b, kept_b = order(near_b, kept_b)
     far_b = order(scatter_quad_far(kept_b, near_b))
     attn_out_b, residual_b, mid_b = order(into_feedforward(chunks[1], kept_b, near_b, far_b))
     mid_rows_b = gather_line(mid_b).reshape(line * step, model)
@@ -961,17 +979,15 @@
     down_blocks = ([own_down] if quad else []) + list(near_down)
     swapped = swap_all(down_blocks)
     up_a = matmul(mid_rows_a, up_weight)
-    gate_a, up_a, far_down, swapped = order(gate_a, up_a, far_down, swapped)
+    hidden_a, far_down, swapped = order(activation(gate_a, up_a).astype(bf16), far_down, swapped)
     down_weight = fill_down(down_weight, range(3), down_blocks, swapped)
     swapped = swap_all(far_down)
     down_weight, swapped = order(down_weight, swapped)
     down_weight = fill_down(down_weight, (3,), far_down, swapped)
     down_weight = down_weight.reshape(ff_part, model)
 
-    def feedforward(gate_value, up_value):
-        hidden = activation(gate_value, up_value).astype(bf16)
-        down_part = matmul(hidden, down_weight).astype(bf16).reshape(line, step, model)
-        return gate_value, up_value, hidden, down_part
+    def feedforward_end(hidden):
+        return matmul(hidden, down_weight).astype(bf16).reshape(line, step, model)
 
     def output_of(part, residual, down_out):
         down_out = down_out.astype(f32)
@@ -995,17 +1011,21 @@
         grad_attn, grad_post = attn_back(grad_residual)
         return grad_residual, grad_attn.astype(bf16), grad_pre, grad_post
 
-    gate_a, up_a, hidden_a, down_a = order(feedforward(gate_a, up_a))
-    down_a = scatter_line(down_a)
+    down_a = scatter_line(order(feedforward_end(hidden_a)))
     mid_rows_b = order(mid_rows_b)
-    gate_b, up_b, hidden_b, down_b = order(
-        feedforward(matmul(mid_rows_b, gate_weight), matmul(mid_rows_b, up_weight))
-    )
+    gate_b, up_b = matmul(mid_rows_b, gate_weight), matmul(mid_rows_b, up_weight)
+    hidden_b = activation(gate_b, up_b).astype(bf16)
+    down_b = order(feedforward_end(hidden_b))
     down_b = scatter_line(down_b)
     down_a = order(down_a)
     result_a, grad_down_a, post_ff_a = order(output_of(chunks[0], residual_a, down_a))
     down_rows_a = gather_line(grad_down_a).reshape(line * step, model)
-    down_b = order(down_b)
+    column_codes = [codes[pair][..., None] for pair in (0, 1)]
+    lane_segments = jnp.broadcast_to(
+        own_segments[:, :, None, None, :], (2, 2, 8, GROUP, span)
+    ).reshape(2, 2, 8, GROUP * span)
+    lane_segments = [lane_segments[0], lane_segments[1]]
+    down_b, column_codes, lane_segments = order(down_b, column_codes, lane_segments)
     result_b, grad_down_b, post_ff_b = order(output_of(chunks[1], residual_b, down_b))
     down_rows_b = gather_line(grad_down_b).reshape(line * step, model)
     down_rows_a = order(down_rows_a)
@@ -1048,16 +1068,21 @@
     def near_sums(sent):
         return scatter_quad_near(sent) if quad else ()
 
-    def far_sums(kept, near):
-        if not quad:
-            return ()
-        return across(add_second(kept[1], near[0]), 2), across(add_second(kept[2], near[1]), 1)
-
-    def line_parts(sent, kept, near, far):
+    def far_terms(kept, near):
+        return (add_second(kept[1], near[0]), add_second(kept[2], near[1])) if quad else ()
+
+    def far_sums(terms):
+        return (across(terms[0], 2), across(terms[1], 1)) if quad else ()
+
+    def line_parts(*terms):
         if quad:
-            return to_line(place, kept[0], near, far, line)
-        total = lax.psum_scatter(sent, "dp", scatter_dimension=0).reshape(line, rows, ff_part)
-        return [pick(total, 0, (line_at + k) % line) for k in range(line)]
+            return to_line(place, [(kept[0], near, far) for _, kept, near, far in terms], line)
+        totals = [
+            lax.psum_scatter(sent, "dp", scatter_dimension=0).reshape(line, rows, ff_part)
+            for sent, _, _, _ in terms
+        ]
+        totals = jnp.stack(totals, axis=1)
+        return [pick(totals, 0, (line_at + k) % line) for k in range(line)]
 
     mid_rows, hiddens, down_rows = (mid_rows_a, mid_rows_b), (hidden_a, hidden_b), (
         down_rows_a, down_rows_b
@@ -1073,25 +1098,25 @@
         grad_residual_a, grad_attn, pre_ff_a, post_attn_a, gate_other
     )
     near_a = gather_quad_near(grad_attn)
-    gate_sent, gate_kept = combine(gate_own, gate_other, per_device)
-    near_a, gate_sent, gate_kept, mid_rows, grad_ups = order(
-        near_a, gate_sent, gate_kept, mid_rows, grad_ups
-    )
-    far_a = gather_quad_far_parts(*near_a)
+    gate_sent, gate_kept, near_a, mid_rows, grad_ups = order(
+        *combine(gate_own, gate_other, per_device), near_a, mid_rows, grad_ups
+    )
     gate_near = near_sums(gate_sent)
     up_own, up_other = halves(mid_rows, grad_ups, rows)
-    far_a, gate_near, up_own, up_other = order(far_a, gate_near, up_own, up_other)
-    quad_a = [grad_attn, *near_a, jnp.concatenate(far_a, axis=0)]
-    gate_far = far_sums(gate_kept, gate_near)
+    up_own, up_other, gate_near, grad_mid_b = order(up_own, up_other, gate_near, grad_mid_b)
     up_other = swap_core(up_other)
-    grad_mid_b = order(grad_mid_b)
-    grad_residual_b, grad_attn, pre_ff_b, post_attn_b = order(
-        attention_grad(chunks[1], residual_b, attn_out_b, grad_mid_b)
-    )
+    gate_far = far_terms(gate_kept, gate_near)
+    attn_grads, gate_far, up_other, up_own = order(
+        attention_grad(chunks[1], residual_b, attn_out_b, grad_mid_b), gate_far, up_other, up_own
+    )
+    quad_a = [grad_attn, *near_a]
+    grad_residual_b, grad_attn, pre_ff_b, post_attn_b = attn_grads
     near_b = gather_quad_near(grad_attn)
+    gate_far = far_sums(gate_far)
     up_sent, up_kept = combine(up_own, up_other, per_device)
-    near_b, up_sent, up_kept, gate_far, quad_a = order(near_b, up_sent, up_kept, gate_far, quad_a)
+    near_b, up_sent, up_kept, near_a = order(near_b, up_sent, up_kept, near_a)
     far_b = gather_quad_far_parts(*near_b)
+    far_a = gather_quad_far_parts(*near_a)
     grad_residual = jnp.concatenate([grad_residual_a, grad_residual_b], axis=0)
 
     def attention_rows(blocks_a, blocks_b):
@@ -1108,59 +1133,59 @@
             column_codes[pair], log_total[pair], lane_segments[pair],
         )
 
-    def owned_gains(terms):
+    def gains_over_dp(terms):
         terms = jnp.stack(terms, axis=1)
-        count = terms.shape[1]
         if not quad:
             return lax.psum_scatter(terms, ("dp", "seq"), scatter_dimension=0, tiled=True)
-        terms = terms.reshape(dp, line, 2, rows * count)
-        terms = sum(
-            (across(pick(terms, 0, head ^ k), k) for k in (1, 2, 3)), pick(terms, 0, head)
-        )
+        terms = terms.reshape(dp, line, 2, -1)
+        return [pick(terms, 0, head)] + [across(pick(terms, 0, head ^ k), k) for k in (1, 2, 3)]
+
+    def gains_over_seq(terms):
+        if not quad:
+            return terms
+        terms = sum(terms)
         terms = pick(terms, 1, core) + swap_core(pick(terms, 1, 1 - core))
-        return jnp.sum(exchange_line(terms, line_at), axis=0).reshape(rows, count)
-
-    def project_back(grad_queries, key_grads):
-        grad_projected = jnp.concatenate([grad_queries, key_grads], axis=2)
-        return grad_projected, grad_projected.reshape(2 * span, 2 * width)
+        return jnp.sum(exchange_line(terms, line_at), axis=0).reshape(rows, -1)
 
     first_attn = attention_rows(quad_a[:2], [grad_attn, near_b[0]])
-    gate_line = line_parts(gate_sent, gate_kept, gate_near, gate_far)
-    far_b, grad_attended, gate_line = order(far_b, attended_grad(first_attn), gate_line)
+    grad_attended, gate_far, far_a = order(attended_grad(first_attn), gate_far, far_a)
+    gate_line = order(line_parts((gate_sent, gate_kept, gate_near, gate_far)))
     gate_line = exchange_line_parts(gate_line)
+    first_grads, own_grad, other_grad, far_b, gate_line, up_sent = order(
+        *attend_back(0, grad_attended), far_b, gate_line, up_sent
+    )
     up_near = near_sums(up_sent)
-    first_grads, own_grad, other_grad, far_b, gate_line = order(
-        *attend_back(0, grad_attended), far_b, gate_line
-    )
     swapped = swap_core(other_grad)
-    second_attn = attention_rows(quad_a[2:], [near_b[1], jnp.concatenate(far_b, axis=0)])
+    second_attn = attention_rows(
+        [quad_a[2], jnp.concatenate(far_a, axis=0)], [near_b[1], jnp.concatenate(far_b, axis=0)]
+    )
     grad_attended = attended_grad(second_attn)
     swapped, grad_attended = order(swapped, grad_attended)
-    first_key_grads, up_near = order(own_grad + swapped, up_near)
+    first_key_grads = order(own_grad + swapped)
     first_key_grads = scatter_line(first_key_grads)
-    up_far = far_sums(up_kept, up_near)
-    second_grads, own_grad, other_grad, up_far = order(*attend_back(1, grad_attended), up_far)
+    second_grads, own_grad, other_grad, up_near = order(*attend_back(1, grad_attended), up_near)
     swapped = swap_core(other_grad)
-    up_line = line_parts(up_sent, up_kept, up_near, up_far)
-    swapped, up_line = order(swapped, up_line)
+    up_far = far_terms(up_kept, up_near)
+    swapped, up_far = order(swapped, up_far)
     second_key_grads, first_key_grads, hiddens, down_rows = order(
         own_grad + swapped, first_key_grads, hiddens, down_rows
     )
     second_key_grads = scatter_line(second_key_grads)
 
+    up_far = far_sums(up_far)
     down_own, down_other = halves(hiddens, down_rows, ff_rows)
     output_term = inner_t(attended[0].reshape(2 * span, width), first_attn)
     output_term += inner_t(attended[1].reshape(2 * span, width), second_attn)
     output_term = output_term.astype(bf16)
-    second_key_grads, up_line, down_own, down_other, output_term = order(
-        second_key_grads, up_line, down_own, down_other, output_term
-    )
-
-    first_grad, first_rows = project_back(first_grads, first_key_grads)
-    second_grad, second_rows = project_back(second_grads, second_key_grads)
-    sent, kept = quad_terms((first_grad, second_grad), in_weight, slice(0, span), True)
-    sent, kept, first_rows, second_rows = order(sent, kept, first_rows, second_rows)
+    up_line = line_parts((up_sent, up_kept, up_near, up_far))
+    second_key_grads, down_own, down_other, output_term, up_line = order(
+        second_key_grads, down_own, down_other, output_term, up_line
+    )
+
+    grads = [(first_grads, second_grads), (first_key_grads, second_key_grads)]
+    sent, grads = order(quad_terms(grads, in_weight, slice(0, span), True, True), grads)
     near = scatter_quad_near(sent)
+    kept = quad_terms(grads, in_weight, slice(0, span), True, False)
     if quad:
         output_shard = lax.psum_scatter(output_term, "seq", scatter_dimension=0, tiled=True)
     else:
@@ -1174,17 +1199,23 @@
     up_line = exchange_line_parts(up_line)
     down_other = swap_core(down_other)
     if quad:
-        in_term = order(input_terms(normed_rows, (first_rows, second_rows), dp, seq))
+        flat = [[x.reshape(2 * span, width) for x in pair] for pair in grads]
+        in_term = input_terms(normed_rows, flat, dp, seq)
+        down_sent, down_kept = combine(down_own, down_other, ff_rows)
+        near, kept, in_term, down_sent, down_kept, up_line = order(
+            near, kept, in_term, down_sent, down_kept, up_line
+        )
+        far = scatter_quad_far(kept, near)
         in_part = lax.psum_scatter(
             in_term.reshape(model, 2 * width), "seq", scatter_dimension=0, tiled=True
         )
-        near, up_line = order(near, up_line)
-        far = scatter_quad_far(kept, near)
-        down_sent, down_kept = combine(down_own, down_other, ff_rows)
-        far, down_sent, down_kept = order(far, down_sent, down_kept)
+        far, down_sent = order(far, down_sent)
         down_near = scatter_quad_near(down_sent)
     else:
-        in_term = inner_t(normed_rows[0], first_rows) + inner_t(normed_rows[1], second_rows)
+        in_term = sum(
+            inner_t(left, jnp.concatenate(right, axis=2).reshape(2 * span, 2 * width))
+            for left, right in zip(normed_rows, zip(*grads))
+        )
         near, in_term = order(near, in_term.astype(bf16))
         far = order(scatter_quad_far(kept, near))
         down_mine, _ = combine(down_own, down_other, ff_rows)
@@ -1193,18 +1224,20 @@
     _, in_back = jax.vjp(normed, inputs, pre_attention)
     grad_inputs, grad_pre_attn = in_back(grad_in)
     grad_pre_attn, grad_inputs = order(grad_pre_attn, grad_inputs)
-    gains = owned_gains(
+    gains = gains_over_dp(
         [grad_pre_attn, post_attn_a + post_attn_b, pre_ff_a + pre_ff_b, post_ff_a + post_ff_b]
     )
     tokens_grad = grad_residual + grad_inputs
     if quad:
-        gains, down_near, in_part = order(gains, down_near, in_part)
+        gains, down_near = order(gains, down_near)
         down_far = scatter_quad_far(down_kept, down_near)
+        in_part = order(in_part)
+        part_shard = exchange_quad(in_part.reshape(dp, rows, 2 * width), head)
+        part_shard, down_far = order(part_shard, down_far)
         down_shard = scatter_quad_end(down_kept, down_near, down_far)
-    gate_shard, up_shard = join_columns(place, gate_line, dp), join_columns(place, up_line, dp)
-    if quad:
-        part_shard = exchange_quad(in_part.reshape(dp, rows, 2 * width), head)
-    else:
+    gains = gains_over_seq(gains)
+    gate_shard, up_shard = (join_columns(place, x, 0, dp) for x in (gate_line, up_line))
+    if not quad:
         spread = jnp.zeros((KEY_VALUE_HEADS, model, 2 * width), bf16).at[head].set(in_term)
         part_shard = lax.psum_scatter(spread, ("dp", "seq"), scatter_dimension=1, tiled=True)
     part_shard = part_shard.astype(f32).transpose(1, 0, 2)

time: 1280 us -> 1220 us (0.953)
  waiting for transfers between devices: 522 us -> 440 us
  Pallas kernels: 274 us -> 287 us
    ppermute x12, waiting for transfers between devices: 112 us -> 43.7 us  [exchange_line_parts(): lax.ppermute(parts[k], 'seq', line_route(line, k))]
    reduce_scatter x6, waiting for transfers between devices: 108 us -> 78.8 us  [scatter_line(): lax.psum_scatter(x, 'seq', scatter_dimension=0, axis_index_groups=line_gr...]
    ppermute x53, waiting for transfers between devices: 145 us -> 159 us  [across(): lax.ppermute(x, 'dp', [(i, i ^ bits) for i in range(lax.axis_size('dp'))])]
    pallas_call x6 -> x9, Pallas kernels: 43.1 us -> 54.9 us  [the longest x6 32.4 us: quad_terms(): pl.pallas_call(kernel, out_shape=[jax.ShapeDtypeStruct(shape, jnp.bfloat1...]
    unnamed x304 -> x299, local copies, waits for them, and re-layouts: 44.9 us -> 42.6 us
  transfers between devices with their start and end apart: 97 -> 97, of which waited for: 46 -> 52; matrix products, arithmetic and copies ran while one was open for 24% -> 26% of each run, Pallas kernels for 21% -> 23%
where the time goes in v3:
time: 1220 us; the launch traced here: 1210 us
  waiting for transfers between devices  440 us (36%)
  Pallas kernels  287 us (24%)
  matrix products  191 us (16%)
  starting transfers between devices  96.7 us (8%)
  other arithmetic  90.5 us (7%)
  local copies, waits for them, and re-layouts  86.5 us (7%)
  between operations  15.7 us (1%)
    ppermute x53, waiting for transfers between devices, across(): lax.ppermute(x, 'dp', [(i, i ^ bits) for i in range(lax.axis_size('dp'))])  159 us
    all_gather x6, waiting for transfers between devices, gather_line(): return lax.all_gather(x, 'seq', axis=0, axis_index_groups=line_groups())  122 us
    dot_general x8, matrix products, matmul_t(): lax.dot_general(a, b, (((1,), (1,)), ((), ())), preferred_element_type=jn...  94.8 us
    dot_general x8, matrix products, matmul(): return jnp.dot(a, b, preferred_element_type=jnp.float32)  88.3 us
    pallas_call x3, Pallas kernels, weight_halves(): pl.pallas_call(kernel, grid=(model // block,), in_specs=[pl.BlockSpec(mem...  81.1 us
    reduce_scatter x6, waiting for transfers between devices, scatter_line(): lax.psum_scatter(x, 'seq', scatter_dimension=0, axis_index_groups=line_gr...  78.8 us
    ppermute x53, starting transfers between devices, across(): lax.ppermute(x, 'dp', [(i, i ^ bits) for i in range(lax.axis_size('dp'))])  62.9 us
    ppermute x12, waiting for transfers between devices, exchange_line_parts(): lax.ppermute(parts[k], 'seq', line_route(line, k))  43.7 us
  transfers between devices with their start and end apart: 97, of which 52 were waited for; matrix products, arithmetic and copies ran while one was open for 26% of the time, Pallas kernels for 23%

profile of v3, /device:TPU:0, one launch (start us, length us, event | category | flops | bytes accessed | tf_op | source)
XLA Modules:
  0.0 1206.9 jit_solution(7323464734332766614)
XLA Ops:
  40.4 23.8 %collective-permute-done.3.refs_1_ = bf16[320,2304]{1,0:T(8,128)(2,1)S(1)} collective-permute-done((bf16[320,2304]{1,0:T(8,128)(2,1)}, bf16[320,2304]{1,0:T(8,128)(2,1)S(1)}, u32[]{:S(2)}, u32[]{:S(2)}) %collective-permute-start.3) | collective-permute-done | bytes 1474592 | tf_op jit(solution)/shard_map/ppermute | solution.py:42
  70.4 39.7 %collective-permute-done.6.refs_8_ = bf16[2,72,2304]{2,1,0:T(8,128)(2,1)} collective-permute-done((bf16[2,72,2304]{2,1,0:T(8,128)(2,1)}, bf16[2,72,2304]{2,1,0:T(8,128)(2,1)}, u32[]{:S(2)}, u32[]{:S(2)}) %collective-permute-start.6) | collective-permute-done | bytes 663584 | tf_op jit(solution)/shard_map/ppermute | solution.py:66
  158.6 34.9 %all-gather.20.cloned.1.call-done = bf16[8,320,512]{2,1,0:T(8,128)(2,1)} async-done(((bf16[2,320,512]{2,1,0:T(8,128)(2,1)}), bf16[8,320,512]{2,1,0:T(8,128)(2,1)}) %all-gather.20.cloned.1.call-update) | async-done | bytes 2621456 | tf_op jit(solution)/shard_map/all_gather | solution.py:55
  202.5 11.4 shard_map.259
  220.5 28.5 %collective-permute-done.16 = bf16[288,2304]{1,0:T(8,128)(2,1)S(1)} collective-permute-done((bf16[288,2304]{1,0:T(8,128)(2,1)S(1)}, bf16[288,2304]{1,0:T(8,128)(2,1)S(1)}, u32[]{:S(2)}, u32[]{:S(2)}) %collective-permute-start.16) | collective-permute-done | bytes 1327136 | tf_op jit(solution)/shard_map/ppermute | solution.py:42
  265.7 11.6 shard_map.266
  277.3 13.7 %all-gather.16.cloned.1.call-done.refs_5_ = bf16[512,2304]{1,0:T(8,128)(2,1)} async-done(((bf16[64,2304]{1,0:T(8,128)(2,1)}), bf16[512,2304]{1,0:T(8,128)(2,1)}) %all-gather.16.cloned.1.call-update) | async-done | bytes 2359312 | tf_op jit(solution)/shard_map/all_gather | solution.py:926
  302.2 11.8 collective-permute-done.20.refs_1_
  356.2 11.4 shard_map.280
  377.5 17.1 %all-gather.24.cloned.1.call-done.refs_1_ = bf16[640,2304]{1,0:T(8,128)(2,1)} async-done(((bf16[160,2304]{1,0:T(8,128)(2,1)}), bf16[640,2304]{1,0:T(8,128)(2,1)}) %all-gather.24.cloned.1.call-update) | async-done | bytes 2949136 | tf_op jit(solution)/shard_map/all_gather | solution.py:55
  394.7 13.3 %fusion.72.refs_1_ = f32[640,2304]{1,0:T(8,128)} fusion(bf16[640,2304]{1,0:T(8,128)(2,1)} %get-tuple-element.491.refs_2_, bf16[2304,2304]{1,0:T(8,128)(2,1)} %bitcast.227), kind=kOutput, calls=%fused_computation.235 | convolution fusion | flops 6794772480 | bytes 19464192 | tf_op jit(solution)/shard_map/dot_general | solution.py:30
  414.9 14.8 %multiply_convert_fusion.3 = (bf16[640,2304]{1,0:T(8,128)(2,1)}, f32[640,2304]{1,0:T(8,128)}) fusion(f32[640,2304]{1,0:T(8,128)} %get-tuple-element.494, bf16[640,2304]{1,0:T(8,128)(2,1)} %get-tuple-element.495.left_a.refs_8_, bf16[2304,2304]{1,0:T(8,128)(2,1)} %bitcast.233), kind=kOutput, calls=%fused_computation.23 | convolution fusion | flops 6809518080 | bytes 28311552 | tf_op jit(solution)/shard_map/dot_general | solution.py:30
  443.7 12.4 %convolution_convert_fusion.1 = bf16[640,2304]{1,0:T(8,128)(2,1)} fusion(bf16[640,2304]{1,0:T(8,128)(2,1)S(1)} %copy-done.19, bf16[2304,2304]{1,0:T(8,128)(2,1)} %bitcast.241), kind=kOutput, calls=%fused_computation.28 | convolution fusion | flops 6796247040 | bytes 16515072 | tf_op jit(solution)/shard_map/dot_general | solution.py:30
  456.4 13.5 %fusion.73 = f32[640,2304]{1,0:T(8,128)} fusion(bf16[640,2304]{1,0:T(8,128)(2,1)} %get-tuple-element.511.left_b.refs_9_, bf16[2304,2304]{1,0:T(8,128)(2,1)} %bitcast.228), kind=kOutput, calls=%fused_computation.236 | convolution fusion | flops 6794772480 | bytes 19464192 | tf_op jit(solution)/shard_map/dot_general | solution.py:30
  469.9 11.4 multiply_convert_fusion.2
  494.2 19.0 %reduce-scatter.9.cloned.1.call-done = bf16[1,160,2304]{2,1,0:T(8,128)(2,1)} async-done(((bf16[4,160,2304]{2,1,0:T(8,128)(2,1)}), bf16[1,160,2304]{2,1,0:T(8,128)(2,1)}) %reduce-scatter.9.cloned.1.call-update) | async-done | bytes 737296 | tf_op jit(solution)/shard_map/reduce_scatter | solution.py:78
  531.5 41.3 %reduce-scatter.11.cloned.1.call-done = bf16[1,160,2304]{2,1,0:T(8,128)(2,1)} async-done(((bf16[4,160,2304]{2,1,0:T(8,128)(2,1)}), bf16[1,160,2304]{2,1,0:T(8,128)(2,1)}) %reduce-scatter.11.cloned.1.call-update) | async-done | bytes 737296 | tf_op jit(solution)/shard_map/reduce_scatter | solution.py:78
  581.7 52.9 %all-gather.28.cloned.1.call-done.refs_1_ = bf16[640,2304]{1,0:T(8,128)(2,1)} async-done(((bf16[160,2304]{1,0:T(8,128)(2,1)}), bf16[640,2304]{1,0:T(8,128)(2,1)}) %all-gather.28.cloned.1.call-update) | async-done | bytes 2949136 | tf_op jit(solution)/shard_map/all_gather | solution.py:55
  634.6 18.9 %multiply_convert_fusion.1 = (bf16[640,2304]{1,0:T(8,128)(2,1)}, bf16[640,2304]{1,0:T(8,128)(2,1)}) fusion(f32[640,2304]{1,0:T(8,128)} %get-tuple-element.494, f32[640,2304]{1,0:T(8,128)} %get-tuple-element.813, bf16[640,2304]{1,0:T(8,128)(2,1)} %get-tuple-element.527.refs_5_, bf16[2304,2304]{1,0:T(8,128)(2,1)} %bitcast.242), kind=kOutput, calls=%fused_computation.21 | convolution fusion | flops 6830161920 | bytes 31260672 | tf_op jit(solution)/shard_map/dot_general | solution.py:34
  663.8 13.8 %add_convert_fusion.1 = bf16[640,2304]{1,0:T(8,128)(2,1)} fusion(f32[640,2304]{1,0:T(8,128)} %fusion.74, bf16[640,2304]{1,0:T(8,128)(2,1)} %get-tuple-element.767.refs_1_, bf16[2304,2304]{1,0:T(8,128)(2,1)} %bitcast.229), kind=kOutput, calls=%fused_computation.20 | convolution fusion | flops 6797721600 | bytes 22413312 | tf_op jit(solution)/shard_map/dot_general | solution.py:34
  678.1 16.9 %all-gather.30.cloned.1.call-done.refs_1_ = bf16[640,2304]{1,0:T(8,128)(2,1)} async-done(((bf16[160,2304]{1,0:T(8,128)(2,1)}), bf16[640,2304]{1,0:T(8,128)(2,1)}) %all-gather.30.cloned.1.call-update) | async-done | bytes 2949136 | tf_op jit(solution)/shard_map/all_gather | solution.py:55
  695.0 18.9 %multiply_convert_fusion = (bf16[640,2304]{1,0:T(8,128)(2,1)}, bf16[640,2304]{1,0:T(8,128)(2,1)}) fusion(f32[640,2304]{1,0:T(8,128)} %fusion.73, f32[640,2304]{1,0:T(8,128)} %get-tuple-element.815, bf16[640,2304]{1,0:T(8,128)(2,1)} %get-tuple-element.531.refs_6_, bf16[2304,2304]{1,0:T(8,128)(2,1)} %bitcast.243), kind=kOutput, calls=%fused_computation.19 | convolution fusion | flops 6830161920 | bytes 31260672 | tf_op jit(solution)/shard_map/dot_general | solution.py:34
  724.2 13.8 %add_convert_fusion = bf16[640,2304]{1,0:T(8,128)(2,1)} fusion(f32[640,2304]{1,0:T(8,128)} %fusion.75, bf16[640,2304]{1,0:T(8,128)(2,1)} %get-tuple-element.764.refs_2_, bf16[2304,2304]{1,0:T(8,128)(2,1)} %bitcast.234), kind=kOutput, calls=%fused_computation.18 | convolution fusion | flops 6797721600 | bytes 22413312 | tf_op jit(solution)/shard_map/dot_general | solution.py:34
  738.0 27.0 %shard_map.300 = (bf16[16,72,2304]{2,1,0:T(8,128)(2,1)}, bf16[16,72,2304]{2,1,0:T(8,128)(2,1)}) custom-call(s32[4]{0:T(128)} %get-tuple-element.383.place_ref.place, bf16[640,2304]{1,0:T(8,128)(2,1)} %get-tuple-element.495.left_a.refs_8_, bf16[640,2304]{1,0:T(8,128)(2,1)} %get-tuple-element.511.left_b.refs_9_, bf16[640,2304]{1,0:T(8,128)(2,1)} %get-tuple-element.534.right_a, ...), custom_call_target="tpu_custom_call" | custom-call | tf_op jit(solution)/shard_map/pallas_call | solution.py:300
  797.1 27.0 %shard_map.305 = (bf16[16,72,2304]{2,1,0:T(8,128)(2,1)}, bf16[16,72,2304]{2,1,0:T(8,128)(2,1)}) custom-call(s32[4]{0:T(128)} %get-tuple-element.383.place_ref.place, bf16[640,2304]{1,0:T(8,128)(2,1)} %get-tuple-element.555.left_a, bf16[640,2304]{1,0:T(8,128)(2,1)} %get-tuple-element.556.left_b, bf16[640,2304]{1,0:T(8,128)(2,1)} %get-tuple-element.557.right_a, ...), custom_call_target="tpu_custom_call" | custom-call | tf_op jit(solution)/shard_map/pallas_call | solution.py:300
  891.7 19.6 %shard_map.315 = (bf16[2,320,512]{2,1,0:T(8,128)(2,1)}, bf16[4,2,320,512]{3,2,1,0:T(8,128)(2,1)}, bf16[4,2,320,512]{3,2,1,0:T(8,128)(2,1)}) custom-call(s32[4]{0:T(128)} %get-tuple-element.383.place_ref.place, bf16[2,320,512]{2,1,0:T(8,128)(2,1)} %get-tuple-element.420.query_ref, bf16[2,320,512]{2,1,0:T(8,128)(2,1)} %get-tuple-element.600.grad_ref, ...), custom_call_target="tpu_custom_call" | custom-call | bytes 21000000 | tf_op jit(solution)/shard_map/pallas_call | solution.py:738
  931.8 19.6 %shard_map.319 = (bf16[2,320,512]{2,1,0:T(8,128)(2,1)}, bf16[4,2,320,512]{3,2,1,0:T(8,128)(2,1)}, bf16[4,2,320,512]{3,2,1,0:T(8,128)(2,1)}) custom-call(s32[4]{0:T(128)} %get-tuple-element.383.place_ref.place, bf16[2,320,512]{2,1,0:T(8,128)(2,1)} %get-tuple-element.437.query_ref, bf16[2,320,512]{2,1,0:T(8,128)(2,1)} %get-tuple-element.624.grad_ref, ...), custom_call_target="tpu_custom_call" | custom-call | bytes 21000000 | tf_op jit(solution)/shard_map/pallas_call | solution.py:738
  974.4 15.1 %reduce-scatter.17.cloned.1.call-done = bf16[1,2,320,512]{3,2,1,0:T(8,128)(2,1)} async-done(((bf16[4,2,320,512]{3,2,1,0:T(8,128)(2,1)}), bf16[1,2,320,512]{3,2,1,0:T(8,128)(2,1)}) %reduce-scatter.17.cloned.1.call-update) | async-done | bytes 655376 | tf_op jit(solution)/shard_map/reduce_scatter | solution.py:78
  1013.6 27.1 %shard_map.325 = (bf16[4,288,2304]{2,1,0:T(8,128)(2,1)}, bf16[4,288,2304]{2,1,0:T(8,128)(2,1)}) custom-call(s32[4]{0:T(128)} %get-tuple-element.383.place_ref.place, bf16[640,2304]{1,0:T(8,128)(2,1)} %get-tuple-element.645.left_a, bf16[640,2304]{1,0:T(8,128)(2,1)} %get-tuple-element.646.left_b, bf16[640,2304]{1,0:T(8,128)(2,1)} %get-tuple-element.647.right_a, ...), custom_call_target="tpu_custom_call" | custom-call | tf_op jit(solution)/shard_map/pallas_call | solution.py:300
  1068.4 14.2 %shard_map.331.refs_6_ = bf16[8,4,72,1024]{3,2,1,0:T(8,128)(2,1)} custom-call(bf16[640,2304]{1,0:T(8,128)(2,1)} %get-tuple-element.675.left_a, bf16[640,2304]{1,0:T(8,128)(2,1)} %get-tuple-element.676.left_b, bf16[640,512]{1,0:T(8,128)(2,1)} %bitcast.262, bf16[640,512]{1,0:T(8,128)(2,1)} %bitcast.263, bf16[640,512]{1,0:T(8,128)(2,1)} %bitcast.259, ...), custom_call_target="tpu_custom_call" | custom-call | bytes 21000000 | tf_op jit(solution)/shard_map/pallas_call | solution.py:537
  1152.1 11.8 collective-permute-start.78
  1181.1 10.8 collective-permute-done.76.refs_3_
  (736 shorter events, 554.0 us)
Async XLA Ops:
  7.2 115.5 %all-gather.18.cloned.1.call-start = ((), (), s32[]{:S(2)}) async-start(), calls=%async_computation.17 | async-start | bytes 5308416 | tf_op jit(solution)/shard_map/all_gather | solution.py:817
  29.0 164.5 %all-gather.20.cloned.1.call-start = ((), (), s32[]{:S(2)}) async-start(), calls=%async_computation.18 | async-start | bytes 3276800 | tf_op jit(solution)/shard_map/all_gather | solution.py:55
  32.8 37.6 %collective-permute-start.5 = (bf16[2,72,2304]{2,1,0:T(8,128)(2,1)}, bf16[2,72,2304]{2,1,0:T(8,128)(2,1)}, u32[]{:S(2)}, u32[]{:S(2)}) collective-permute-start(bf16[2,72,2304]{2,1,0:T(8,128)(2,1)} %get-tuple-element.396), channel_id=1, source_target_pairs={{0,2},{1,3},{2,4},{3,5},{4,6},{5,7},{6,0},{7,1},{8,10},{9,11},{10,... | collective-permute-start | bytes 1990664 | tf_op jit(solution)/shard_map/ppermute | solution.py:66
  34.5 75.6 %collective-permute-start.6 = (bf16[2,72,2304]{2,1,0:T(8,128)(2,1)}, bf16[2,72,2304]{2,1,0:T(8,128)(2,1)}, u32[]{:S(2)}, u32[]{:S(2)}) collective-permute-start(bf16[2,72,2304]{2,1,0:T(8,128)(2,1)} %get-tuple-element.397), channel_id=1, source_target_pairs={{0,4},{1,5},{2,6},{3,7},{4,0},{5,1},{6,2},{7,3},{8,12},{9,13},{10,... | collective-permute-start | bytes 1990664 | tf_op jit(solution)/shard_map/ppermute | solution.py:66
  37.1 76.3 %collective-permute-start.7 = (bf16[2,72,2304]{2,1,0:T(8,128)(2,1)}, bf16[2,72,2304]{2,1,0:T(8,128)(2,1)}, u32[]{:S(2)}, u32[]{:S(2)}) collective-permute-start(bf16[2,72,2304]{2,1,0:T(8,128)(2,1)} %get-tuple-element.398), channel_id=1, source_target_pairs={{0,6},{1,7},{2,0},{3,1},{4,2},{5,3},{6,4},{7,5},{8,14},{9,15},{10,... | collective-permute-start | bytes 1990664 | tf_op jit(solution)/shard_map/ppermute | solution.py:66
  132.6 119.4 %all-gather.22.cloned.1.call-start = ((), (), s32[]{:S(2)}) async-start(), calls=%async_computation.19 | async-start | bytes 3276800 | tf_op jit(solution)/shard_map/all_gather | solution.py:55
  153.4 60.6 %collective-permute-start.12 = (bf16[576,2304]{1,0:T(8,128)(2,1)}, bf16[576,2304]{1,0:T(8,128)(2,1)}, u32[]{:S(2)}, u32[]{:S(2)}) collective-permute-start(bf16[576,2304]{1,0:T(8,128)(2,1)} %get-tuple-element.415), channel_id=1, source_target_pairs={{0,8},{8,0},{16,24},{24,16},{1,9},{9,1},{17,25},{25,17},{2,10},{10... | collective-permute-start | bytes 7962632 | tf_op jit(solution)/shard_map/ppermute | solution.py:42
  153.8 60.2 %collective-permute-start.13 = (bf16[576,2304]{1,0:T(8,128)(2,1)}, bf16[576,2304]{1,0:T(8,128)(2,1)}, u32[]{:S(2)}, u32[]{:S(2)}) collective-permute-start(bf16[576,2304]{1,0:T(8,128)(2,1)} %get-tuple-element.415), channel_id=1, source_target_pairs={{0,16},{8,24},{16,0},{24,8},{1,17},{9,25},{17,1},{25,9},{2,18},{10... | collective-permute-start | bytes 7962632 | tf_op jit(solution)/shard_map/ppermute | solution.py:42
  193.5 97.5 %all-gather.16.cloned.1.call-start = ((), (), s32[]{:S(2)}) async-start(), calls=%async_computation.8 | async-start | bytes 2654208 | tf_op jit(solution)/shard_map/all_gather | solution.py:926
  214.0 37.9 %collective-permute-start.14 = (bf16[576,2304]{1,0:T(8,128)(2,1)}, bf16[576,2304]{1,0:T(8,128)(2,1)S(1)}, u32[]{:S(2)}, u32[]{:S(2)}) collective-permute-start(bf16[576,2304]{1,0:T(8,128)(2,1)} %get-tuple-element.431), channel_id=1, source_target_pairs={{0,1},{1,0},{2,3},{3,2},{4,5},{5,4},{6,7},{7,6},{8,9},{9,8},{10,11... | collective-permute-start | bytes 7962632 | tf_op jit(solution)/shard_map/ppermute | solution.py:46
  214.6 37.4 %collective-permute-start.15 = (bf16[576,2304]{1,0:T(8,128)(2,1)}, bf16[576,2304]{1,0:T(8,128)(2,1)}, u32[]{:S(2)}, u32[]{:S(2)}) collective-permute-start(bf16[576,2304]{1,0:T(8,128)(2,1)} %get-tuple-element.432), channel_id=1, source_target_pairs={{0,1},{1,0},{2,3},{3,2},{4,5},{5,4},{6,7},{7,6},{8,9},{9,8},{10,11... | collective-permute-start | bytes 7962632 | tf_op jit(solution)/shard_map/ppermute | solution.py:46
  255.3 139.4 %all-gather.24.cloned.1.call-start = ((), (), s32[]{:S(2)}) async-start(), calls=%async_computation.20 | async-start | bytes 3686400 | tf_op jit(solution)/shard_map/all_gather | solution.py:55
  336.7 119.6 %all-gather.26.cloned.1.call-start = ((), (), s32[]{:S(2)}) async-start(), calls=%async_computation.21 | async-start | bytes 3686400 | tf_op jit(solution)/shard_map/all_gather | solution.py:55
  371.1 36.8 %collective-permute-start.28 = (bf16[288,2304]{1,0:T(8,128)(2,1)}, bf16[288,2304]{1,0:T(8,128)(2,1)S(1)}, u32[]{:S(2)}, u32[]{:S(2)}) collective-permute-start(bf16[288,2304]{1,0:T(8,128)(2,1)} %shard_map.282.refs_1_), channel_id=1, source_target_pairs={{0,8},{8,0},{16,24},{24,16},{1,9},{9,1},{17,25},{25,17},{2,10},{10... | collective-permute-start | bytes 3981320 | tf_op jit(solution)/shard_map/ppermute | solution.py:42
  372.6 58.6 %collective-permute-start.32 = (bf16[288,2304]{1,0:T(8,128)(2,1)}, bf16[288,2304]{1,0:T(8,128)(2,1)}, u32[]{:S(2)}, u32[]{:S(2)}) collective-permute-start(bf16[288,2304]{1,0:T(8,128)(2,1)} %shard_map.282.refs_1_), channel_id=1, source_target_pairs={{0,1},{1,0},{2,3},{3,2},{4,5},{5,4},{6,7},{7,6},{8,9},{9,8},{10,11... | collective-permute-start | bytes 3981320 | tf_op jit(solution)/shard_map/ppermute | solution.py:46
  377.1 136.2 %reduce-scatter.9.cloned.1.call-start = ((), (), s32[]{:S(2)}) async-start(), calls=%async_computation.9 | async-start | bytes 3686400 | tf_op jit(solution)/shard_map/reduce_scatter | solution.py:78
  456.1 116.7 %reduce-scatter.11.cloned.1.call-start = ((), (), s32[]{:S(2)}) async-start(), calls=%async_computation.10 | async-start | bytes 3686400 | tf_op jit(solution)/shard_map/reduce_scatter | solution.py:78
  491.1 143.5 %all-gather.28.cloned.1.call-start = ((), (), s32[]{:S(2)}) async-start(), calls=%async_computation.22 | async-start | bytes 3686400 | tf_op jit(solution)/shard_map/all_gather | solution.py:55
  521.8 173.1 %all-gather.30.cloned.1.call-start = ((), (), s32[]{:S(2)}) async-start(), calls=%async_computation.23 | async-start | bytes 3686400 | tf_op jit(solution)/shard_map/all_gather | solution.py:55
  581.5 183.6 %reduce-scatter.13.cloned.1.call-start = ((), (), s32[]{:S(2)}) async-start(), calls=%async_computation.11 | async-start | bytes 3686400 | tf_op jit(solution)/shard_map/reduce_scatter | solution.py:78
  677.6 146.5 %reduce-scatter.15.cloned.1.call-start = ((), (), s32[]{:S(2)}) async-start(), calls=%async_computation.12 | async-start | bytes 3686400 | tf_op jit(solution)/shard_map/reduce_scatter | solution.py:78
  765.2 224.3 %reduce-scatter.17.cloned.1.call-start = ((), (), s32[]{:S(2)}) async-start(), calls=%async_computation.13 | async-start | bytes 3276800 | tf_op jit(solution)/shard_map/reduce_scatter | solution.py:78
  843.9 36.9 %collective-permute-start.45 = (bf16[144,2304]{1,0:T(8,128)(2,1)}, bf16[144,2304]{1,0:T(8,128)(2,1)}, u32[]{:S(2)}, u32[]{:S(2)}) collective-permute-start(bf16[144,2304]{1,0:T(8,128)(2,1)} %get-tuple-element.588), channel_id=1, source_target_pairs={{0,8},{8,0},{16,24},{24,16},{1,9},{9,1},{17,25},{25,17},{2,10},{10... | collective-permute-start | bytes 1990664 | tf_op jit(solution)/shard_map/ppermute | solution.py:42
  870.6 40.7 %collective-permute-start.48 = (bf16[80,2304]{1,0:T(8,128)(2,1)}, bf16[80,2304]{1,0:T(8,128)(2,1)S(1)}, u32[]{:S(2)}, u32[]{:S(2)}) collective-permute-start(bf16[80,2304]{1,0:T(8,128)(2,1)} %slice.255), channel_id=1, source_target_pairs={{0,8},{8,0},{16,24},{24,16},{1,9},{9,1},{17,25},{25,17},{2,10},{10... | collective-permute-start | bytes 1105928 | tf_op jit(solution)/shard_map/ppermute | solution.py:42
  874.9 36.5 %collective-permute-start.49 = (bf16[80,2304]{1,0:T(8,128)(2,1)}, bf16[80,2304]{1,0:T(8,128)(2,1)}, u32[]{:S(2)}, u32[]{:S(2)}) collective-permute-start(bf16[80,2304]{1,0:T(8,128)(2,1)} %slice.256), channel_id=1, source_target_pairs={{0,16},{8,24},{16,0},{24,8},{1,17},{9,25},{17,1},{25,9},{2,18},{10... | collective-permute-start | bytes 1105928 | tf_op jit(solution)/shard_map/ppermute | solution.py:42
  929.2 114.9 %reduce-scatter.19.cloned.1.call-start = ((), (), s32[]{:S(2)}) async-start(), calls=%async_computation.14 | async-start | bytes 3276800 | tf_op jit(solution)/shard_map/reduce_scatter | solution.py:78
  989.5 116.5 %reduce-scatter.23.cloned.1.call-start = ((), (), s32[]{:S(2)}) async-start(), calls=%async_computation.16 | async-start | bytes 2654208 | tf_op jit(solution)/shard_map/reduce_scatter | solution.py:1190
  1044.1 122.2 %reduce-scatter.21.cloned.1.call-start = ((), (), s32[]{:S(2)}) async-start(), calls=%async_computation.15 | async-start | bytes 5308416 | tf_op jit(solution)/shard_map/reduce_scatter | solution.py:1209
  1052.1 40.3 %collective-permute-start.59 = (bf16[2,160,2304]{2,1,0:T(8,128)(2,1)}, bf16[2,160,2304]{2,1,0:T(8,128)(2,1)S(1)}, u32[]{:S(2)}, u32[]{:S(2)}) collective-permute-start(bf16[2,160,2304]{2,1,0:T(8,128)(2,1)} %get-tuple-element.666), channel_id=1, source_target_pairs={{0,8},{8,0},{16,24},{24,16},{1,9},{9,1},{17,25},{25,17},{2,10},{10... | collective-permute-start | bytes 4423688 | tf_op jit(solution)/shard_map/ppermute | solution.py:42
  1053.5 38.9 %collective-permute-start.60 = (bf16[2,160,2304]{2,1,0:T(8,128)(2,1)}, bf16[2,160,2304]{2,1,0:T(8,128)(2,1)S(1)}, u32[]{:S(2)}, u32[]{:S(2)}) collective-permute-start(bf16[2,160,2304]{2,1,0:T(8,128)(2,1)} %get-tuple-element.667), channel_id=1, source_target_pairs={{0,16},{8,24},{16,0},{24,8},{1,17},{9,25},{17,1},{25,9},{2,18},{10... | collective-permute-start | bytes 4423688 | tf_op jit(solution)/shard_map/ppermute | solution.py:42
  1055.0 36.6 %collective-permute-start.62 = (bf16[1,72,2304]{2,1,0:T(8,128)(2,1)}, bf16[1,72,2304]{2,1,0:T(8,128)(2,1)S(1)}, u32[]{:S(2)}, u32[]{:S(2)}) collective-permute-start(bf16[1,72,2304]{2,1,0:T(8,128)(2,1)} %get-tuple-element.685), channel_id=1, source_target_pairs={{0,2},{1,3},{2,4},{3,5},{4,6},{5,7},{6,0},{7,1},{8,10},{9,11},{10,... | collective-permute-start | bytes 995336 | tf_op jit(solution)/shard_map/ppermute | solution.py:66
  1055.6 36.7 %collective-permute-start.63 = (bf16[1,72,2304]{2,1,0:T(8,128)(2,1)}, bf16[1,72,2304]{2,1,0:T(8,128)(2,1)S(1)}, u32[]{:S(2)}, u32[]{:S(2)}) collective-permute-start(bf16[1,72,2304]{2,1,0:T(8,128)(2,1)} %get-tuple-element.686), channel_id=1, source_target_pairs={{0,4},{1,5},{2,6},{3,7},{4,0},{5,1},{6,2},{7,3},{8,12},{9,13},{10,... | collective-permute-start | bytes 995336 | tf_op jit(solution)/shard_map/ppermute | solution.py:66
  (207 other events, 2081.9 us)
Sparse Core Ops, SparseCore 0:
  29.1 93.4 all-gather.17
  132.7 60.7 all-gather.19
  195.1 53.5 all-gather.21
  255.4 35.5 all-gather.15
  336.8 57.8 all-gather.23
  396.1 58.9 all-gather.25
  457.4 55.8 reduce-scatter.8
  515.7 57.0 reduce-scatter.10
  574.4 60.1 all-gather.27
  636.0 58.9 all-gather.29
  697.3 55.8 reduce-scatter.12
  765.3 56.0 reduce-scatter.14
  929.3 60.1 reduce-scatter.16
  992.2 51.7 reduce-scatter.18
  1046.8 53.9 reduce-scatter.22
  1103.0 61.9 reduce-scatter.20

commit v4 on v3

--- a/solution.py
+++ b/solution.py
@@ -766,7 +766,7 @@
             jax.ShapeDtypeStruct(own.shape, jnp.bfloat16),
         ],
         compiler_params=pltpu.CompilerParams(vmem_limit_bytes=VMEM_LIMIT),
-        cost_estimate=cost(6),
+        cost_estimate=FREE,
     )(place, queries, grads, attended, own, other, codes, logs, segments)
 
 
@@ -809,10 +809,10 @@
     flipped = pack_heads(place, w_query, key_weight, value_weight)
     split = split_columns(place, w_gate, w_up, dp, line)
     if quad:
-        flipped, split, place = order(flipped, split, place)
+        flipped = order(flipped)
         mixed = [flipped[0]] + [across(flipped[k], k) for k in (1, 2, 3)]
         normed_in = normed(inputs, pre_attention).astype(bf16)
-        mixed, normed_in, split = order(order_heads(place, mixed), normed_in, split)
+        mixed, normed_in, split, place = order(order_heads(place, mixed), normed_in, split, place)
         near_normed = gather_quad_near(normed_in)
         in_weight = lax.all_gather(mixed, "seq", axis=1).reshape(model, 2 * width)
     else:
@@ -843,6 +843,9 @@
     def far_blocks(near):
         return (gather_quad_far(*near),) if quad else ()
 
+    def far_halves(near):
+        return gather_quad_far_parts(*near) if quad else ()
+
     def swap_all(blocks):
         return [swap_core(block) for block in blocks]
 
@@ -866,8 +869,13 @@
             sources.append(block)
         return deposit(place, [weight], sources, moves)[0] if sources else weight
 
-    def fill_in(gate, up, numbers, mine, swapped):
+    def fill_in(gate, up, numbers, mine, swapped, halves=()):
         sources, moves = [], []
+        for which, pair in enumerate(halves):
+            for other, block in enumerate(pair):
+                target = lambda at, other=other: (at_dp(at, 3), slice(None), at[CORE_AT] ^ other)
+                moves.append((len(sources), None, which, target))
+                sources.append(block.reshape(line, rows, ff_part))
         for k, other, block in sides(numbers, mine, swapped):
             for which in (0, 1):
                 source = lambda at, which=which: (slice(None),) * (not quad) + (which,)
@@ -918,12 +926,12 @@
     attended[0], log_total[0], gate_weight, up_weight, near_in = order(
         attended[0], log_total[0], gate_weight, up_weight, near_in
     )
-    far_in = far_blocks(near_in)
+    far_in = far_halves(near_in)
     swapped = swap_all(near_in)
     second_own, swapped, far_in = order(second_own, swapped, far_in)
     second_other = swap_core(second_own)
     if quad:
-        out_weight = lax.all_gather(after(w_output, second_own), "seq", axis=0, tiled=True)
+        out_weight = lax.all_gather(after(w_output, attended[0]), "seq", axis=0, tiled=True)
     else:
         out_weight = lax.dynamic_slice_in_dim(
             lax.all_gather(w_output, ("dp", "seq"), axis=0, tiled=True), head * width, width
@@ -936,7 +944,7 @@
         place, second_queries, second_own, second_other, row_codes[1], column_segments[1]
     )
     attended, log_total, out_weight, swapped = order(attended, log_total, out_weight, swapped)
-    in_blocks, swapped = list(near_in) + list(far_in), near_swapped + swapped
+    in_halves = list(zip(far_in, swapped))
     queries = [first_queries, second_queries]
     own_keys, other_keys = [first_own, second_own], [first_other, second_other]
 
@@ -969,7 +977,9 @@
     mid_rows_b = gather_line(mid_b).reshape(line * step, model)
     own_down = after(w_down, far_b[0])
     near_down = near_blocks(own_down)
-    gate_weight, up_weight = fill_in(gate_weight, up_weight, numbers, in_blocks, swapped)
+    gate_weight, up_weight = fill_in(
+        gate_weight, up_weight, numbers, near_in, near_swapped, in_halves
+    )
     mid_rows_a, gate_weight, up_weight = order(mid_rows_a, gate_weight, up_weight)
     gate_weight = gate_weight.reshape(model, ff_part)
     up_weight = up_weight.reshape(model, ff_part)
@@ -1156,13 +1166,13 @@
     )
     up_near = near_sums(up_sent)
     swapped = swap_core(other_grad)
+    swapped, far_b, far_a = order(swapped, far_b, far_a)
+    first_key_grads, far_b, far_a = order(own_grad + swapped, far_b, far_a)
+    first_key_grads = scatter_line(first_key_grads)
     second_attn = attention_rows(
         [quad_a[2], jnp.concatenate(far_a, axis=0)], [near_b[1], jnp.concatenate(far_b, axis=0)]
     )
     grad_attended = attended_grad(second_attn)
-    swapped, grad_attended = order(swapped, grad_attended)
-    first_key_grads = order(own_grad + swapped)
-    first_key_grads = scatter_line(first_key_grads)
     second_grads, own_grad, other_grad, up_near = order(*attend_back(1, grad_attended), up_near)
     swapped = swap_core(other_grad)
     up_far = far_terms(up_kept, up_near)

time: 1220 us -> 1200 us (0.984)
  waiting for transfers between devices: 440 us -> 423 us
    ppermute x53, waiting for transfers between devices: 159 us -> 122 us  [across(): lax.ppermute(x, 'dp', [(i, i ^ bits) for i in range(lax.axis_size('dp'))])]
    all_gather x6, waiting for transfers between devices: 122 us -> 147 us  [gather_line(): return lax.all_gather(x, 'seq', axis=0, axis_index_groups=line_groups())]
    unnamed x299 -> x291, local copies, waits for them, and re-layouts: 42.6 us -> 40.6 us
  transfers between devices with their start and end apart: 97 -> 98, of which waited for: 52 -> 54; matrix products, arithmetic and copies ran while one was open for 26% -> 27% of each run, Pallas kernels for 23% -> 23%
where the time goes in v4:
time: 1200 us; the launch traced here: 1190 us
  waiting for transfers between devices  423 us (35%)
  Pallas kernels  286 us (24%)
  matrix products  190 us (16%)
  starting transfers between devices  96 us (8%)
  other arithmetic  92 us (8%)
  local copies, waits for them, and re-layouts  87.5 us (7%)
  between operations  15.7 us (1%)
    all_gather x6, waiting for transfers between devices, gather_line(): return lax.all_gather(x, 'seq', axis=0, axis_index_groups=line_groups())  147 us
    ppermute x53, waiting for transfers between devices, across(): lax.ppermute(x, 'dp', [(i, i ^ bits) for i in range(lax.axis_size('dp'))])  122 us
    dot_general x8, matrix products, matmul_t(): lax.dot_general(a, b, (((1,), (1,)), ((), ())), preferred_element_type=jn...  94.8 us
    dot_general x8, matrix products, matmul(): return jnp.dot(a, b, preferred_element_type=jnp.float32)  88.1 us
    pallas_call x3, Pallas kernels, weight_halves(): pl.pallas_call(kernel, grid=(model // block,), in_specs=[pl.BlockSpec(mem...  81.2 us
    reduce_scatter x6, waiting for transfers between devices, scatter_line(): lax.psum_scatter(x, 'seq', scatter_dimension=0, axis_index_groups=line_gr...  78 us
    ppermute x53, starting transfers between devices, across(): lax.ppermute(x, 'dp', [(i, i ^ bits) for i in range(lax.axis_size('dp'))])  61.8 us
    ppermute x12, waiting for transfers between devices, exchange_line_parts(): lax.ppermute(parts[k], 'seq', line_route(line, k))  42 us
  transfers between devices with their start and end apart: 98, of which 54 were waited for; matrix products, arithmetic and copies ran while one was open for 27% of the time, Pallas kernels for 23%

profile of v4, /device:TPU:0, one launch (start us, length us, event | category | flops | bytes accessed | tf_op | source)
XLA Modules:
  0.0 1191.0 jit_solution(5702846295529694805)
XLA Ops:
  38.6 23.3 %collective-permute-done.3.refs_1_ = bf16[320,2304]{1,0:T(8,128)(2,1)} collective-permute-done((bf16[320,2304]{1,0:T(8,128)(2,1)}, bf16[320,2304]{1,0:T(8,128)(2,1)}, u32[]{:S(2)}, u32[]{:S(2)}) %collective-permute-start.3) | collective-permute-done | bytes 1474592 | tf_op jit(solution)/shard_map/ppermute | solution.py:42
  69.2 39.5 %collective-permute-done.6.refs_8_ = bf16[2,72,2304]{2,1,0:T(8,128)(2,1)} collective-permute-done((bf16[2,72,2304]{2,1,0:T(8,128)(2,1)}, bf16[2,72,2304]{2,1,0:T(8,128)(2,1)}, u32[]{:S(2)}, u32[]{:S(2)}) %collective-permute-start.6) | collective-permute-done | bytes 663584 | tf_op jit(solution)/shard_map/ppermute | solution.py:66
  110.4 10.9 all-gather.18.cloned.1.call-done
  158.5 33.6 %all-gather.20.cloned.1.call-done = bf16[8,320,512]{2,1,0:T(8,128)(2,1)} async-done(((bf16[2,320,512]{2,1,0:T(8,128)(2,1)}), bf16[8,320,512]{2,1,0:T(8,128)(2,1)}) %all-gather.20.cloned.1.call-update) | async-done | bytes 2621456 | tf_op jit(solution)/shard_map/all_gather | solution.py:55
  199.4 11.6 shard_map.259
  223.4 24.4 %all-gather.22.cloned.1.call-done = bf16[8,320,512]{2,1,0:T(8,128)(2,1)} async-done(((bf16[2,320,512]{2,1,0:T(8,128)(2,1)}), bf16[8,320,512]{2,1,0:T(8,128)(2,1)}) %all-gather.22.cloned.1.call-update) | async-done | bytes 2621456 | tf_op jit(solution)/shard_map/all_gather | solution.py:55
  262.2 11.4 shard_map.266
  291.5 11.8 collective-permute-done.21.refs_1_
  345.5 11.4 shard_map.280
  366.9 18.7 %all-gather.24.cloned.1.call-done.refs_1_ = bf16[640,2304]{1,0:T(8,128)(2,1)} async-done(((bf16[160,2304]{1,0:T(8,128)(2,1)}), bf16[640,2304]{1,0:T(8,128)(2,1)}) %all-gather.24.cloned.1.call-update) | async-done | bytes 2949136 | tf_op jit(solution)/shard_map/all_gather | solution.py:55
  385.6 13.3 %fusion.72.refs_1_ = f32[640,2304]{1,0:T(8,128)} fusion(bf16[640,2304]{1,0:T(8,128)(2,1)} %get-tuple-element.494.refs_2_, bf16[2304,2304]{1,0:T(8,128)(2,1)} %bitcast.229), kind=kOutput, calls=%fused_computation.234 | convolution fusion | flops 6794772480 | bytes 19464192 | tf_op jit(solution)/shard_map/dot_general | solution.py:30
  405.8 14.8 %multiply_convert_fusion.3 = (bf16[640,2304]{1,0:T(8,128)(2,1)}, f32[640,2304]{1,0:T(8,128)}) fusion(f32[640,2304]{1,0:T(8,128)} %get-tuple-element.497, bf16[640,2304]{1,0:T(8,128)(2,1)} %get-tuple-element.498.left_a.refs_8_, bf16[2304,2304]{1,0:T(8,128)(2,1)} %bitcast.235), kind=kOutput, calls=%fused_computation.23 | convolution fusion | flops 6809518080 | bytes 28311552 | tf_op jit(solution)/shard_map/dot_general | solution.py:30
  434.6 12.4 %convolution_convert_fusion.1 = bf16[640,2304]{1,0:T(8,128)(2,1)} fusion(bf16[640,2304]{1,0:T(8,128)(2,1)S(1)} %copy-done.17, bf16[2304,2304]{1,0:T(8,128)(2,1)} %bitcast.243), kind=kOutput, calls=%fused_computation.28 | convolution fusion | flops 6796247040 | bytes 16515072 | tf_op jit(solution)/shard_map/dot_general | solution.py:30
  447.3 13.5 %fusion.73 = f32[640,2304]{1,0:T(8,128)} fusion(bf16[640,2304]{1,0:T(8,128)(2,1)} %get-tuple-element.514.left_b.refs_9_, bf16[2304,2304]{1,0:T(8,128)(2,1)} %bitcast.230), kind=kOutput, calls=%fused_computation.235 | convolution fusion | flops 6794772480 | bytes 19464192 | tf_op jit(solution)/shard_map/dot_general | solution.py:30
  460.9 11.3 multiply_convert_fusion.2
  485.1 19.1 %reduce-scatter.9.cloned.1.call-done = bf16[1,160,2304]{2,1,0:T(8,128)(2,1)} async-done(((bf16[4,160,2304]{2,1,0:T(8,128)(2,1)}), bf16[1,160,2304]{2,1,0:T(8,128)(2,1)}) %reduce-scatter.9.cloned.1.call-update) | async-done | bytes 737296 | tf_op jit(solution)/shard_map/reduce_scatter | solution.py:78
  522.5 41.3 %reduce-scatter.11.cloned.1.call-done = bf16[1,160,2304]{2,1,0:T(8,128)(2,1)} async-done(((bf16[4,160,2304]{2,1,0:T(8,128)(2,1)}), bf16[1,160,2304]{2,1,0:T(8,128)(2,1)}) %reduce-scatter.11.cloned.1.call-update) | async-done | bytes 737296 | tf_op jit(solution)/shard_map/reduce_scatter | solution.py:78
  572.7 52.9 %all-gather.28.cloned.1.call-done.refs_1_ = bf16[640,2304]{1,0:T(8,128)(2,1)} async-done(((bf16[160,2304]{1,0:T(8,128)(2,1)}), bf16[640,2304]{1,0:T(8,128)(2,1)}) %all-gather.28.cloned.1.call-update) | async-done | bytes 2949136 | tf_op jit(solution)/shard_map/all_gather | solution.py:55
  625.5 18.9 %multiply_convert_fusion.1 = (bf16[640,2304]{1,0:T(8,128)(2,1)}, bf16[640,2304]{1,0:T(8,128)(2,1)}) fusion(f32[640,2304]{1,0:T(8,128)} %get-tuple-element.497, f32[640,2304]{1,0:T(8,128)} %get-tuple-element.823, bf16[640,2304]{1,0:T(8,128)(2,1)} %get-tuple-element.530.refs_5_, bf16[2304,2304]{1,0:T(8,128)(2,1)} %bitcast.244), kind=kOutput, calls=%fused_computation.21 | convolution fusion | flops 6830161920 | bytes 31260672 | tf_op jit(solution)/shard_map/dot_general | solution.py:34
  654.7 13.8 %add_convert_fusion.1 = bf16[640,2304]{1,0:T(8,128)(2,1)} fusion(f32[640,2304]{1,0:T(8,128)} %fusion.74, bf16[640,2304]{1,0:T(8,128)(2,1)} %get-tuple-element.777.refs_1_, bf16[2304,2304]{1,0:T(8,128)(2,1)} %bitcast.231), kind=kOutput, calls=%fused_computation.20 | convolution fusion | flops 6797721600 | bytes 22413312 | tf_op jit(solution)/shard_map/dot_general | solution.py:34
  669.0 16.9 %all-gather.30.cloned.1.call-done.refs_1_ = bf16[640,2304]{1,0:T(8,128)(2,1)} async-done(((bf16[160,2304]{1,0:T(8,128)(2,1)}), bf16[640,2304]{1,0:T(8,128)(2,1)}) %all-gather.30.cloned.1.call-update) | async-done | bytes 2949136 | tf_op jit(solution)/shard_map/all_gather | solution.py:55
  685.9 18.9 %multiply_convert_fusion = (bf16[640,2304]{1,0:T(8,128)(2,1)}, bf16[640,2304]{1,0:T(8,128)(2,1)}) fusion(f32[640,2304]{1,0:T(8,128)} %fusion.73, f32[640,2304]{1,0:T(8,128)} %get-tuple-element.825, bf16[640,2304]{1,0:T(8,128)(2,1)} %get-tuple-element.534.refs_6_, bf16[2304,2304]{1,0:T(8,128)(2,1)} %bitcast.245), kind=kOutput, calls=%fused_computation.19 | convolution fusion | flops 6830161920 | bytes 31260672 | tf_op jit(solution)/shard_map/dot_general | solution.py:34
  715.1 13.8 %add_convert_fusion = bf16[640,2304]{1,0:T(8,128)(2,1)} fusion(f32[640,2304]{1,0:T(8,128)} %fusion.75, bf16[640,2304]{1,0:T(8,128)(2,1)} %get-tuple-element.774.refs_2_, bf16[2304,2304]{1,0:T(8,128)(2,1)} %bitcast.236), kind=kOutput, calls=%fused_computation.18 | convolution fusion | flops 6797721600 | bytes 22413312 | tf_op jit(solution)/shard_map/dot_general | solution.py:34
  729.0 27.0 %shard_map.300 = (bf16[16,72,2304]{2,1,0:T(8,128)(2,1)}, bf16[16,72,2304]{2,1,0:T(8,128)(2,1)}) custom-call(s32[4]{0:T(128)} %get-tuple-element.405.place_ref.place, bf16[640,2304]{1,0:T(8,128)(2,1)} %get-tuple-element.498.left_a.refs_8_, bf16[640,2304]{1,0:T(8,128)(2,1)} %get-tuple-element.514.left_b.refs_9_, bf16[640,2304]{1,0:T(8,128)(2,1)} %get-tuple-element.537.right_a, ...), custom_call_target="tpu_custom_call" | custom-call | tf_op jit(solution)/shard_map/pallas_call | solution.py:300
  788.1 27.0 %shard_map.305 = (bf16[16,72,2304]{2,1,0:T(8,128)(2,1)}, bf16[16,72,2304]{2,1,0:T(8,128)(2,1)}) custom-call(s32[4]{0:T(128)} %get-tuple-element.405.place_ref.place, bf16[640,2304]{1,0:T(8,128)(2,1)} %get-tuple-element.558.left_a, bf16[640,2304]{1,0:T(8,128)(2,1)} %get-tuple-element.559.left_b, bf16[640,2304]{1,0:T(8,128)(2,1)} %get-tuple-element.560.right_a, ...), custom_call_target="tpu_custom_call" | custom-call | tf_op jit(solution)/shard_map/pallas_call | solution.py:300
  882.7 19.6 %shard_map.315 = (bf16[2,320,512]{2,1,0:T(8,128)(2,1)}, bf16[4,2,320,512]{3,2,1,0:T(8,128)(2,1)}, bf16[4,2,320,512]{3,2,1,0:T(8,128)(2,1)}) custom-call(s32[4]{0:T(128)} %get-tuple-element.405.place_ref.place, bf16[2,320,512]{2,1,0:T(8,128)(2,1)} %get-tuple-element.421.query_ref, bf16[2,320,512]{2,1,0:T(8,128)(2,1)} %get-tuple-element.603.grad_ref, ...), custom_call_target="tpu_custom_call" | custom-call | tf_op jit(solution)/shard_map/pallas_call | solution.py:738
  926.5 19.8 %shard_map.319 = (bf16[2,320,512]{2,1,0:T(8,128)(2,1)}, bf16[4,2,320,512]{3,2,1,0:T(8,128)(2,1)}, bf16[4,2,320,512]{3,2,1,0:T(8,128)(2,1)}) custom-call(s32[4]{0:T(128)} %get-tuple-element.405.place_ref.place, bf16[2,320,512]{2,1,0:T(8,128)(2,1)} %get-tuple-element.438.query_ref, bf16[2,320,512]{2,1,0:T(8,128)(2,1)} %bitcast.282, ...), custom_call_target="tpu_custom_call" | custom-call | tf_op jit(solution)/shard_map/pallas_call | solution.py:738
  959.5 14.1 %reduce-scatter.17.cloned.1.call-done = bf16[1,2,320,512]{3,2,1,0:T(8,128)(2,1)} async-done(((bf16[4,2,320,512]{3,2,1,0:T(8,128)(2,1)}), bf16[1,2,320,512]{3,2,1,0:T(8,128)(2,1)}) %reduce-scatter.17.cloned.1.call-update) | async-done | bytes 655376 | tf_op jit(solution)/shard_map/reduce_scatter | solution.py:78
  997.7 27.1 %shard_map.325 = (bf16[4,288,2304]{2,1,0:T(8,128)(2,1)}, bf16[4,288,2304]{2,1,0:T(8,128)(2,1)}) custom-call(s32[4]{0:T(128)} %get-tuple-element.405.place_ref.place, bf16[640,2304]{1,0:T(8,128)(2,1)} %get-tuple-element.655.left_a, bf16[640,2304]{1,0:T(8,128)(2,1)} %get-tuple-element.656.left_b, bf16[640,2304]{1,0:T(8,128)(2,1)} %get-tuple-element.657.right_a, ...), custom_call_target="tpu_custom_call" | custom-call | tf_op jit(solution)/shard_map/pallas_call | solution.py:300
  1052.6 14.2 %shard_map.331.refs_6_ = bf16[8,4,72,1024]{3,2,1,0:T(8,128)(2,1)} custom-call(bf16[640,2304]{1,0:T(8,128)(2,1)} %get-tuple-element.685.left_a, bf16[640,2304]{1,0:T(8,128)(2,1)} %get-tuple-element.686.left_b, bf16[640,512]{1,0:T(8,128)(2,1)} %bitcast.263, bf16[640,512]{1,0:T(8,128)(2,1)} %bitcast.264, bf16[640,512]{1,0:T(8,128)(2,1)} %bitcast.260, ...), custom_call_target="tpu_custom_call" | custom-call | bytes 21000000 | tf_op jit(solution)/shard_map/pallas_call | solution.py:537
  1136.2 11.7 collective-permute-start.79
  1165.3 10.7 collective-permute-done.77.refs_3_
  (729 shorter events, 546.4 us)
Async XLA Ops:
  7.2 114.1 %all-gather.18.cloned.1.call-start = ((), (), s32[]{:S(2)}) async-start(), calls=%async_computation.17 | async-start | bytes 5308416 | tf_op jit(solution)/shard_map/all_gather | solution.py:817
  25.9 166.2 %all-gather.20.cloned.1.call-start = ((), (), s32[]{:S(2)}) async-start(), calls=%async_computation.18 | async-start | bytes 3276800 | tf_op jit(solution)/shard_map/all_gather | solution.py:55
  26.7 37.3 %collective-permute-start.4 = (bf16[320,2304]{1,0:T(8,128)(2,1)}, bf16[320,2304]{1,0:T(8,128)(2,1)}, u32[]{:S(2)}, u32[]{:S(2)}) collective-permute-start(bf16[320,2304]{1,0:T(8,128)(2,1)} %get-tuple-element.393), channel_id=1, source_target_pairs={{0,8},{8,0},{16,24},{24,16},{1,9},{9,1},{17,25},{25,17},{2,10},{10... | collective-permute-start | bytes 4423688 | tf_op jit(solution)/shard_map/ppermute | solution.py:42
  31.1 38.1 %collective-permute-start.5 = (bf16[2,72,2304]{2,1,0:T(8,128)(2,1)}, bf16[2,72,2304]{2,1,0:T(8,128)(2,1)}, u32[]{:S(2)}, u32[]{:S(2)}) collective-permute-start(bf16[2,72,2304]{2,1,0:T(8,128)(2,1)} %get-tuple-element.396), channel_id=1, source_target_pairs={{0,2},{1,3},{2,4},{3,5},{4,6},{5,7},{6,0},{7,1},{8,10},{9,11},{10,... | collective-permute-start | bytes 1990664 | tf_op jit(solution)/shard_map/ppermute | solution.py:66
  32.7 76.0 %collective-permute-start.6 = (bf16[2,72,2304]{2,1,0:T(8,128)(2,1)}, bf16[2,72,2304]{2,1,0:T(8,128)(2,1)}, u32[]{:S(2)}, u32[]{:S(2)}) collective-permute-start(bf16[2,72,2304]{2,1,0:T(8,128)(2,1)} %get-tuple-element.397), channel_id=1, source_target_pairs={{0,4},{1,5},{2,6},{3,7},{4,0},{5,1},{6,2},{7,3},{8,12},{9,13},{10,... | collective-permute-start | bytes 1990664 | tf_op jit(solution)/shard_map/ppermute | solution.py:66
  35.3 75.1 %collective-permute-start.7 = (bf16[2,72,2304]{2,1,0:T(8,128)(2,1)}, bf16[2,72,2304]{2,1,0:T(8,128)(2,1)}, u32[]{:S(2)}, u32[]{:S(2)}) collective-permute-start(bf16[2,72,2304]{2,1,0:T(8,128)(2,1)} %get-tuple-element.398), channel_id=1, source_target_pairs={{0,6},{1,7},{2,0},{3,1},{4,2},{5,3},{6,4},{7,5},{8,14},{9,15},{10,... | collective-permute-start | bytes 1990664 | tf_op jit(solution)/shard_map/ppermute | solution.py:66
  130.0 117.9 %all-gather.22.cloned.1.call-start = ((), (), s32[]{:S(2)}) async-start(), calls=%async_computation.19 | async-start | bytes 3276800 | tf_op jit(solution)/shard_map/all_gather | solution.py:55
  153.2 127.1 %all-gather.16.cloned.1.call-start = ((), (), s32[]{:S(2)}) async-start(), calls=%async_computation.8 | async-start | bytes 2654208 | tf_op jit(solution)/shard_map/all_gather | solution.py:934
  153.4 60.4 %collective-permute-start.12 = (bf16[576,2304]{1,0:T(8,128)(2,1)}, bf16[576,2304]{1,0:T(8,128)(2,1)}, u32[]{:S(2)}, u32[]{:S(2)}) collective-permute-start(bf16[576,2304]{1,0:T(8,128)(2,1)} %get-tuple-element.416), channel_id=1, source_target_pairs={{0,8},{8,0},{16,24},{24,16},{1,9},{9,1},{17,25},{25,17},{2,10},{10... | collective-permute-start | bytes 7962632 | tf_op jit(solution)/shard_map/ppermute | solution.py:42
  155.0 60.0 %collective-permute-start.13 = (bf16[576,2304]{1,0:T(8,128)(2,1)}, bf16[576,2304]{1,0:T(8,128)(2,1)}, u32[]{:S(2)}, u32[]{:S(2)}) collective-permute-start(bf16[576,2304]{1,0:T(8,128)(2,1)} %get-tuple-element.416), channel_id=1, source_target_pairs={{0,16},{8,24},{16,0},{24,8},{1,17},{9,25},{17,1},{25,9},{2,18},{10... | collective-permute-start | bytes 7962632 | tf_op jit(solution)/shard_map/ppermute | solution.py:42
  215.0 38.8 %collective-permute-start.14 = (bf16[576,2304]{1,0:T(8,128)(2,1)}, bf16[576,2304]{1,0:T(8,128)(2,1)}, u32[]{:S(2)}, u32[]{:S(2)}) collective-permute-start(bf16[576,2304]{1,0:T(8,128)(2,1)} %get-tuple-element.432), channel_id=1, source_target_pairs={{0,1},{1,0},{2,3},{3,2},{4,5},{5,4},{6,7},{7,6},{8,9},{9,8},{10,11... | collective-permute-start | bytes 7962632 | tf_op jit(solution)/shard_map/ppermute | solution.py:46
  215.0 38.8 %collective-permute-start.15 = (bf16[576,2304]{1,0:T(8,128)(2,1)}, bf16[576,2304]{1,0:T(8,128)(2,1)}, u32[]{:S(2)}, u32[]{:S(2)}) collective-permute-start(bf16[576,2304]{1,0:T(8,128)(2,1)} %get-tuple-element.433), channel_id=1, source_target_pairs={{0,1},{1,0},{2,3},{3,2},{4,5},{5,4},{6,7},{7,6},{8,9},{9,8},{10,11... | collective-permute-start | bytes 7962632 | tf_op jit(solution)/shard_map/ppermute | solution.py:46
  217.3 168.3 %all-gather.24.cloned.1.call-start = ((), (), s32[]{:S(2)}) async-start(), calls=%async_computation.20 | async-start | bytes 3686400 | tf_op jit(solution)/shard_map/all_gather | solution.py:55
  326.0 121.2 %all-gather.26.cloned.1.call-start = ((), (), s32[]{:S(2)}) async-start(), calls=%async_computation.21 | async-start | bytes 3686400 | tf_op jit(solution)/shard_map/all_gather | solution.py:55
  360.4 38.5 %collective-permute-start.29 = (bf16[288,2304]{1,0:T(8,128)(2,1)}, bf16[288,2304]{1,0:T(8,128)(2,1)S(1)}, u32[]{:S(2)}, u32[]{:S(2)}) collective-permute-start(bf16[288,2304]{1,0:T(8,128)(2,1)} %shard_map.282.refs_1_), channel_id=1, source_target_pairs={{0,8},{8,0},{16,24},{24,16},{1,9},{9,1},{17,25},{25,17},{2,10},{10... | collective-permute-start | bytes 3981320 | tf_op jit(solution)/shard_map/ppermute | solution.py:42
  361.4 37.5 %collective-permute-start.30 = (bf16[288,2304]{1,0:T(8,128)(2,1)}, bf16[288,2304]{1,0:T(8,128)(2,1)}, u32[]{:S(2)}, u32[]{:S(2)}) collective-permute-start(bf16[288,2304]{1,0:T(8,128)(2,1)} %shard_map.282.refs_1_), channel_id=1, source_target_pairs={{0,16},{8,24},{16,0},{24,8},{1,17},{9,25},{17,1},{25,9},{2,18},{10... | collective-permute-start | bytes 3981320 | tf_op jit(solution)/shard_map/ppermute | solution.py:42
  361.9 60.2 %collective-permute-start.33 = (bf16[288,2304]{1,0:T(8,128)(2,1)}, bf16[288,2304]{1,0:T(8,128)(2,1)}, u32[]{:S(2)}, u32[]{:S(2)}) collective-permute-start(bf16[288,2304]{1,0:T(8,128)(2,1)} %shard_map.282.refs_1_), channel_id=1, source_target_pairs={{0,1},{1,0},{2,3},{3,2},{4,5},{5,4},{6,7},{7,6},{8,9},{9,8},{10,11... | collective-permute-start | bytes 3981320 | tf_op jit(solution)/shard_map/ppermute | solution.py:46
  366.4 137.8 %reduce-scatter.9.cloned.1.call-start = ((), (), s32[]{:S(2)}) async-start(), calls=%async_computation.9 | async-start | bytes 3686400 | tf_op jit(solution)/shard_map/reduce_scatter | solution.py:78
  447.0 116.7 %reduce-scatter.11.cloned.1.call-start = ((), (), s32[]{:S(2)}) async-start(), calls=%async_computation.10 | async-start | bytes 3686400 | tf_op jit(solution)/shard_map/reduce_scatter | solution.py:78
  482.0 143.5 %all-gather.28.cloned.1.call-start = ((), (), s32[]{:S(2)}) async-start(), calls=%async_computation.22 | async-start | bytes 3686400 | tf_op jit(solution)/shard_map/all_gather | solution.py:55
  512.8 173.1 %all-gather.30.cloned.1.call-start = ((), (), s32[]{:S(2)}) async-start(), calls=%async_computation.23 | async-start | bytes 3686400 | tf_op jit(solution)/shard_map/all_gather | solution.py:55
  572.4 183.6 %reduce-scatter.13.cloned.1.call-start = ((), (), s32[]{:S(2)}) async-start(), calls=%async_computation.11 | async-start | bytes 3686400 | tf_op jit(solution)/shard_map/reduce_scatter | solution.py:78
  668.5 146.6 %reduce-scatter.15.cloned.1.call-start = ((), (), s32[]{:S(2)}) async-start(), calls=%async_computation.12 | async-start | bytes 3686400 | tf_op jit(solution)/shard_map/reduce_scatter | solution.py:78
  756.2 217.4 %reduce-scatter.17.cloned.1.call-start = ((), (), s32[]{:S(2)}) async-start(), calls=%async_computation.13 | async-start | bytes 3276800 | tf_op jit(solution)/shard_map/reduce_scatter | solution.py:78
  834.9 36.9 %collective-permute-start.46 = (bf16[144,2304]{1,0:T(8,128)(2,1)}, bf16[144,2304]{1,0:T(8,128)(2,1)}, u32[]{:S(2)}, u32[]{:S(2)}) collective-permute-start(bf16[144,2304]{1,0:T(8,128)(2,1)} %get-tuple-element.591), channel_id=1, source_target_pairs={{0,8},{8,0},{16,24},{24,16},{1,9},{9,1},{17,25},{25,17},{2,10},{10... | collective-permute-start | bytes 1990664 | tf_op jit(solution)/shard_map/ppermute | solution.py:42
  861.8 40.5 %collective-permute-start.49 = (bf16[80,2304]{1,0:T(8,128)(2,1)}, bf16[80,2304]{1,0:T(8,128)(2,1)S(1)}, u32[]{:S(2)}, u32[]{:S(2)}) collective-permute-start(bf16[80,2304]{1,0:T(8,128)(2,1)} %slice.255), channel_id=1, source_target_pairs={{0,8},{8,0},{16,24},{24,16},{1,9},{9,1},{17,25},{25,17},{2,10},{10... | collective-permute-start | bytes 1105928 | tf_op jit(solution)/shard_map/ppermute | solution.py:42
  913.4 114.9 %reduce-scatter.19.cloned.1.call-start = ((), (), s32[]{:S(2)}) async-start(), calls=%async_computation.14 | async-start | bytes 3276800 | tf_op jit(solution)/shard_map/reduce_scatter | solution.py:78
  973.6 116.7 %reduce-scatter.23.cloned.1.call-start = ((), (), s32[]{:S(2)}) async-start(), calls=%async_computation.16 | async-start | bytes 2654208 | tf_op jit(solution)/shard_map/reduce_scatter | solution.py:1200
  1028.3 122.0 %reduce-scatter.21.cloned.1.call-start = ((), (), s32[]{:S(2)}) async-start(), calls=%async_computation.15 | async-start | bytes 5308416 | tf_op jit(solution)/shard_map/reduce_scatter | solution.py:1219
  1036.3 40.2 %collective-permute-start.60 = (bf16[2,160,2304]{2,1,0:T(8,128)(2,1)}, bf16[2,160,2304]{2,1,0:T(8,128)(2,1)S(1)}, u32[]{:S(2)}, u32[]{:S(2)}) collective-permute-start(bf16[2,160,2304]{2,1,0:T(8,128)(2,1)} %get-tuple-element.676), channel_id=1, source_target_pairs={{0,8},{8,0},{16,24},{24,16},{1,9},{9,1},{17,25},{25,17},{2,10},{10... | collective-permute-start | bytes 4423688 | tf_op jit(solution)/shard_map/ppermute | solution.py:42
  1037.7 38.8 %collective-permute-start.61 = (bf16[2,160,2304]{2,1,0:T(8,128)(2,1)}, bf16[2,160,2304]{2,1,0:T(8,128)(2,1)S(1)}, u32[]{:S(2)}, u32[]{:S(2)}) collective-permute-start(bf16[2,160,2304]{2,1,0:T(8,128)(2,1)} %get-tuple-element.677), channel_id=1, source_target_pairs={{0,16},{8,24},{16,0},{24,8},{1,17},{9,25},{17,1},{25,9},{2,18},{10... | collective-permute-start | bytes 4423688 | tf_op jit(solution)/shard_map/ppermute | solution.py:42
  1039.8 36.7 %collective-permute-start.64 = (bf16[1,72,2304]{2,1,0:T(8,128)(2,1)}, bf16[1,72,2304]{2,1,0:T(8,128)(2,1)S(1)}, u32[]{:S(2)}, u32[]{:S(2)}) collective-permute-start(bf16[1,72,2304]{2,1,0:T(8,128)(2,1)} %get-tuple-element.696), channel_id=1, source_target_pairs={{0,4},{1,5},{2,6},{3,7},{4,0},{5,1},{6,2},{7,3},{8,12},{9,13},{10,... | collective-permute-start | bytes 995336 | tf_op jit(solution)/shard_map/ppermute | solution.py:66
  (204 other events, 2033.7 us)
Sparse Core Ops, SparseCore 0:
  26.0 95.2 all-gather.17
  130.1 61.9 all-gather.19
  194.2 53.5 all-gather.21
  249.9 30.3 all-gather.15
  326.1 59.4 all-gather.23
  387.0 58.9 all-gather.25
  448.3 55.8 reduce-scatter.8
  506.6 57.0 reduce-scatter.10
  565.3 60.1 all-gather.27
  626.9 58.9 all-gather.29
  688.2 55.8 reduce-scatter.12
  756.3 56.0 reduce-scatter.14
  913.5 60.0 reduce-scatter.16
  976.3 51.9 reduce-scatter.18
  1031.0 54.1 reduce-scatter.22
  1087.4 61.8 reduce-scatter.20

commit v5 on v4

--- a/solution.py
+++ b/solution.py
@@ -1212,8 +1212,8 @@
         flat = [[x.reshape(2 * span, width) for x in pair] for pair in grads]
         in_term = input_terms(normed_rows, flat, dp, seq)
         down_sent, down_kept = combine(down_own, down_other, ff_rows)
-        near, kept, in_term, down_sent, down_kept, up_line = order(
-            near, kept, in_term, down_sent, down_kept, up_line
+        near, kept, in_term, down_sent, down_kept = order(
+            near, kept, in_term, down_sent, down_kept
         )
         far = scatter_quad_far(kept, near)
         in_part = lax.psum_scatter(
@@ -1241,7 +1241,7 @@
     if quad:
         gains, down_near = order(gains, down_near)
         down_far = scatter_quad_far(down_kept, down_near)
-        in_part = order(in_part)
+        in_part, up_line = order(in_part, up_line)
         part_shard = exchange_quad(in_part.reshape(dp, rows, 2 * width), head)
         part_shard, down_far = order(part_shard, down_far)
         down_shard = scatter_quad_end(down_kept, down_near, down_far)

time: 1200 us -> 1220 us (1.017)
  waiting for transfers between devices: 423 us -> 438 us
    ppermute x53, waiting for transfers between devices: 122 us -> 146 us  [across(): lax.ppermute(x, 'dp', [(i, i ^ bits) for i in range(lax.axis_size('dp'))])]
    ppermute x12, waiting for transfers between devices: 42 us -> 56.4 us  [exchange_line_parts(): lax.ppermute(parts[k], 'seq', line_route(line, k))]
    all_gather x6, waiting for transfers between devices: 147 us -> 133 us  [gather_line(): return lax.all_gather(x, 'seq', axis=0, axis_index_groups=line_groups())]
    ppermute x12, starting transfers between devices: 29.1 us -> 15.7 us  [exchange_line_parts(): lax.ppermute(parts[k], 'seq', line_route(line, k))]
    unnamed x291 -> x293, local copies, waits for them, and re-layouts: 40.6 us -> 41.2 us
  transfers between devices with their start and end apart: 98 -> 98, of which waited for: 54 -> 52; matrix products, arithmetic and copies ran while one was open for 27% -> 27% of each run, Pallas kernels for 23% -> 23%
where the time goes in v5:
time: 1220 us; the launch traced here: 1200 us
  waiting for transfers between devices  438 us (36%)
  Pallas kernels  286 us (23%)
  matrix products  190 us (16%)
  starting transfers between devices  93.2 us (8%)
  other arithmetic  92.1 us (8%)
  local copies, waits for them, and re-layouts  88.1 us (7%)
  between operations  15.7 us (1%)
    ppermute x53, waiting for transfers between devices, across(): lax.ppermute(x, 'dp', [(i, i ^ bits) for i in range(lax.axis_size('dp'))])  146 us
    all_gather x6, waiting for transfers between devices, gather_line(): return lax.all_gather(x, 'seq', axis=0, axis_index_groups=line_groups())  133 us
    dot_general x8, matrix products, matmul_t(): lax.dot_general(a, b, (((1,), (1,)), ((), ())), preferred_element_type=jn...  94.8 us
    dot_general x8, matrix products, matmul(): return jnp.dot(a, b, preferred_element_type=jnp.float32)  88.2 us
    pallas_call x3, Pallas kernels, weight_halves(): pl.pallas_call(kernel, grid=(model // block,), in_specs=[pl.BlockSpec(mem...  81.1 us
    reduce_scatter x6, waiting for transfers between devices, scatter_line(): lax.psum_scatter(x, 'seq', scatter_dimension=0, axis_index_groups=line_gr...  77.9 us
    ppermute x53, starting transfers between devices, across(): lax.ppermute(x, 'dp', [(i, i ^ bits) for i in range(lax.axis_size('dp'))])  60.4 us
    ppermute x12, waiting for transfers between devices, exchange_line_parts(): lax.ppermute(parts[k], 'seq', line_route(line, k))  56.4 us
  transfers between devices with their start and end apart: 98, of which 52 were waited for; matrix products, arithmetic and copies ran while one was open for 27% of the time, Pallas kernels for 23%

profile of v5, /device:TPU:0, one launch (start us, length us, event | category | flops | bytes accessed | tf_op | source)
XLA Modules:
  0.0 1204.0 jit_solution(2103322312852597709)
XLA Ops:
  38.5 23.3 %collective-permute-done.3.refs_1_ = bf16[320,2304]{1,0:T(8,128)(2,1)} collective-permute-done((bf16[320,2304]{1,0:T(8,128)(2,1)}, bf16[320,2304]{1,0:T(8,128)(2,1)}, u32[]{:S(2)}, u32[]{:S(2)}) %collective-permute-start.3) | collective-permute-done | bytes 1474592 | tf_op jit(solution)/shard_map/ppermute | solution.py:42
  69.1 39.5 %collective-permute-done.6.refs_8_ = bf16[2,72,2304]{2,1,0:T(8,128)(2,1)} collective-permute-done((bf16[2,72,2304]{2,1,0:T(8,128)(2,1)}, bf16[2,72,2304]{2,1,0:T(8,128)(2,1)}, u32[]{:S(2)}, u32[]{:S(2)}) %collective-permute-start.6) | collective-permute-done | bytes 663584 | tf_op jit(solution)/shard_map/ppermute | solution.py:66
  153.1 11.8 all-gather.16.cloned.1.call-start
  167.2 24.8 %all-gather.20.cloned.1.call-done = bf16[8,320,512]{2,1,0:T(8,128)(2,1)} async-done(((bf16[2,320,512]{2,1,0:T(8,128)(2,1)}), bf16[8,320,512]{2,1,0:T(8,128)(2,1)}) %all-gather.20.cloned.1.call-update) | async-done | bytes 2621456 | tf_op jit(solution)/shard_map/all_gather | solution.py:55
  199.3 11.5 shard_map.259
  210.8 14.5 %collective-permute-done.12.refs_5_ = bf16[576,2304]{1,0:T(8,128)(2,1)} collective-permute-done((bf16[576,2304]{1,0:T(8,128)(2,1)}, bf16[576,2304]{1,0:T(8,128)(2,1)}, u32[]{:S(2)}, u32[]{:S(2)}) %collective-permute-start.12) | collective-permute-done | bytes 2654240 | tf_op jit(solution)/shard_map/ppermute | solution.py:42
  235.0 12.8 %all-gather.22.cloned.1.call-done = bf16[8,320,512]{2,1,0:T(8,128)(2,1)} async-done(((bf16[2,320,512]{2,1,0:T(8,128)(2,1)}), bf16[8,320,512]{2,1,0:T(8,128)(2,1)}) %all-gather.22.cloned.1.call-update) | async-done | bytes 2621456 | tf_op jit(solution)/shard_map/all_gather | solution.py:55
  247.8 17.3 %collective-permute-done.16.refs_4_ = bf16[288,2304]{1,0:T(8,128)(2,1)S(1)} collective-permute-done((bf16[288,2304]{1,0:T(8,128)(2,1)}, bf16[288,2304]{1,0:T(8,128)(2,1)S(1)}, u32[]{:S(2)}, u32[]{:S(2)}) %collective-permute-start.16) | collective-permute-done | bytes 1327136 | tf_op jit(solution)/shard_map/ppermute | solution.py:42
  273.6 11.4 shard_map.266
  295.9 13.1 %collective-permute-done.21.refs_1_ = bf16[2,80,2304]{2,1,0:T(8,128)(2,1)S(1)} collective-permute-done((bf16[2,80,2304]{2,1,0:T(8,128)(2,1)}, bf16[2,80,2304]{2,1,0:T(8,128)(2,1)S(1)}, u32[]{:S(2)}, u32[]{:S(2)}) %collective-permute-start.21) | collective-permute-done | bytes 737312 | tf_op jit(solution)/shard_map/ppermute | solution.py:42
  349.7 11.4 shard_map.280
  371.8 25.4 %all-gather.24.cloned.1.call-done.refs_1_ = bf16[640,2304]{1,0:T(8,128)(2,1)} async-done(((bf16[160,2304]{1,0:T(8,128)(2,1)}), bf16[640,2304]{1,0:T(8,128)(2,1)}) %all-gather.24.cloned.1.call-update) | async-done | bytes 2949136 | tf_op jit(solution)/shard_map/all_gather | solution.py:55
  397.2 13.3 %fusion.72.refs_1_ = f32[640,2304]{1,0:T(8,128)} fusion(bf16[640,2304]{1,0:T(8,128)(2,1)} %get-tuple-element.494.refs_2_, bf16[2304,2304]{1,0:T(8,128)(2,1)} %bitcast.229), kind=kOutput, calls=%fused_computation.234 | convolution fusion | flops 6794772480 | bytes 19464192 | tf_op jit(solution)/shard_map/dot_general | solution.py:30
  417.4 14.8 %multiply_convert_fusion.3 = (bf16[640,2304]{1,0:T(8,128)(2,1)}, f32[640,2304]{1,0:T(8,128)}) fusion(f32[640,2304]{1,0:T(8,128)} %get-tuple-element.497, bf16[640,2304]{1,0:T(8,128)(2,1)} %get-tuple-element.498.left_a.refs_8_, bf16[2304,2304]{1,0:T(8,128)(2,1)} %bitcast.235), kind=kOutput, calls=%fused_computation.23 | convolution fusion | flops 6809518080 | bytes 28311552 | tf_op jit(solution)/shard_map/dot_general | solution.py:30
  446.2 12.4 %convolution_convert_fusion.1 = bf16[640,2304]{1,0:T(8,128)(2,1)} fusion(bf16[640,2304]{1,0:T(8,128)(2,1)S(1)} %copy-done.17, bf16[2304,2304]{1,0:T(8,128)(2,1)} %bitcast.243), kind=kOutput, calls=%fused_computation.28 | convolution fusion | flops 6796247040 | bytes 16515072 | tf_op jit(solution)/shard_map/dot_general | solution.py:30
  458.9 13.5 %fusion.73 = f32[640,2304]{1,0:T(8,128)} fusion(bf16[640,2304]{1,0:T(8,128)(2,1)} %get-tuple-element.514.left_b.refs_9_, bf16[2304,2304]{1,0:T(8,128)(2,1)} %bitcast.230), kind=kOutput, calls=%fused_computation.235 | convolution fusion | flops 6794772480 | bytes 19464192 | tf_op jit(solution)/shard_map/dot_general | solution.py:30
  472.4 11.4 multiply_convert_fusion.2
  496.8 19.0 %reduce-scatter.9.cloned.1.call-done = bf16[1,160,2304]{2,1,0:T(8,128)(2,1)} async-done(((bf16[4,160,2304]{2,1,0:T(8,128)(2,1)}), bf16[1,160,2304]{2,1,0:T(8,128)(2,1)}) %reduce-scatter.9.cloned.1.call-update) | async-done | bytes 737296 | tf_op jit(solution)/shard_map/reduce_scatter | solution.py:78
  534.1 41.2 %reduce-scatter.11.cloned.1.call-done = bf16[1,160,2304]{2,1,0:T(8,128)(2,1)} async-done(((bf16[4,160,2304]{2,1,0:T(8,128)(2,1)}), bf16[1,160,2304]{2,1,0:T(8,128)(2,1)}) %reduce-scatter.11.cloned.1.call-update) | async-done | bytes 737296 | tf_op jit(solution)/shard_map/reduce_scatter | solution.py:78
  584.2 52.9 %all-gather.28.cloned.1.call-done.refs_1_ = bf16[640,2304]{1,0:T(8,128)(2,1)} async-done(((bf16[160,2304]{1,0:T(8,128)(2,1)}), bf16[640,2304]{1,0:T(8,128)(2,1)}) %all-gather.28.cloned.1.call-update) | async-done | bytes 2949136 | tf_op jit(solution)/shard_map/all_gather | solution.py:55
  637.1 18.9 %multiply_convert_fusion.1 = (bf16[640,2304]{1,0:T(8,128)(2,1)}, bf16[640,2304]{1,0:T(8,128)(2,1)}) fusion(f32[640,2304]{1,0:T(8,128)} %get-tuple-element.497, f32[640,2304]{1,0:T(8,128)} %get-tuple-element.823, bf16[640,2304]{1,0:T(8,128)(2,1)} %get-tuple-element.530.refs_5_, bf16[2304,2304]{1,0:T(8,128)(2,1)} %bitcast.244), kind=kOutput, calls=%fused_computation.21 | convolution fusion | flops 6830161920 | bytes 31260672 | tf_op jit(solution)/shard_map/dot_general | solution.py:34
  666.3 13.8 %add_convert_fusion.1 = bf16[640,2304]{1,0:T(8,128)(2,1)} fusion(f32[640,2304]{1,0:T(8,128)} %fusion.74, bf16[640,2304]{1,0:T(8,128)(2,1)} %get-tuple-element.777.refs_1_, bf16[2304,2304]{1,0:T(8,128)(2,1)} %bitcast.231), kind=kOutput, calls=%fused_computation.20 | convolution fusion | flops 6797721600 | bytes 22413312 | tf_op jit(solution)/shard_map/dot_general | solution.py:34
  680.6 16.9 %all-gather.30.cloned.1.call-done.refs_1_ = bf16[640,2304]{1,0:T(8,128)(2,1)} async-done(((bf16[160,2304]{1,0:T(8,128)(2,1)}), bf16[640,2304]{1,0:T(8,128)(2,1)}) %all-gather.30.cloned.1.call-update) | async-done | bytes 2949136 | tf_op jit(solution)/shard_map/all_gather | solution.py:55
  697.5 18.9 %multiply_convert_fusion = (bf16[640,2304]{1,0:T(8,128)(2,1)}, bf16[640,2304]{1,0:T(8,128)(2,1)}) fusion(f32[640,2304]{1,0:T(8,128)} %fusion.73, f32[640,2304]{1,0:T(8,128)} %get-tuple-element.825, bf16[640,2304]{1,0:T(8,128)(2,1)} %get-tuple-element.534.refs_6_, bf16[2304,2304]{1,0:T(8,128)(2,1)} %bitcast.245), kind=kOutput, calls=%fused_computation.19 | convolution fusion | flops 6830161920 | bytes 31260672 | tf_op jit(solution)/shard_map/dot_general | solution.py:34
  726.8 13.8 %add_convert_fusion = bf16[640,2304]{1,0:T(8,128)(2,1)} fusion(f32[640,2304]{1,0:T(8,128)} %fusion.75, bf16[640,2304]{1,0:T(8,128)(2,1)} %get-tuple-element.774.refs_2_, bf16[2304,2304]{1,0:T(8,128)(2,1)} %bitcast.236), kind=kOutput, calls=%fused_computation.18 | convolution fusion | flops 6797721600 | bytes 22413312 | tf_op jit(solution)/shard_map/dot_general | solution.py:34
  740.6 27.0 %shard_map.300 = (bf16[16,72,2304]{2,1,0:T(8,128)(2,1)}, bf16[16,72,2304]{2,1,0:T(8,128)(2,1)}) custom-call(s32[4]{0:T(128)} %get-tuple-element.405.place_ref.place, bf16[640,2304]{1,0:T(8,128)(2,1)} %get-tuple-element.498.left_a.refs_8_, bf16[640,2304]{1,0:T(8,128)(2,1)} %get-tuple-element.514.left_b.refs_9_, bf16[640,2304]{1,0:T(8,128)(2,1)} %get-tuple-element.537.right_a, ...), custom_call_target="tpu_custom_call" | custom-call | tf_op jit(solution)/shard_map/pallas_call | solution.py:300
  799.7 27.0 %shard_map.305 = (bf16[16,72,2304]{2,1,0:T(8,128)(2,1)}, bf16[16,72,2304]{2,1,0:T(8,128)(2,1)}) custom-call(s32[4]{0:T(128)} %get-tuple-element.405.place_ref.place, bf16[640,2304]{1,0:T(8,128)(2,1)} %get-tuple-element.558.left_a, bf16[640,2304]{1,0:T(8,128)(2,1)} %get-tuple-element.559.left_b, bf16[640,2304]{1,0:T(8,128)(2,1)} %get-tuple-element.560.right_a, ...), custom_call_target="tpu_custom_call" | custom-call | tf_op jit(solution)/shard_map/pallas_call | solution.py:300
  894.3 19.6 %shard_map.315 = (bf16[2,320,512]{2,1,0:T(8,128)(2,1)}, bf16[4,2,320,512]{3,2,1,0:T(8,128)(2,1)}, bf16[4,2,320,512]{3,2,1,0:T(8,128)(2,1)}) custom-call(s32[4]{0:T(128)} %get-tuple-element.405.place_ref.place, bf16[2,320,512]{2,1,0:T(8,128)(2,1)} %get-tuple-element.421.query_ref, bf16[2,320,512]{2,1,0:T(8,128)(2,1)} %get-tuple-element.603.grad_ref, ...), custom_call_target="tpu_custom_call" | custom-call | tf_op jit(solution)/shard_map/pallas_call | solution.py:738
  938.1 19.8 %shard_map.319 = (bf16[2,320,512]{2,1,0:T(8,128)(2,1)}, bf16[4,2,320,512]{3,2,1,0:T(8,128)(2,1)}, bf16[4,2,320,512]{3,2,1,0:T(8,128)(2,1)}) custom-call(s32[4]{0:T(128)} %get-tuple-element.405.place_ref.place, bf16[2,320,512]{2,1,0:T(8,128)(2,1)} %get-tuple-element.438.query_ref, bf16[2,320,512]{2,1,0:T(8,128)(2,1)} %bitcast.282, ...), custom_call_target="tpu_custom_call" | custom-call | tf_op jit(solution)/shard_map/pallas_call | solution.py:738
  971.1 14.1 %reduce-scatter.17.cloned.1.call-done = bf16[1,2,320,512]{3,2,1,0:T(8,128)(2,1)} async-done(((bf16[4,2,320,512]{3,2,1,0:T(8,128)(2,1)}), bf16[1,2,320,512]{3,2,1,0:T(8,128)(2,1)}) %reduce-scatter.17.cloned.1.call-update) | async-done | bytes 655376 | tf_op jit(solution)/shard_map/reduce_scatter | solution.py:78
  1009.3 27.1 %shard_map.325 = (bf16[4,288,2304]{2,1,0:T(8,128)(2,1)}, bf16[4,288,2304]{2,1,0:T(8,128)(2,1)}) custom-call(s32[4]{0:T(128)} %get-tuple-element.405.place_ref.place, bf16[640,2304]{1,0:T(8,128)(2,1)} %get-tuple-element.655.left_a, bf16[640,2304]{1,0:T(8,128)(2,1)} %get-tuple-element.656.left_b, bf16[640,2304]{1,0:T(8,128)(2,1)} %get-tuple-element.657.right_a, ...), custom_call_target="tpu_custom_call" | custom-call | tf_op jit(solution)/shard_map/pallas_call | solution.py:300
  1059.3 14.2 %shard_map.331.refs_6_ = bf16[8,4,72,1024]{3,2,1,0:T(8,128)(2,1)} custom-call(bf16[640,2304]{1,0:T(8,128)(2,1)} %get-tuple-element.685.left_a, bf16[640,2304]{1,0:T(8,128)(2,1)} %get-tuple-element.686.left_b, bf16[640,512]{1,0:T(8,128)(2,1)} %bitcast.263, bf16[640,512]{1,0:T(8,128)(2,1)} %bitcast.264, bf16[640,512]{1,0:T(8,128)(2,1)} %bitcast.260, ...), custom_call_target="tpu_custom_call" | custom-call | bytes 21000000 | tf_op jit(solution)/shard_map/pallas_call | solution.py:537
  (731 shorter events, 561.6 us)
Async XLA Ops:
  7.2 114.0 %all-gather.18.cloned.1.call-start = ((), (), s32[]{:S(2)}) async-start(), calls=%async_computation.17 | async-start | bytes 5308416 | tf_op jit(solution)/shard_map/all_gather | solution.py:817
  25.8 166.2 %all-gather.20.cloned.1.call-start = ((), (), s32[]{:S(2)}) async-start(), calls=%async_computation.18 | async-start | bytes 3276800 | tf_op jit(solution)/shard_map/all_gather | solution.py:55
  26.6 37.3 %collective-permute-start.4 = (bf16[320,2304]{1,0:T(8,128)(2,1)}, bf16[320,2304]{1,0:T(8,128)(2,1)}, u32[]{:S(2)}, u32[]{:S(2)}) collective-permute-start(bf16[320,2304]{1,0:T(8,128)(2,1)} %get-tuple-element.393), channel_id=1, source_target_pairs={{0,8},{8,0},{16,24},{24,16},{1,9},{9,1},{17,25},{25,17},{2,10},{10... | collective-permute-start | bytes 4423688 | tf_op jit(solution)/shard_map/ppermute | solution.py:42
  31.0 38.1 %collective-permute-start.5 = (bf16[2,72,2304]{2,1,0:T(8,128)(2,1)}, bf16[2,72,2304]{2,1,0:T(8,128)(2,1)}, u32[]{:S(2)}, u32[]{:S(2)}) collective-permute-start(bf16[2,72,2304]{2,1,0:T(8,128)(2,1)} %get-tuple-element.396), channel_id=1, source_target_pairs={{0,2},{1,3},{2,4},{3,5},{4,6},{5,7},{6,0},{7,1},{8,10},{9,11},{10,... | collective-permute-start | bytes 1990664 | tf_op jit(solution)/shard_map/ppermute | solution.py:66
  32.6 76.0 %collective-permute-start.6 = (bf16[2,72,2304]{2,1,0:T(8,128)(2,1)}, bf16[2,72,2304]{2,1,0:T(8,128)(2,1)}, u32[]{:S(2)}, u32[]{:S(2)}) collective-permute-start(bf16[2,72,2304]{2,1,0:T(8,128)(2,1)} %get-tuple-element.397), channel_id=1, source_target_pairs={{0,4},{1,5},{2,6},{3,7},{4,0},{5,1},{6,2},{7,3},{8,12},{9,13},{10,... | collective-permute-start | bytes 1990664 | tf_op jit(solution)/shard_map/ppermute | solution.py:66
  35.2 75.1 %collective-permute-start.7 = (bf16[2,72,2304]{2,1,0:T(8,128)(2,1)}, bf16[2,72,2304]{2,1,0:T(8,128)(2,1)}, u32[]{:S(2)}, u32[]{:S(2)}) collective-permute-start(bf16[2,72,2304]{2,1,0:T(8,128)(2,1)} %get-tuple-element.398), channel_id=1, source_target_pairs={{0,6},{1,7},{2,0},{3,1},{4,2},{5,3},{6,4},{7,5},{8,14},{9,15},{10,... | collective-permute-start | bytes 1990664 | tf_op jit(solution)/shard_map/ppermute | solution.py:66
  129.9 117.9 %all-gather.22.cloned.1.call-start = ((), (), s32[]{:S(2)}) async-start(), calls=%async_computation.19 | async-start | bytes 3276800 | tf_op jit(solution)/shard_map/all_gather | solution.py:55
  153.1 131.9 %all-gather.16.cloned.1.call-start = ((), (), s32[]{:S(2)}) async-start(), calls=%async_computation.8 | async-start | bytes 2654208 | tf_op jit(solution)/shard_map/all_gather | solution.py:934
  165.0 60.4 %collective-permute-start.12 = (bf16[576,2304]{1,0:T(8,128)(2,1)}, bf16[576,2304]{1,0:T(8,128)(2,1)}, u32[]{:S(2)}, u32[]{:S(2)}) collective-permute-start(bf16[576,2304]{1,0:T(8,128)(2,1)} %get-tuple-element.416), channel_id=1, source_target_pairs={{0,8},{8,0},{16,24},{24,16},{1,9},{9,1},{17,25},{25,17},{2,10},{10... | collective-permute-start | bytes 7962632 | tf_op jit(solution)/shard_map/ppermute | solution.py:42
  166.6 60.0 %collective-permute-start.13 = (bf16[576,2304]{1,0:T(8,128)(2,1)}, bf16[576,2304]{1,0:T(8,128)(2,1)}, u32[]{:S(2)}, u32[]{:S(2)}) collective-permute-start(bf16[576,2304]{1,0:T(8,128)(2,1)} %get-tuple-element.416), channel_id=1, source_target_pairs={{0,16},{8,24},{16,0},{24,8},{1,17},{9,25},{17,1},{25,9},{2,18},{10... | collective-permute-start | bytes 7962632 | tf_op jit(solution)/shard_map/ppermute | solution.py:42
  226.6 38.8 %collective-permute-start.14 = (bf16[576,2304]{1,0:T(8,128)(2,1)}, bf16[576,2304]{1,0:T(8,128)(2,1)}, u32[]{:S(2)}, u32[]{:S(2)}) collective-permute-start(bf16[576,2304]{1,0:T(8,128)(2,1)} %get-tuple-element.432), channel_id=1, source_target_pairs={{0,1},{1,0},{2,3},{3,2},{4,5},{5,4},{6,7},{7,6},{8,9},{9,8},{10,11... | collective-permute-start | bytes 7962632 | tf_op jit(solution)/shard_map/ppermute | solution.py:46
  226.6 38.8 %collective-permute-start.15 = (bf16[576,2304]{1,0:T(8,128)(2,1)}, bf16[576,2304]{1,0:T(8,128)(2,1)}, u32[]{:S(2)}, u32[]{:S(2)}) collective-permute-start(bf16[576,2304]{1,0:T(8,128)(2,1)} %get-tuple-element.433), channel_id=1, source_target_pairs={{0,1},{1,0},{2,3},{3,2},{4,5},{5,4},{6,7},{7,6},{8,9},{9,8},{10,11... | collective-permute-start | bytes 7962632 | tf_op jit(solution)/shard_map/ppermute | solution.py:46
  228.8 168.4 %all-gather.24.cloned.1.call-start = ((), (), s32[]{:S(2)}) async-start(), calls=%async_computation.20 | async-start | bytes 3686400 | tf_op jit(solution)/shard_map/all_gather | solution.py:55
  330.1 128.7 %all-gather.26.cloned.1.call-start = ((), (), s32[]{:S(2)}) async-start(), calls=%async_computation.21 | async-start | bytes 3686400 | tf_op jit(solution)/shard_map/all_gather | solution.py:55
  364.5 46.0 %collective-permute-start.29 = (bf16[288,2304]{1,0:T(8,128)(2,1)}, bf16[288,2304]{1,0:T(8,128)(2,1)S(1)}, u32[]{:S(2)}, u32[]{:S(2)}) collective-permute-start(bf16[288,2304]{1,0:T(8,128)(2,1)} %shard_map.282.refs_1_), channel_id=1, source_target_pairs={{0,8},{8,0},{16,24},{24,16},{1,9},{9,1},{17,25},{25,17},{2,10},{10... | collective-permute-start | bytes 3981320 | tf_op jit(solution)/shard_map/ppermute | solution.py:42
  365.4 45.1 %collective-permute-start.30 = (bf16[288,2304]{1,0:T(8,128)(2,1)}, bf16[288,2304]{1,0:T(8,128)(2,1)}, u32[]{:S(2)}, u32[]{:S(2)}) collective-permute-start(bf16[288,2304]{1,0:T(8,128)(2,1)} %shard_map.282.refs_1_), channel_id=1, source_target_pairs={{0,16},{8,24},{16,0},{24,8},{1,17},{9,25},{17,1},{25,9},{2,18},{10... | collective-permute-start | bytes 3981320 | tf_op jit(solution)/shard_map/ppermute | solution.py:42
  366.8 66.9 %collective-permute-start.33 = (bf16[288,2304]{1,0:T(8,128)(2,1)}, bf16[288,2304]{1,0:T(8,128)(2,1)}, u32[]{:S(2)}, u32[]{:S(2)}) collective-permute-start(bf16[288,2304]{1,0:T(8,128)(2,1)} %shard_map.282.refs_1_), channel_id=1, source_target_pairs={{0,1},{1,0},{2,3},{3,2},{4,5},{5,4},{6,7},{7,6},{8,9},{9,8},{10,11... | collective-permute-start | bytes 3981320 | tf_op jit(solution)/shard_map/ppermute | solution.py:46
  371.3 144.5 %reduce-scatter.9.cloned.1.call-start = ((), (), s32[]{:S(2)}) async-start(), calls=%async_computation.9 | async-start | bytes 3686400 | tf_op jit(solution)/shard_map/reduce_scatter | solution.py:78
  458.6 116.8 %reduce-scatter.11.cloned.1.call-start = ((), (), s32[]{:S(2)}) async-start(), calls=%async_computation.10 | async-start | bytes 3686400 | tf_op jit(solution)/shard_map/reduce_scatter | solution.py:78
  493.6 143.5 %all-gather.28.cloned.1.call-start = ((), (), s32[]{:S(2)}) async-start(), calls=%async_computation.22 | async-start | bytes 3686400 | tf_op jit(solution)/shard_map/all_gather | solution.py:55
  524.4 173.1 %all-gather.30.cloned.1.call-start = ((), (), s32[]{:S(2)}) async-start(), calls=%async_computation.23 | async-start | bytes 3686400 | tf_op jit(solution)/shard_map/all_gather | solution.py:55
  584.0 183.6 %reduce-scatter.13.cloned.1.call-start = ((), (), s32[]{:S(2)}) async-start(), calls=%async_computation.11 | async-start | bytes 3686400 | tf_op jit(solution)/shard_map/reduce_scatter | solution.py:78
  680.1 146.7 %reduce-scatter.15.cloned.1.call-start = ((), (), s32[]{:S(2)}) async-start(), calls=%async_computation.12 | async-start | bytes 3686400 | tf_op jit(solution)/shard_map/reduce_scatter | solution.py:78
  767.8 217.4 %reduce-scatter.17.cloned.1.call-start = ((), (), s32[]{:S(2)}) async-start(), calls=%async_computation.13 | async-start | bytes 3276800 | tf_op jit(solution)/shard_map/reduce_scatter | solution.py:78
  846.6 36.9 %collective-permute-start.46 = (bf16[144,2304]{1,0:T(8,128)(2,1)}, bf16[144,2304]{1,0:T(8,128)(2,1)}, u32[]{:S(2)}, u32[]{:S(2)}) collective-permute-start(bf16[144,2304]{1,0:T(8,128)(2,1)} %get-tuple-element.591), channel_id=1, source_target_pairs={{0,8},{8,0},{16,24},{24,16},{1,9},{9,1},{17,25},{25,17},{2,10},{10... | collective-permute-start | bytes 1990664 | tf_op jit(solution)/shard_map/ppermute | solution.py:42
  873.3 40.7 %collective-permute-start.49 = (bf16[80,2304]{1,0:T(8,128)(2,1)}, bf16[80,2304]{1,0:T(8,128)(2,1)S(1)}, u32[]{:S(2)}, u32[]{:S(2)}) collective-permute-start(bf16[80,2304]{1,0:T(8,128)(2,1)} %slice.255), channel_id=1, source_target_pairs={{0,8},{8,0},{16,24},{24,16},{1,9},{9,1},{17,25},{25,17},{2,10},{10... | collective-permute-start | bytes 1105928 | tf_op jit(solution)/shard_map/ppermute | solution.py:42
  877.6 36.4 %collective-permute-start.50 = (bf16[80,2304]{1,0:T(8,128)(2,1)}, bf16[80,2304]{1,0:T(8,128)(2,1)S(1)}, u32[]{:S(2)}, u32[]{:S(2)}) collective-permute-start(bf16[80,2304]{1,0:T(8,128)(2,1)} %slice.256), channel_id=1, source_target_pairs={{0,16},{8,24},{16,0},{24,8},{1,17},{9,25},{17,1},{25,9},{2,18},{10... | collective-permute-start | bytes 1105928 | tf_op jit(solution)/shard_map/ppermute | solution.py:42
  925.1 114.9 %reduce-scatter.19.cloned.1.call-start = ((), (), s32[]{:S(2)}) async-start(), calls=%async_computation.14 | async-start | bytes 3276800 | tf_op jit(solution)/shard_map/reduce_scatter | solution.py:78
  985.2 113.6 %reduce-scatter.23.cloned.1.call-start = ((), (), s32[]{:S(2)}) async-start(), calls=%async_computation.16 | async-start | bytes 2654208 | tf_op jit(solution)/shard_map/reduce_scatter | solution.py:1200
  1040.0 123.1 %reduce-scatter.21.cloned.1.call-start = ((), (), s32[]{:S(2)}) async-start(), calls=%async_computation.15 | async-start | bytes 5308416 | tf_op jit(solution)/shard_map/reduce_scatter | solution.py:1219
  1048.4 34.9 %collective-permute-start.60 = (bf16[2,160,2304]{2,1,0:T(8,128)(2,1)}, bf16[2,160,2304]{2,1,0:T(8,128)(2,1)S(1)}, u32[]{:S(2)}, u32[]{:S(2)}) collective-permute-start(bf16[2,160,2304]{2,1,0:T(8,128)(2,1)} %get-tuple-element.676), channel_id=1, source_target_pairs={{0,8},{8,0},{16,24},{24,16},{1,9},{9,1},{17,25},{25,17},{2,10},{10... | collective-permute-start | bytes 4423688 | tf_op jit(solution)/shard_map/ppermute | solution.py:42
  1109.3 35.2 %collective-permute-start.68 = (bf16[2,144,2304]{2,1,0:T(8,128)(2,1)}, bf16[2,144,2304]{2,1,0:T(8,128)(2,1)}, u32[]{:S(2)}, u32[]{:S(2)}) collective-permute-start(bf16[2,144,2304]{2,1,0:T(8,128)(2,1)} %get-tuple-element.714), channel_id=1, source_target_pairs={{0,8},{8,0},{16,24},{24,16},{1,9},{9,1},{17,25},{25,17},{2,10},{10... | collective-permute-start | bytes 3981320 | tf_op jit(solution)/shard_map/ppermute | solution.py:42
  (205 other events, 2098.1 us)
Sparse Core Ops, SparseCore 0:
  25.9 95.2 all-gather.17
  130.0 61.9 all-gather.19
  194.2 53.5 all-gather.21
  249.8 30.3 all-gather.15
  330.2 66.9 all-gather.23
  398.6 58.9 all-gather.25
  459.9 55.8 reduce-scatter.8
  518.2 57.0 reduce-scatter.10
  576.9 60.1 all-gather.27
  638.5 58.9 all-gather.29
  699.8 55.8 reduce-scatter.12
  767.9 56.0 reduce-scatter.14
  925.2 59.9 reduce-scatter.16
  987.9 51.9 reduce-scatter.18
  1042.7 35.9 reduce-scatter.22
  1085.7 53.9 reduce-scatter.20
